TPU v7x, 128 devices: a whole 4x4x4 slice. The times are simulated.
128 devices in a mesh: seq: 16 (over z, x_hi, core), head: 8 (over y, x_lo).
Axes of the slice: x: 4 (x_hi: 2, x_lo: 2; x = x_hi * 2 + x_lo), y: 4, z: 4, core: 2. Of those that a mesh axis runs over, the one named last changes fastest.
Arguments:
- residual: bfloat16 [128, 4, 32, 4096], P('head', None, 'seq'), may hold values from -6 to 6
- spatial_query: bfloat16 [128, 4, 32, 4096], P(None, None, 'seq', 'head'), may hold values from -6 to 6
- spatial_key: bfloat16 [128, 4, 32, 4096], P(None, None, 'seq', 'head'), may hold values from -6 to 6
- spatial_value: bfloat16 [128, 4, 32, 4096], P(None, None, 'seq', 'head'), may hold values from -6 to 6
- spatial_out: bfloat16 [4096, 4096], P('head', 'seq'), may hold values from -0.09375 to 0.09375
- temporal_query: bfloat16 [4096, 4096], P('seq', 'head'), may hold values from -0.09375 to 0.09375
- temporal_key: bfloat16 [4096, 4096], P('seq', 'head'), may hold values from -0.09375 to 0.09375
- temporal_value: bfloat16 [4096, 4096], P('seq', 'head'), may hold values from -0.09375 to 0.09375
- temporal_out: bfloat16 [4096, 4096], P('head', 'seq'), may hold values from -0.09375 to 0.09375
Outputs:
- video_out: bfloat16 [128, 4, 32, 4096], P('head', None, 'seq')
All inputs are finite; a program needn't handle non-finite values.
Results may differ from a plain program's by a relative error of at most 0.014.
Values may be sent and summed in bfloat16 or wider, within the bound.
No kernel may reach another device: no remote copies, remote signals or barrier semaphores. Data moves between devices by JAX's collectives and lax.ppermute only.
A program may use at most 128 MiB of HBM per device.

v0:
```python
import jax
import jax.numpy as jnp
from jax import lax
from jax.sharding import PartitionSpec as P

HDIM = 128


def attend(queries, keys_in, values_in, seq_first):
    head_total = queries.shape[-1] // HDIM
    shaped = [
        member.reshape(member.shape[:2] + (head_total, HDIM))
        for member in (queries, keys_in, values_in)
    ]
    if seq_first:
        patterns = ("ighc,jghc->ghij", "ghij,jghc->ighc")
    else:
        patterns = ("gihc,gjhc->ghij", "ghij,gjhc->gihc")
    scores = jnp.einsum(
        patterns[0], shaped[0], shaped[1], preferred_element_type=jnp.float32
    ) * HDIM ** (-0.5)
    exponent = jnp.exp(scores)
    weights = (exponent / jnp.sum(exponent, axis=-1, keepdims=True)).astype(jnp.bfloat16)
    context = jnp.einsum(patterns[1], weights, shaped[2], preferred_element_type=jnp.float32)
    return context.astype(jnp.bfloat16).reshape(queries.shape)


def layer_norm(values_in):
    values_f = values_in.astype(jnp.float32)
    centred = values_f - jnp.mean(values_f, axis=-1, keepdims=True)
    variance = jnp.mean(centred * centred, axis=-1, keepdims=True)
    return (centred * lax.rsqrt(variance + 1e-06)).astype(jnp.bfloat16)


def shards(
    residual,
    spatial_query,
    spatial_key,
    spatial_value,
    spatial_out,
    temporal_query,
    temporal_key,
    temporal_value,
    temporal_out,
):
    head_count = lax.axis_size("head")
    positions, videos, frames_local, local_width = spatial_query.shape
    model_width = residual.shape[-1]
    out_full, tout_full = (
        lax.all_gather(spatial_out, "seq", axis=1, tiled=True),
        lax.all_gather(temporal_out, "seq", axis=1, tiled=True),
    )
    in_full = (
        lax.all_gather(temporal_query, "seq", axis=0, tiled=True),
        lax.all_gather(temporal_key, "seq", axis=0, tiled=True),
        lax.all_gather(temporal_value, "seq", axis=0, tiled=True),
    )
    layout = (positions, videos * frames_local, local_width)
    spatial_context = attend(
        spatial_query.reshape(layout),
        spatial_key.reshape(layout),
        spatial_value.reshape(layout),
        True,
    )
    spatial_summed = lax.psum_scatter(
        jnp.dot(
            spatial_context.reshape(-1, local_width), out_full, preferred_element_type=jnp.float32
        ).astype(jnp.bfloat16),
        "head",
        scatter_dimension=0,
        tiled=True,
    ).astype(jnp.float32)
    middle = (residual.reshape(-1, model_width).astype(jnp.float32) + spatial_summed).astype(
        jnp.bfloat16
    )
    middle = middle.reshape((positions // head_count, videos, frames_local, model_width))
    gathered = lax.all_gather(layer_norm(middle), "head", axis=0, tiled=True)
    token_rows = gathered.reshape(-1, model_width)
    projected_parts = [
        jnp.dot(token_rows, weight, preferred_element_type=jnp.float32).astype(jnp.bfloat16)
        for weight in in_full
    ]
    projected = jnp.concatenate(projected_parts, axis=1).reshape(
        (positions, videos, frames_local, 3 * local_width)
    )
    attend_projected = lax.all_to_all(projected, "seq", split_axis=0, concat_axis=2, tiled=True)
    flattened = attend_projected.reshape((-1,) + attend_projected.shape[2:])
    temporal_context = attend(
        flattened[..., :local_width],
        flattened[..., local_width : 2 * local_width],
        flattened[..., 2 * local_width :],
        False,
    )
    temporal_context = temporal_context.reshape(attend_projected.shape[:3] + (local_width,))
    returned = lax.all_to_all(temporal_context, "seq", split_axis=2, concat_axis=0, tiled=True)
    summed = lax.psum_scatter(
        jnp.dot(
            returned.reshape(-1, local_width), tout_full, preferred_element_type=jnp.float32
        ).astype(jnp.bfloat16),
        "head",
        scatter_dimension=0,
        tiled=True,
    ).astype(jnp.float32)
    finished = middle.reshape(-1, model_width).astype(jnp.float32) + summed
    return finished.astype(jnp.bfloat16).reshape(middle.shape)


def solution(mesh):
    in_specs = (
        P("head", None, "seq", None),
        P(None, None, "seq", "head"),
        P(None, None, "seq", "head"),
        P(None, None, "seq", "head"),
        P("head", "seq"),
        P("seq", "head"),
        P("seq", "head"),
        P("seq", "head"),
        P("head", "seq"),
    )
    out_specs = P("head", None, "seq", None)
    return jax.shard_map(shards, mesh=mesh, in_specs=in_specs, out_specs=out_specs, check_vma=False)
```

profile of v0, /device:TPU:1, one launch (start us, length us, event | category | flops | bytes accessed | tf_op | source)
XLA Modules:
  0.0 898.1 jit_solution(8925348346568494841)
XLA Ops:
  7.3 1.7 reshape_reshape.15
  9.1 1.7 reshape_reshape.16
  10.8 1.5 reshape_reshape.17
  14.4 55.8 %all-gather.7.cloned.1.call-done = bf16[512,4096]{1,0:T(8,128)(2,1)} async-done(((bf16[512,256]{1,0:T(8,128)(2,1)}), bf16[512,4096]{1,0:T(8,128)(2,1)}) %all-gather.7.cloned.1.call-update) | async-done | bytes 4194320 | tf_op jit(solution)/shard_map/all_gather | solution.py:50
  70.2 10.5 %convolution_convert_fusion.1 = bf16[1024,4096]{1,0:T(8,128)(2,1)} fusion(bf16[512,4096]{1,0:T(8,128)(2,1)} %all-gather.7.cloned.1.call-done, bf16[128,8,4,128]{3,0,2,1:T(8,128)(2,1)S(1)} %fusion.4), kind=kOutput, calls=%fused_computation.1 | convolution fusion | flops 4299161600 | bytes 13631488 | tf_op jit(solution)/shard_map/dot_general | solution.py:66
  80.9 1.1 copy-done
  82.3 165.0 %reduce-scatter.3.cloned.1.call-done = bf16[128,4096]{1,0:T(8,128)(2,1)} async-done(((bf16[1024,4096]{1,0:T(8,128)(2,1)}), bf16[128,4096]{1,0:T(8,128)(2,1)}) %reduce-scatter.3.cloned.1.call-update) | async-done | bytes 1048592 | tf_op jit(solution)/shard_map/reduce_scatter | solution.py:65
  247.4 1.6 convert_reduce_fusion
  249.0 1.3 reshape.72
  251.5 3.1 fusion.1
  257.1 166.9 %all-gather.9.cloned.1.call-done = bf16[128,4,2,4096]{3,1,2,0:T(4,128)(2,1)} async-done(((bf16[16,4,2,4096]{3,1,2,0:T(4,128)(2,1)}), bf16[128,4,2,4096]{3,1,2,0:T(4,128)(2,1)}) %all-gather.9.cloned.1.call-update) | async-done | bytes 8388624 | tf_op jit(solution)/shard_map/all_gather | solution.py:77
  424.0 16.3 %copy.53 = bf16[128,4,2,4096]{3,2,1,0:T(2,128)(2,1)} copy(bf16[128,4,2,4096]{3,1,2,0:T(4,128)(2,1)} %all-gather.9.cloned.1.call-done) | data formatting | bytes 16777216 | tf_op jit(solution)/shard_map/all_gather | solution.py:77
  440.3 13.3 %reshape.63 = bf16[1024,4096]{1,0:T(8,128)(2,1)} reshape(bf16[128,4,2,4096]{3,2,1,0:T(2,128)(2,1)} %copy.53) | data formatting | bytes 16777216 | tf_op jit(solution)/shard_map/reshape | solution.py:78
  453.6 29.7 %all-gather.15.cloned.1.call-done = bf16[4096,512]{1,0:T(8,128)(2,1)} async-done(((bf16[256,512]{1,0:T(8,128)(2,1)}), bf16[4096,512]{1,0:T(8,128)(2,1)}) %all-gather.15.cloned.1.call-update) | async-done | bytes 4194320 | tf_op jit(solution)/shard_map/all_gather | solution.py:56
  483.3 9.1 %convolution_convert_fusion.2 = bf16[1024,512]{0,1:T(8,128)(2,1)S(1)} fusion(bf16[1024,4096]{1,0:T(8,128)(2,1)} %reshape.63, bf16[4096,512]{1,0:T(8,128)(2,1)} %all-gather.15.cloned.1.call-done), kind=kOutput, calls=%fused_computation.17 | convolution fusion | flops 4295491584 | bytes 13631488 | tf_op jit(solution)/shard_map/dot_general | solution.py:80
  492.4 46.4 %all-gather.13.cloned.1.call-done = bf16[4096,512]{1,0:T(8,128)(2,1)} async-done(((bf16[256,512]{1,0:T(8,128)(2,1)}), bf16[4096,512]{1,0:T(8,128)(2,1)}) %all-gather.13.cloned.1.call-update) | async-done | bytes 4194320 | tf_op jit(solution)/shard_map/all_gather | solution.py:55
  538.8 9.1 %convolution_convert_fusion.3 = bf16[1024,512]{0,1:T(8,128)(2,1)S(1)} fusion(bf16[1024,4096]{1,0:T(8,128)(2,1)} %reshape.63, bf16[4096,512]{1,0:T(8,128)(2,1)} %all-gather.13.cloned.1.call-done), kind=kOutput, calls=%fused_computation.18 | convolution fusion | flops 4295491584 | bytes 13631488 | tf_op jit(solution)/shard_map/dot_general | solution.py:80
  547.9 46.4 %all-gather.11.cloned.1.call-done = bf16[4096,512]{1,0:T(8,128)(2,1)} async-done(((bf16[256,512]{1,0:T(8,128)(2,1)}), bf16[4096,512]{1,0:T(8,128)(2,1)}) %all-gather.11.cloned.1.call-update) | async-done | bytes 4194320 | tf_op jit(solution)/shard_map/all_gather | solution.py:54
  594.4 9.3 %convolution_convert_fusion.4 = bf16[1024,512]{0,1:T(8,128)(2,1)S(1)} fusion(bf16[1024,4096]{1,0:T(8,128)(2,1)} %reshape.63, bf16[4096,512]{1,0:T(8,128)(2,1)} %all-gather.11.cloned.1.call-done), kind=kOutput, calls=%fused_computation.19 | convolution fusion | flops 4295491584 | bytes 13631488 | tf_op jit(solution)/shard_map/dot_general | solution.py:80
  603.7 2.0 pad_maximum_fusion
  605.7 4.7 copy.54
  610.3 7.2 reshape.64
  617.6 54.5 %all_to_all.30 = bf16[128,4,2,1536]{3,2,1,0:T(2,128)(2,1)S(1)} all-to-all(bf16[128,4,2,1536]{3,2,1,0:T(2,128)(2,1)} %reshape.64), channel_id=1, replica_groups=mesh['seq'=16,'head'=8] {'seq'}, dimensions={0} | all-to-all | bytes 6291456 | tf_op jit(solution)/shard_map/all_to_all | solution.py:86
  672.0 5.0 copy.107
  677.0 7.5 reshape.65
  684.5 2.4 slice_bitcast_fusion.1
  689.3 20.9 %all_to_all.31 = bf16[8,4,32,512]{3,1,0,2:T(4,128)(2,1)S(1)} all-to-all(bf16[8,4,32,512]{3,1,0,2:T(4,128)(2,1)S(1)} %reshape.73), channel_id=1, replica_groups=mesh['seq'=16,'head'=8] {'seq'}, dimensions={2} | all-to-all | bytes 2097152 | tf_op jit(solution)/shard_map/all_to_all | solution.py:95
  710.2 1.6 copy.108
  712.3 8.9 convolution_convert_fusion
  721.2 166.6 %reduce-scatter.5.cloned.1.call-done = bf16[128,4096]{1,0:T(8,128)(2,1)} async-done(((bf16[1024,4096]{1,0:T(8,128)(2,1)}), bf16[128,4096]{1,0:T(8,128)(2,1)}) %reduce-scatter.5.cloned.1.call-update) | async-done | bytes 1048592 | tf_op jit(solution)/shard_map/reduce_scatter | solution.py:96
  887.9 1.5 add_convert_fusion
  889.3 1.5 reshape.70
  (37 shorter events, 9.7 us)
Async XLA Ops:
  6.5 4.3 copy-start.1
  6.5 63.7 %all-gather.7.cloned.1.call-start = ((), (), s32[]{:S(2)}) async-start(), calls=%async_computation.4 | async-start | bytes 4456448 | tf_op jit(solution)/shard_map/all_gather | solution.py:50
  7.3 240.1 %reduce-scatter.3.cloned.1.call-start = ((), (), s32[]{:S(2)}) async-start(), calls=%async_computation.5 | async-start | bytes 9437184 | tf_op jit(solution)/shard_map/reduce_scatter | solution.py:65
  12.3 1.2 copy-start.2
  80.8 1.2 copy-start
  80.8 343.2 %all-gather.9.cloned.1.call-start = ((), (), s32[]{:S(2)}) async-start(), calls=%async_computation.6 | async-start | bytes 9437184 | tf_op jit(solution)/shard_map/all_gather | solution.py:77
  254.6 228.7 %all-gather.15.cloned.1.call-start = ((), (), s32[]{:S(2)}) async-start(), calls=%async_computation.9 | async-start | bytes 4456448 | tf_op jit(solution)/shard_map/all_gather | solution.py:56
  255.2 283.6 %all-gather.13.cloned.1.call-start = ((), (), s32[]{:S(2)}) async-start(), calls=%async_computation.8 | async-start | bytes 4456448 | tf_op jit(solution)/shard_map/all_gather | solution.py:55
  255.8 338.6 %all-gather.11.cloned.1.call-start = ((), (), s32[]{:S(2)}) async-start(), calls=%async_computation.7 | async-start | bytes 4456448 | tf_op jit(solution)/shard_map/all_gather | solution.py:54
  256.4 455.9 %all-gather.17.cloned.1.call-start = ((), (), s32[]{:S(2)}) async-start(), calls=%async_computation.10 | async-start | bytes 4456448 | tf_op jit(solution)/shard_map/all_gather | solution.py:51
  257.1 630.8 %reduce-scatter.5.cloned.1.call-start = ((), (), s32[]{:S(2)}) async-start(), calls=%async_computation.11 | async-start | bytes 9437184 | tf_op jit(solution)/shard_map/reduce_scatter | solution.py:96
Sparse Core Ops, SparseCore 0:
  9.7 60.4 all-gather.6
  80.9 166.3 reduce-scatter.2
  254.7 169.2 all-gather.8
  426.3 56.8 all-gather.14
  485.6 53.1 all-gather.12
  541.1 53.1 all-gather.10
  596.7 69.0 all-gather.16
  721.3 166.4 reduce-scatter.4
where the time goes:
time: 907 us; the launch traced here: 898 us
  waiting for transfers between devices  680 us (75%)
  blocking collectives  75.3 us (8%)
  local copies, waits for them, and re-layouts  69.5 us (8%)
  matrix products  50.4 us (6%)
  between operations  14.1 us (2%)
    all_gather x1, waiting for transfers between devices, shards(): gathered = lax.all_gather(layer_norm(middle), 'head', axis=0, tiled=True)  167 us
    reduce_scatter x1, waiting for transfers between devices, shards(): lax.psum_scatter(jnp.dot(returned.reshape(-1, local_width), tout_full, pr...  167 us
    reduce_scatter x1, waiting for transfers between devices, shards(): lax.psum_scatter(jnp.dot(spatial_context.reshape(-1, local_width), out_fu...  165 us
    all_gather x1, waiting for transfers between devices, shards(): lax.all_gather(spatial_out, 'seq', axis=1, tiled=True)  55.8 us
    all_to_all x1, blocking collectives, shards(): lax.all_to_all(projected, 'seq', split_axis=0, concat_axis=2, tiled=True)  54.5 us
    all_gather x1, waiting for transfers between devices, shards(): lax.all_gather(temporal_query, 'seq', axis=0, tiled=True)  46.4 us
    all_gather x1, waiting for transfers between devices, shards(): lax.all_gather(temporal_key, 'seq', axis=0, tiled=True)  46.4 us
    all_gather x1, waiting for transfers between devices, shards(): lax.all_gather(temporal_value, 'seq', axis=0, tiled=True)  29.7 us
  transfers between devices with their start and end apart: 8, of which 7 were waited for; matrix products, arithmetic and copies ran while one was open for 11% of the time, Pallas kernels for 0%

commit v1 on v0

v1 whole, which is shorter than its diff:
```python
import numpy as np

import jax
import jax.numpy as jnp
from jax import lax
from jax.experimental import pallas as pl
from jax.experimental.pallas import tpu as pltpu
from jax.sharding import Mesh
from jax.sharding import PartitionSpec as P

HDIM = 128
AXES = ("z", "xh", "c", "y", "xl")
SIZES = (4, 2, 2, 4, 2)
RING = 4
VMEM_LIMIT = 58 * 1024 * 1024


def permutation(move):
    pairs = []
    for source in range(int(np.prod(SIZES))):
        z, xh, c, y, xl = (int(v) for v in np.unravel_index(source, SIZES))
        z, x, c, y = (v % n for v, n in zip(move(z, 2 * xh + xl, c, y), (4, 4, 2, 4)))
        pairs.append((source, int(np.ravel_multi_index((z, x // 2, c, y, x % 2), SIZES))))
    return pairs


def from_y(array, d):
    return lax.ppermute(array, AXES, permutation(lambda z, x, c, y: (z, x, c, y - d)))


def to_y(array, d):
    return lax.ppermute(array, AXES, permutation(lambda z, x, c, y: (z, x, c, y + d)))


def swap_xl(array):
    return lax.ppermute(array, AXES, permutation(lambda z, x, c, y: (z, x ^ 1, c, y)))


def swap_core(array):
    return lax.ppermute(array, AXES, permutation(lambda z, x, c, y: (z, x, 1 - c, y)))


def from_first(array, d):
    return lax.ppermute(
        array, AXES, permutation(lambda z, x, c, y: (z - d * c, x - d * (1 - c), c, y))
    )


def from_second(array, d):
    return lax.ppermute(
        array, AXES, permutation(lambda z, x, c, y: (z - d * (1 - c), x - d * c, c, y))
    )


def gather_weight(shard):
    first = jnp.stack([shard] + [from_first(shard, d) for d in range(1, RING)])
    own = [first] + [from_second(first, d) for d in range(1, RING)]
    return own + [swap_core(part) for part in own]


def places(coords):
    z, x, c = coords[0], coords[1], coords[2]
    found = []
    for other in range(2):
        core = c + other - 2 * c * other
        for j in range(RING):
            for i in range(RING):
                dx, dz = i + core * (j - i), j + core * (i - j)
                px, pz = lax.rem(x + dx, RING), lax.rem(z + dz, RING)
                s = pz * 4 + lax.div(px, 2) * 2 + core
                found.append((other * RING + j, i, s, lax.rem(px, 2)))
    return found


def out_copies(coords, refs, weight, sems):
    copies = []
    for n, (array, entry, s, xl) in enumerate(places(coords)):
        rows = pl.ds(pl.multiple_of(xl * 512, 512), 512)
        copies.append(
            pltpu.make_async_copy(refs[array].at[entry], weight.at[s, rows], sems.at[n])
        )
    return copies


def project_out(context, weight, outs):
    def step(s, carry):
        part = jnp.dot(context[...], weight[s], preferred_element_type=jnp.float32)
        part = part.astype(jnp.bfloat16)
        columns = pl.ds(pl.multiple_of(s * 256, 256), 256)
        for d in range(RING):
            outs[d][:, columns] = part[d * 128 : (d + 1) * 128]
        return carry

    lax.fori_loop(0, 16, step, 0)


def spatial_out_kernel(coords, own, other, *rest):
    refs, outs, (context, weight, ctx_sems, sems) = rest[:8], rest[8:12], rest[12:]
    y, xl = coords[3], coords[4]
    copies = out_copies(coords, refs, weight, sems)
    for copy in copies:
        copy.start()
    context_copies = []
    for d in range(RING):
        block = lax.rem(y + d, RING)
        for n, (source, half) in enumerate(((own, xl), (other, 1 - xl))):
            columns = pl.ds(pl.multiple_of(half * 512, 512), 512)
            context_copies.append(
                pltpu.make_async_copy(
                    source.at[block],
                    context.at[pl.ds(d * 128, 128), columns],
                    ctx_sems.at[2 * d + n],
                )
            )
    for copy in context_copies:
        copy.start()
    for copy in context_copies:
        copy.wait()
    for copy in copies:
        copy.wait()
    project_out(context, weight, outs)


def spatial_out_call(coords, own, other, weights):
    anywhere = pl.BlockSpec(memory_space=pl.ANY)
    return pl.pallas_call(
        spatial_out_kernel,
        out_shape=[jax.ShapeDtypeStruct((128, 4096), jnp.bfloat16)] * RING,
        in_specs=[pl.BlockSpec(memory_space=pltpu.SMEM)] + [anywhere] * 10,
        out_specs=[pl.BlockSpec(memory_space=pltpu.VMEM)] * RING,
        scratch_shapes=[
            pltpu.VMEM((512, 1024), jnp.bfloat16),
            pltpu.VMEM((16, 1024, 256), jnp.bfloat16),
            pltpu.SemaphoreType.DMA((8,)),
            pltpu.SemaphoreType.DMA((32,)),
        ],
        compiler_params=pltpu.CompilerParams(vmem_limit_bytes=VMEM_LIMIT),
        cost_estimate=pl.CostEstimate(
            flops=2 * 512 * 1024 * 4096, bytes_accessed=14 << 20, transcendentals=0
        ),
        name="spatial_out",
    )(coords, own, other, *weights)


def temporal_kernel(coords, *rest):
    blocks, qkv_refs, out_refs = rest[:4], rest[4:12], rest[12:20]
    outs = rest[20:24]
    tokens, weight, out_weight, projected, context, token_sems, sems, out_sems = rest[24:]
    token_copies = [
        pltpu.make_async_copy(
            blocks[d], tokens.at[pl.ds(d * 128, 128)], token_sems.at[d]
        )
        for d in range(RING)
    ]
    for copy in token_copies:
        copy.start()
    spots = places(coords)
    copies = [[], [], []]
    for w in range(3):
        for n, (array, entry, s, xl) in enumerate(spots):
            rows = pl.ds(pl.multiple_of(s * 256, 256), 256)
            copies[w].append(
                pltpu.make_async_copy(
                    qkv_refs[array].at[entry, w], weight.at[w, xl, rows], sems.at[w, n]
                )
            )
        for copy in copies[w]:
            copy.start()
    last_copies = out_copies(coords, out_refs, out_weight, out_sems)
    for copy in last_copies:
        copy.start()
    for copy in token_copies:
        copy.wait()
    for w in range(3):
        for copy in copies[w]:
            copy.wait()

        def project(n, carry, w=w):
            xl = lax.div(n, 2)
            columns = pl.ds(pl.multiple_of(lax.rem(n, 2) * 256, 256), 256)
            part = jnp.dot(
                tokens[...], weight[w, xl, :, columns], preferred_element_type=jnp.float32
            )
            projected[w, :, pl.ds(pl.multiple_of(n * 256, 256), 256)] = part.astype(
                jnp.bfloat16
            )
            return carry

        lax.fori_loop(0, 4, project, 0)

    video = lax.rem(lax.div(lax.broadcasted_iota(jnp.int32, (128, 128), 0), 2), 4)
    video_key = lax.rem(lax.div(lax.broadcasted_iota(jnp.int32, (128, 128), 1), 2), 4)
    same = video == video_key

    def attend_block(d, carry):
        rows = pl.ds(pl.multiple_of(d * 128, 128), 128)
        for head in range(8):
            columns = pl.ds(head * HDIM, HDIM)
            query, key, value = (projected[w, rows, columns] for w in range(3))
            scores = lax.dot_general(
                query, key, (((1,), (1,)), ((), ())), preferred_element_type=jnp.float32
            ) * HDIM ** (-0.5)
            exponent = jnp.where(same, jnp.exp(scores), 0.0)
            weights = exponent / jnp.sum(exponent, axis=-1, keepdims=True)
            context[rows, columns] = jnp.dot(
                weights.astype(jnp.bfloat16), value, preferred_element_type=jnp.float32
            ).astype(jnp.bfloat16)
        return carry

    lax.fori_loop(0, RING, attend_block, 0)
    for copy in last_copies:
        copy.wait()
    project_out(context, out_weight, outs)


def temporal_call(coords, blocks, qkv, out_weights):
    anywhere = pl.BlockSpec(memory_space=pl.ANY)
    return pl.pallas_call(
        temporal_kernel,
        out_shape=[jax.ShapeDtypeStruct((128, 4096), jnp.bfloat16)] * RING,
        in_specs=[pl.BlockSpec(memory_space=pltpu.SMEM)] + [anywhere] * 20,
        out_specs=[pl.BlockSpec(memory_space=pltpu.VMEM)] * RING,
        scratch_shapes=[
            pltpu.VMEM((512, 4096), jnp.bfloat16),
            pltpu.VMEM((3, 2, 4096, 512), jnp.bfloat16),
            pltpu.VMEM((16, 1024, 256), jnp.bfloat16),
            pltpu.VMEM((3, 512, 1024), jnp.bfloat16),
            pltpu.VMEM((512, 1024), jnp.bfloat16),
            pltpu.SemaphoreType.DMA((4,)),
            pltpu.SemaphoreType.DMA((3, 32)),
            pltpu.SemaphoreType.DMA((32,)),
        ],
        compiler_params=pltpu.CompilerParams(vmem_limit_bytes=VMEM_LIMIT),
        cost_estimate=pl.CostEstimate(
            flops=2 * 512 * 4096 * 4096, bytes_accessed=40 << 20, transcendentals=512 * 1024
        ),
        name="temporal",
    )(coords, *blocks, *qkv, *out_weights)


def attend(queries, keys_in, values_in):
    head_total = queries.shape[-1] // HDIM
    shaped = [
        member.reshape(member.shape[:2] + (head_total, HDIM))
        for member in (queries, keys_in, values_in)
    ]
    scores = jnp.einsum(
        "ighc,jghc->ghij", shaped[0], shaped[1], preferred_element_type=jnp.float32
    ) * HDIM ** (-0.5)
    exponent = jnp.exp(scores)
    weights = (exponent / jnp.sum(exponent, axis=-1, keepdims=True)).astype(jnp.bfloat16)
    context = jnp.einsum(
        "ghij,jghc->ighc", weights, shaped[2], preferred_element_type=jnp.float32
    )
    return context.astype(jnp.bfloat16).reshape(queries.shape)


def layer_norm(values_in):
    values_f = values_in.astype(jnp.float32)
    centred = values_f - jnp.mean(values_f, axis=-1, keepdims=True)
    variance = jnp.mean(centred * centred, axis=-1, keepdims=True)
    return (centred * lax.rsqrt(variance + 1e-06)).astype(jnp.bfloat16)


def sum_over_y(parts):
    total = parts[0].astype(jnp.float32)
    for d in range(1, RING):
        total = total + to_y(parts[d], d).astype(jnp.float32)
    return total


def shards(
    residual,
    spatial_query,
    spatial_key,
    spatial_value,
    spatial_out,
    temporal_query,
    temporal_key,
    temporal_value,
    temporal_out,
):
    z, xh, c, y, xl = (lax.axis_index(name) for name in AXES)
    coords = jnp.stack([z, 2 * xh + xl, c, y, xl]).astype(jnp.int32)
    spatial_weights = gather_weight(spatial_out)
    qkv_weights = gather_weight(jnp.stack([temporal_query, temporal_key, temporal_value]))
    out_weights = gather_weight(temporal_out)

    layout = (128, 8, 512)
    context = attend(
        spatial_query.reshape(layout), spatial_key.reshape(layout), spatial_value.reshape(layout)
    ).reshape(RING, 2, 128, 512)
    own = lax.dynamic_index_in_dim(context, xl, axis=1, keepdims=False)
    other = swap_xl(lax.dynamic_index_in_dim(context, 1 - xl, axis=1, keepdims=False))
    parts = spatial_out_call(coords, own, other, spatial_weights)
    middle = (residual.reshape(128, 4096).astype(jnp.float32) + sum_over_y(parts)).astype(
        jnp.bfloat16
    )
    normed = layer_norm(middle).reshape(16, 8, 4096)
    normed = lax.all_to_all(
        normed, ("z", "xh", "c"), split_axis=0, concat_axis=0, tiled=True
    ).reshape(128, 4096)
    blocks = [normed] + [from_y(normed, d) for d in range(1, RING)]
    parts = temporal_call(coords, blocks, qkv_weights, out_weights)
    summed = sum_over_y(parts).astype(jnp.bfloat16).reshape(16, 8, 4096)
    summed = lax.all_to_all(summed, ("z", "xh", "c"), split_axis=0, concat_axis=0, tiled=True)
    finished = middle.astype(jnp.float32) + summed.reshape(128, 4096).astype(jnp.float32)
    return finished.astype(jnp.bfloat16).reshape(residual.shape)


def solution(mesh):
    split = Mesh(mesh.devices.reshape(SIZES), AXES)
    seq, head = ("z", "xh", "c"), ("y", "xl")
    in_specs = (
        P(head, None, seq, None),
        P(None, None, seq, head),
        P(None, None, seq, head),
        P(None, None, seq, head),
        P(head, seq),
        P(seq, head),
        P(seq, head),
        P(seq, head),
        P(head, seq),
    )
    out_specs = P(head, None, seq, None)
    return jax.shard_map(shards, mesh=split, in_specs=in_specs, out_specs=out_specs, check_vma=False)
```

time: 907 us -> 373 us (0.41)
  waiting for transfers between devices: 680 us -> 195 us
  Pallas kernels: 0 us -> 60 us
  starting transfers between devices: 0.28 us -> 57.7 us
  local copies, waits for them, and re-layouts: 69.5 us -> 13.9 us
  blocking collectives: 75.3 us -> 26.7 us
  matrix products: 50.4 us -> 4.56 us
  between operations: 14.1 us -> 0.38 us
    all_gather x6 -> x0, waiting for transfers between devices: 345 us -> none  [the longest x1 167 us: shards(): gathered = lax.all_gather(layer_norm(middle), 'head', axis=0, tiled=True)]
    reduce_scatter x2 -> x0, waiting for transfers between devices: 332 us -> none  [the longest x1 167 us: shards(): lax.psum_scatter(jnp.dot(returned.reshape(-1, local_width), tout_full, pr...]
    ppermute x0 -> x40, waiting for transfers between devices: none -> 178 us  [the longest x6 85.8 us: to_y(): lax.ppermute(array, AXES, permutation(lambda z, x, c, y: (z, x, c, y + d)))]
    pallas_call x0 -> x2, Pallas kernels: none -> 60 us  [the longest x1 46.3 us: temporal_call(): pl.pallas_call(temporal_kernel, out_shape=[jax.ShapeDtypeStruct((128, 409...]
    ppermute x0 -> x40, starting transfers between devices: none -> 49.9 us  [the longest x12 15.4 us: swap_core(): lax.ppermute(array, AXES, permutation(lambda z, x, c, y: (z, x, 1 - c, y)))]
    all_to_all x2 -> x1, blocking collectives: 75.3 us -> 26.7 us  [shards(): lax.all_to_all(summed, ('z', 'xh', 'c'), split_axis=0, concat_axis=0, til...]
    dot_general x9 -> x2, matrix products: 50.4 us -> 4.56 us  [the longest x1 2.47 us: attend(): jnp.einsum('ighc,jghc->ghij', shaped[0], shaped[1], preferred_element_typ...]
    reshape x5 -> x1, local copies, waits for them, and re-layouts: 30 us -> 1.5 us  [shards(): return finished.astype(jnp.bfloat16).reshape(residual.shape)]
  transfers between devices with their start and end apart: 8 -> 41, of which waited for: 7 -> 17; matrix products, arithmetic and copies ran while one was open for 11% -> 6% of each run, Pallas kernels for 0% -> 4%
where the time goes in v1:
time: 373 us
  waiting for transfers between devices  195 us (52%)
  Pallas kernels  60 us (16%)
  starting transfers between devices  57.7 us (15%)
  blocking collectives  26.7 us (7%)
  other arithmetic  14.3 us (4%)
  local copies, waits for them, and re-layouts  13.9 us (4%)
  matrix products  4.56 us (1%)
    ppermute x6, waiting for transfers between devices, to_y(): lax.ppermute(array, AXES, permutation(lambda z, x, c, y: (z, x, c, y + d)))  85.8 us
    pallas_call x1, Pallas kernels, temporal_call(): pl.pallas_call(temporal_kernel, out_shape=[jax.ShapeDtypeStruct((128, 409...  46.3 us
    ppermute x3, waiting for transfers between devices, from_y(): lax.ppermute(array, AXES, permutation(lambda z, x, c, y: (z, x, c, y - d)))  43.4 us
    all_to_all x1, blocking collectives, shards(): lax.all_to_all(summed, ('z', 'xh', 'c'), split_axis=0, concat_axis=0, til...  26.7 us
    ppermute x9, waiting for transfers between devices, from_first(): lax.ppermute(array, AXES, permutation(lambda z, x, c, y: (z - d * c, x -...  25.9 us
    ppermute x9, waiting for transfers between devices, from_second(): lax.ppermute(array, AXES, permutation(lambda z, x, c, y: (z - d * (1 - c)...  19.3 us
    all_to_all x1, waiting for transfers between devices, shards(): lax.all_to_all(normed, ('z', 'xh', 'c'), split_axis=0, concat_axis=0, til...  17.2 us
    ppermute x12, starting transfers between devices, swap_core(): lax.ppermute(array, AXES, permutation(lambda z, x, c, y: (z, x, 1 - c, y)))  15.4 us
  transfers between devices with their start and end apart: 41, of which 17 were waited for; matrix products, arithmetic and copies ran while one was open for 6% of the time, Pallas kernels for 4%

profile of v1, /device:TPU:1, one launch (start us, length us, event | category | flops | bytes accessed | tf_op | source)
XLA Modules:
  0.0 372.5 jit_solution(8984658094695811817)
XLA Ops:
  0.0 4.6 %collective-permute-start.1 = (bf16[512,256]{1,0:T(8,128)(2,1)}, bf16[512,256]{1,0:T(8,128)(2,1)}, u32[]{:S(2)}, u32[]{:S(2)}) collective-permute-start(bf16[512,256]{1,0:T(8,128)(2,1)} %param.13), channel_id=1, source_target_pairs={{0,17},{1,0},{2,19},{3,2},{4,21},{5,4},{6,23},{7,6},{8,104},{9,105... | collective-permute-start | bytes 786440 | tf_op jit(solution)/shard_map/ppermute | solution.py:44
  10.3 4.1 %collective-permute-done.3 = bf16[512,256]{1,0:T(8,128)(2,1)} collective-permute-done((bf16[512,256]{1,0:T(8,128)(2,1)}, bf16[512,256]{1,0:T(8,128)(2,1)}, u32[]{:S(2)}, u32[]{:S(2)}) %collective-permute-start.3) | collective-permute-done | bytes 262176 | tf_op jit(solution)/shard_map/ppermute | solution.py:44
  14.5 2.2 pad_maximum_fusion.1.rest_0_
  17.6 2.7 collective-permute-start.5
  21.2 2.5 fusion.5
  25.6 2.1 fusion.6
  30.4 9.6 %collective-permute-done.28 = bf16[512,256]{1,0:T(8,128)(2,1)S(1)} collective-permute-done((bf16[512,256]{1,0:T(8,128)(2,1)S(1)}, bf16[512,256]{1,0:T(8,128)(2,1)S(1)}, u32[]{:S(2)}, u32[]{:S(2)}) %collective-permute-start.28) | collective-permute-done | bytes 262176 | tf_op jit(solution)/shard_map/ppermute | solution.py:44
  40.0 12.6 %collective-permute-start.7 = (bf16[4,512,256]{2,1,0:T(8,128)(2,1)}, bf16[4,512,256]{2,1,0:T(8,128)(2,1)S(1)}, u32[]{:S(2)}, u32[]{:S(2)}) collective-permute-start(bf16[4,512,256]{2,1,0:T(8,128)(2,1)} %pad_maximum_fusion.1.rest_0_), channel_id=1, source_target_pairs={{0,8},{1,9},{2,10},{3,11},{4,12},{5,13},{6,14},{7,15},{8,0},{9,1},... | collective-permute-start | bytes 3145736 | tf_op jit(solution)/shard_map/ppermute | solution.py:40
  54.3 3.4 collective-permute-done.other
  58.0 12.2 %collective-permute-done.18 = bf16[3,256,512]{2,1,0:T(8,128)(2,1)S(1)} collective-permute-done((bf16[3,256,512]{2,1,0:T(8,128)(2,1)}, bf16[3,256,512]{2,1,0:T(8,128)(2,1)S(1)}, u32[]{:S(2)}, u32[]{:S(2)}) %collective-permute-start.18) | collective-permute-done | bytes 786464 | tf_op jit(solution)/shard_map/ppermute | solution.py:44
  75.2 3.4 collective-permute-start.31
  79.2 13.7 %spatial_out.1 = (bf16[128,4096]{1,0:T(8,128)(2,1)}, bf16[128,4096]{1,0:T(8,128)(2,1)}, bf16[128,4096]{1,0:T(8,128)(2,1)}, bf16[128,4096]{1,0:T(8,128)(2,1)}) custom-call(s32[5]{0:T(128)} %stack.80.coords, bf16[4,128,512]{2,1,0:T(8,128)(2,1)} %get-tuple-element.24.own, bf16[4,128,512]{2,1,0:T(8,128)(2,1)} %copy-done.23, ...), custom_call_target="tpu_custom_call" | custom-call | flops 4294967296 | bytes 14680064 | tf_op jit(solution)/shard_map/spatial_out/pallas_call | solution.py:126
  95.4 3.0 pad_maximum_fusion.rest_4_
  98.9 7.5 %collective-permute-done.32.rest_15_ = bf16[4,512,256]{2,1,0:T(8,128)(2,1)} collective-permute-done((bf16[4,512,256]{2,1,0:T(8,128)(2,1)S(1)}, bf16[4,512,256]{2,1,0:T(8,128)(2,1)}, u32[]{:S(2)}, u32[]{:S(2)}) %collective-permute-start.32) | collective-permute-done | bytes 1048608 | tf_op jit(solution)/shard_map/ppermute | solution.py:50
  107.2 2.9 collective-permute-start.12
  110.1 10.3 %collective-permute-done.11 = bf16[128,4096]{1,0:T(8,128)(2,1)} collective-permute-done((bf16[128,4096]{1,0:T(8,128)(2,1)}, bf16[128,4096]{1,0:T(8,128)(2,1)}, u32[]{:S(2)}, u32[]{:S(2)}) %collective-permute-start.11) | collective-permute-done | bytes 1048608 | tf_op jit(solution)/shard_map/ppermute | solution.py:32
  120.5 1.8 collective-permute-start.13
  122.3 21.9 %collective-permute-done.12 = bf16[128,4096]{1,0:T(8,128)(2,1)S(1)} collective-permute-done((bf16[128,4096]{1,0:T(8,128)(2,1)S(1)}, bf16[128,4096]{1,0:T(8,128)(2,1)S(1)}, u32[]{:S(2)}, u32[]{:S(2)}) %collective-permute-start.12) | collective-permute-done | bytes 1048608 | tf_op jit(solution)/shard_map/ppermute | solution.py:32
  144.2 12.4 %collective-permute-done.13 = bf16[128,4096]{1,0:T(8,128)(2,1)S(1)} collective-permute-done((bf16[128,4096]{1,0:T(8,128)(2,1)S(1)}, bf16[128,4096]{1,0:T(8,128)(2,1)S(1)}, u32[]{:S(2)}, u32[]{:S(2)}) %collective-permute-start.13) | collective-permute-done | bytes 1048608 | tf_op jit(solution)/shard_map/ppermute | solution.py:32
  159.5 3.1 convert_reduce_fusion
  163.6 9.9 %collective-permute-done.22.rest_7_ = bf16[4,3,256,512]{3,2,1,0:T(8,128)(2,1)} collective-permute-done((bf16[4,3,256,512]{3,2,1,0:T(8,128)(2,1)}, bf16[4,3,256,512]{3,2,1,0:T(8,128)(2,1)}, u32[]{:S(2)}, u32[]{:S(2)}) %collective-permute-start.22) | collective-permute-done | bytes 3145760 | tf_op jit(solution)/shard_map/ppermute | solution.py:50
  176.9 7.8 %all-to-all-start = ((bf16[16,8,4096]{2,1,0:T(8,128)(2,1)}), bf16[16,8,4096]{2,1,0:T(8,128)(2,1)S(1)}, u32[]{:S(2)}, u32[]{:S(2)}) async-start(bf16[16,8,4096]{2,1,0:T(8,128)(2,1)} %fusion.8), calls=%async_computation | async-start | bytes 2097152 | tf_op jit(solution)/shard_map/all_to_all | solution.py:300
  184.7 17.2 %all-to-all-done = bf16[16,8,4096]{2,1,0:T(8,128)(2,1)S(1)} async-done(((bf16[16,8,4096]{2,1,0:T(8,128)(2,1)}), bf16[16,8,4096]{2,1,0:T(8,128)(2,1)S(1)}, u32[]{:S(2)}, u32[]{:S(2)}) %all-to-all-start) | async-done | bytes 1048608 | tf_op jit(solution)/shard_map/all_to_all | solution.py:300
  203.2 2.6 collective-permute-start.15
  205.8 21.2 %collective-permute-done.16.rest_3_ = bf16[128,4096]{1,0:T(8,128)(2,1)S(1)} collective-permute-done((bf16[128,4096]{1,0:T(8,128)(2,1)S(1)}, bf16[128,4096]{1,0:T(8,128)(2,1)S(1)}, u32[]{:S(2)}, u32[]{:S(2)}) %collective-permute-start.16) | collective-permute-done | bytes 1048608 | tf_op jit(solution)/shard_map/ppermute | solution.py:28
  228.4 22.2 %collective-permute-done.15.rest_2_ = bf16[128,4096]{1,0:T(8,128)(2,1)S(1)} collective-permute-done((bf16[128,4096]{1,0:T(8,128)(2,1)S(1)}, bf16[128,4096]{1,0:T(8,128)(2,1)S(1)}, u32[]{:S(2)}, u32[]{:S(2)}) %collective-permute-start.15) | collective-permute-done | bytes 1048608 | tf_op jit(solution)/shard_map/ppermute | solution.py:28
  251.9 46.3 %temporal.1 = (bf16[128,4096]{1,0:T(8,128)(2,1)}, bf16[128,4096]{1,0:T(8,128)(2,1)}, bf16[128,4096]{1,0:T(8,128)(2,1)}, bf16[128,4096]{1,0:T(8,128)(2,1)}) custom-call(s32[5]{0:T(128)} %stack.80.coords, bf16[128,4096]{1,0:T(8,128)(2,1)} %bitcast.40, bf16[128,4096]{1,0:T(8,128)(2,1)} %copy-done.22, bf16[128,4096]{1,0:T(8,128)(2,1)} %copy-done.21, ...), custom_call_target="tpu_custom_call" | custom-call | flops 17179869184 | bytes 41943040 | tf_op jit(solution)/shard_map/temporal/pallas_call | solution.py:218
  300.9 20.7 %collective-permute-done.37 = bf16[128,4096]{1,0:T(8,128)(2,1)S(1)} collective-permute-done((bf16[128,4096]{1,0:T(8,128)(2,1)}, bf16[128,4096]{1,0:T(8,128)(2,1)S(1)}, u32[]{:S(2)}, u32[]{:S(2)}) %collective-permute-start.37) | collective-permute-done | bytes 1048608 | tf_op jit(solution)/shard_map/ppermute | solution.py:32
  321.6 8.4 %collective-permute-done.38 = bf16[128,4096]{1,0:T(8,128)(2,1)S(1)} collective-permute-done((bf16[128,4096]{1,0:T(8,128)(2,1)}, bf16[128,4096]{1,0:T(8,128)(2,1)S(1)}, u32[]{:S(2)}, u32[]{:S(2)}) %collective-permute-start.38) | collective-permute-done | bytes 1048608 | tf_op jit(solution)/shard_map/ppermute | solution.py:32
  330.1 12.1 %collective-permute-done.39 = bf16[128,4096]{1,0:T(8,128)(2,1)S(1)} collective-permute-done((bf16[128,4096]{1,0:T(8,128)(2,1)}, bf16[128,4096]{1,0:T(8,128)(2,1)S(1)}, u32[]{:S(2)}, u32[]{:S(2)}) %collective-permute-start.39) | collective-permute-done | bytes 1048608 | tf_op jit(solution)/shard_map/ppermute | solution.py:32
  342.2 1.9 fusion.7
  344.1 26.7 %all_to_all.10 = bf16[16,8,4096]{2,1,0:T(8,128)(2,1)S(1)} all-to-all(bf16[16,8,4096]{2,1,0:T(8,128)(2,1)S(1)} %fusion.7), channel_id=1, replica_groups=mesh['z'=4,'xh'=2,'c'=2,'y'=4,'xl'=2] {'z','xh','c'}, dimensions={0} | all-to-all | bytes 2097152 | tf_op jit(solution)/shard_map/all_to_all | solution.py:306
  (122 shorter events, 39.2 us)
Async XLA Ops:
  5.9 23.5 %collective-permute-start.27 = (bf16[512,256]{1,0:T(8,128)(2,1)}, bf16[512,256]{1,0:T(8,128)(2,1)}, u32[]{:S(2)}, u32[]{:S(2)}) collective-permute-start(bf16[512,256]{1,0:T(8,128)(2,1)} %param.17), channel_id=1, source_target_pairs={{0,17},{1,0},{2,19},{3,2},{4,21},{5,4},{6,23},{7,6},{8,104},{9,105... | collective-permute-start | bytes 786440 | tf_op jit(solution)/shard_map/ppermute | solution.py:44
  7.3 22.7 %collective-permute-start.29 = (bf16[512,256]{1,0:T(8,128)(2,1)}, bf16[512,256]{1,0:T(8,128)(2,1)}, u32[]{:S(2)}, u32[]{:S(2)}) collective-permute-start(bf16[512,256]{1,0:T(8,128)(2,1)} %param.17), channel_id=1, source_target_pairs={{0,1},{1,16},{2,3},{3,18},{4,5},{5,20},{6,7},{7,22},{8,40},{9,41},... | collective-permute-start | bytes 786440 | tf_op jit(solution)/shard_map/ppermute | solution.py:44
  16.7 36.0 %collective-permute-start.6 = (bf16[4,512,256]{2,1,0:T(8,128)(2,1)}, bf16[4,512,256]{2,1,0:T(8,128)(2,1)}, u32[]{:S(2)}, u32[]{:S(2)}) collective-permute-start(bf16[4,512,256]{2,1,0:T(8,128)(2,1)} %pad_maximum_fusion.1.rest_0_), channel_id=1, source_target_pairs={{0,32},{1,33},{2,34},{3,35},{4,36},{5,37},{6,38},{7,39},{8,9},{9,2... | collective-permute-start | bytes 3145736 | tf_op jit(solution)/shard_map/ppermute | solution.py:50
  17.6 35.1 %collective-permute-start.5 = (bf16[4,512,256]{2,1,0:T(8,128)(2,1)}, bf16[4,512,256]{2,1,0:T(8,128)(2,1)}, u32[]{:S(2)}, u32[]{:S(2)}) collective-permute-start(bf16[4,512,256]{2,1,0:T(8,128)(2,1)} %pad_maximum_fusion.1.rest_0_), channel_id=1, source_target_pairs={{0,64},{1,65},{2,66},{3,67},{4,68},{5,69},{6,70},{7,71},{8,24},{9,... | collective-permute-start | bytes 3145736 | tf_op jit(solution)/shard_map/ppermute | solution.py:50
  20.3 32.8 %collective-permute-start.4 = (bf16[4,512,256]{2,1,0:T(8,128)(2,1)}, bf16[4,512,256]{2,1,0:T(8,128)(2,1)}, u32[]{:S(2)}, u32[]{:S(2)}) collective-permute-start(bf16[4,512,256]{2,1,0:T(8,128)(2,1)} %pad_maximum_fusion.1.rest_0_), channel_id=1, source_target_pairs={{0,96},{1,97},{2,98},{3,99},{4,100},{5,101},{6,102},{7,103},{8,25}... | collective-permute-start | bytes 3145736 | tf_op jit(solution)/shard_map/ppermute | solution.py:50
  29.4 28.3 %collective-permute-start = (bf16[4,128,512]{2,1,0:T(8,128)(2,1)S(1)}, bf16[4,128,512]{2,1,0:T(8,128)(2,1)S(1)}, u32[]{:S(2)}, u32[]{:S(2)}) collective-permute-start(bf16[4,128,512]{2,1,0:T(8,128)(2,1)S(1)} %get-tuple-element.23), channel_id=1, source_target_pairs={{0,1},{1,0},{2,3},{3,2},{4,5},{5,4},{6,7},{7,6},{8,9},{9,8},{10,11... | collective-permute-start | bytes 1572872 | tf_op jit(solution)/shard_map/ppermute | solution.py:36
  40.0 30.4 %collective-permute-start.7 = (bf16[4,512,256]{2,1,0:T(8,128)(2,1)}, bf16[4,512,256]{2,1,0:T(8,128)(2,1)S(1)}, u32[]{:S(2)}, u32[]{:S(2)}) collective-permute-start(bf16[4,512,256]{2,1,0:T(8,128)(2,1)} %pad_maximum_fusion.1.rest_0_), channel_id=1, source_target_pairs={{0,8},{1,9},{2,10},{3,11},{4,12},{5,13},{6,14},{7,15},{8,0},{9,1},... | collective-permute-start | bytes 3145736 | tf_op jit(solution)/shard_map/ppermute | solution.py:40
  52.6 20.2 %collective-permute-start.10 = (bf16[4,512,256]{2,1,0:T(8,128)(2,1)}, bf16[4,512,256]{2,1,0:T(8,128)(2,1)S(1)}, u32[]{:S(2)}, u32[]{:S(2)}) collective-permute-start(bf16[4,512,256]{2,1,0:T(8,128)(2,1)} %collective-permute-done.6.rest_3_), channel_id=1, source_target_pairs={{0,8},{1,9},{2,10},{3,11},{4,12},{5,13},{6,14},{7,15},{8,0},{9,1},... | collective-permute-start | bytes 3145736 | tf_op jit(solution)/shard_map/ppermute | solution.py:40
  52.7 20.3 %collective-permute-start.9 = (bf16[4,512,256]{2,1,0:T(8,128)(2,1)}, bf16[4,512,256]{2,1,0:T(8,128)(2,1)S(1)}, u32[]{:S(2)}, u32[]{:S(2)}) collective-permute-start(bf16[4,512,256]{2,1,0:T(8,128)(2,1)} %collective-permute-done.5.rest_2_), channel_id=1, source_target_pairs={{0,8},{1,9},{2,10},{3,11},{4,12},{5,13},{6,14},{7,15},{8,0},{9,1},... | collective-permute-start | bytes 3145736 | tf_op jit(solution)/shard_map/ppermute | solution.py:40
  70.2 22.7 %collective-permute-start.17 = (bf16[3,256,512]{2,1,0:T(8,128)(2,1)}, bf16[3,256,512]{2,1,0:T(8,128)(2,1)S(1)}, u32[]{:S(2)}, u32[]{:S(2)}) collective-permute-start(bf16[3,256,512]{2,1,0:T(8,128)(2,1)} %get-tuple-element.26), channel_id=1, source_target_pairs={{0,17},{1,0},{2,19},{3,2},{4,21},{5,4},{6,23},{7,6},{8,104},{9,105... | collective-permute-start | bytes 2359304 | tf_op jit(solution)/shard_map/ppermute | solution.py:44
  70.4 23.7 %collective-permute-start.19 = (bf16[3,256,512]{2,1,0:T(8,128)(2,1)}, bf16[3,256,512]{2,1,0:T(8,128)(2,1)}, u32[]{:S(2)}, u32[]{:S(2)}) collective-permute-start(bf16[3,256,512]{2,1,0:T(8,128)(2,1)} %get-tuple-element.26), channel_id=1, source_target_pairs={{0,1},{1,16},{2,3},{3,18},{4,5},{5,20},{6,7},{7,22},{8,40},{9,41},... | collective-permute-start | bytes 2359304 | tf_op jit(solution)/shard_map/ppermute | solution.py:44
  72.9 25.5 %collective-permute-start.33 = (bf16[4,512,256]{2,1,0:T(8,128)(2,1)S(1)}, bf16[4,512,256]{2,1,0:T(8,128)(2,1)}, u32[]{:S(2)}, u32[]{:S(2)}) collective-permute-start(bf16[4,512,256]{2,1,0:T(8,128)(2,1)S(1)} %pad_maximum_fusion.2.rest_12_), channel_id=1, source_target_pairs={{0,8},{1,9},{2,10},{3,11},{4,12},{5,13},{6,14},{7,15},{8,0},{9,1},... | collective-permute-start | bytes 3145736 | tf_op jit(solution)/shard_map/ppermute | solution.py:40
  73.0 33.4 %collective-permute-start.32 = (bf16[4,512,256]{2,1,0:T(8,128)(2,1)S(1)}, bf16[4,512,256]{2,1,0:T(8,128)(2,1)}, u32[]{:S(2)}, u32[]{:S(2)}) collective-permute-start(bf16[4,512,256]{2,1,0:T(8,128)(2,1)S(1)} %pad_maximum_fusion.2.rest_12_), channel_id=1, source_target_pairs={{0,32},{1,33},{2,34},{3,35},{4,36},{5,37},{6,38},{7,39},{8,9},{9,2... | collective-permute-start | bytes 3145736 | tf_op jit(solution)/shard_map/ppermute | solution.py:50
  75.2 31.2 %collective-permute-start.31 = (bf16[4,512,256]{2,1,0:T(8,128)(2,1)S(1)}, bf16[4,512,256]{2,1,0:T(8,128)(2,1)}, u32[]{:S(2)}, u32[]{:S(2)}) collective-permute-start(bf16[4,512,256]{2,1,0:T(8,128)(2,1)S(1)} %pad_maximum_fusion.2.rest_12_), channel_id=1, source_target_pairs={{0,64},{1,65},{2,66},{3,67},{4,68},{5,69},{6,70},{7,71},{8,24},{9,... | collective-permute-start | bytes 3145736 | tf_op jit(solution)/shard_map/ppermute | solution.py:50
  94.1 26.4 %collective-permute-start.11 = (bf16[128,4096]{1,0:T(8,128)(2,1)}, bf16[128,4096]{1,0:T(8,128)(2,1)}, u32[]{:S(2)}, u32[]{:S(2)}) collective-permute-start(bf16[128,4096]{1,0:T(8,128)(2,1)} %get-tuple-element.14), channel_id=1, source_target_pairs={{0,2},{1,3},{2,4},{3,5},{4,6},{5,7},{6,0},{7,1},{8,10},{9,11},{10,... | collective-permute-start | bytes 3145736 | tf_op jit(solution)/shard_map/ppermute | solution.py:32
  98.3 75.2 %collective-permute-start.22 = (bf16[4,3,256,512]{3,2,1,0:T(8,128)(2,1)}, bf16[4,3,256,512]{3,2,1,0:T(8,128)(2,1)}, u32[]{:S(2)}, u32[]{:S(2)}) collective-permute-start(bf16[4,3,256,512]{3,2,1,0:T(8,128)(2,1)} %pad_maximum_fusion.rest_4_), channel_id=1, source_target_pairs={{0,32},{1,33},{2,34},{3,35},{4,36},{5,37},{6,38},{7,39},{8,9},{9,2... | collective-permute-start | bytes 9437192 | tf_op jit(solution)/shard_map/ppermute | solution.py:50
  106.4 67.1 %collective-permute-start.21 = (bf16[4,3,256,512]{3,2,1,0:T(8,128)(2,1)}, bf16[4,3,256,512]{3,2,1,0:T(8,128)(2,1)}, u32[]{:S(2)}, u32[]{:S(2)}) collective-permute-start(bf16[4,3,256,512]{3,2,1,0:T(8,128)(2,1)} %pad_maximum_fusion.rest_4_), channel_id=1, source_target_pairs={{0,64},{1,65},{2,66},{3,67},{4,68},{5,69},{6,70},{7,71},{8,24},{9,... | collective-permute-start | bytes 9437192 | tf_op jit(solution)/shard_map/ppermute | solution.py:50
  106.4 68.7 %collective-permute-start.20 = (bf16[4,3,256,512]{3,2,1,0:T(8,128)(2,1)}, bf16[4,3,256,512]{3,2,1,0:T(8,128)(2,1)}, u32[]{:S(2)}, u32[]{:S(2)}) collective-permute-start(bf16[4,3,256,512]{3,2,1,0:T(8,128)(2,1)} %pad_maximum_fusion.rest_4_), channel_id=1, source_target_pairs={{0,96},{1,97},{2,98},{3,99},{4,100},{5,101},{6,102},{7,103},{8,25}... | collective-permute-start | bytes 9437192 | tf_op jit(solution)/shard_map/ppermute | solution.py:50
  107.2 37.0 %collective-permute-start.12 = (bf16[128,4096]{1,0:T(8,128)(2,1)S(1)}, bf16[128,4096]{1,0:T(8,128)(2,1)S(1)}, u32[]{:S(2)}, u32[]{:S(2)}) collective-permute-start(bf16[128,4096]{1,0:T(8,128)(2,1)S(1)} %copy-done.19), channel_id=1, source_target_pairs={{0,4},{1,5},{2,6},{3,7},{4,0},{5,1},{6,2},{7,3},{8,12},{9,13},{10,... | collective-permute-start | bytes 3145736 | tf_op jit(solution)/shard_map/ppermute | solution.py:32
  120.5 36.1 %collective-permute-start.13 = (bf16[128,4096]{1,0:T(8,128)(2,1)S(1)}, bf16[128,4096]{1,0:T(8,128)(2,1)S(1)}, u32[]{:S(2)}, u32[]{:S(2)}) collective-permute-start(bf16[128,4096]{1,0:T(8,128)(2,1)S(1)} %copy-done.18), channel_id=1, source_target_pairs={{0,6},{1,7},{2,0},{3,1},{4,2},{5,3},{6,4},{7,5},{8,14},{9,15},{10,... | collective-permute-start | bytes 3145736 | tf_op jit(solution)/shard_map/ppermute | solution.py:32
  163.0 40.2 %collective-permute-start.23 = (bf16[4,3,256,512]{3,2,1,0:T(8,128)(2,1)}, bf16[4,3,256,512]{3,2,1,0:T(8,128)(2,1)}, u32[]{:S(2)}, u32[]{:S(2)}) collective-permute-start(bf16[4,3,256,512]{3,2,1,0:T(8,128)(2,1)} %pad_maximum_fusion.rest_4_), channel_id=1, source_target_pairs={{0,8},{1,9},{2,10},{3,11},{4,12},{5,13},{6,14},{7,15},{8,0},{9,1},... | collective-permute-start | bytes 9437192 | tf_op jit(solution)/shard_map/ppermute | solution.py:40
  163.1 21.6 %collective-permute-start.34 = (bf16[4,512,256]{2,1,0:T(8,128)(2,1)}, bf16[4,512,256]{2,1,0:T(8,128)(2,1)S(1)}, u32[]{:S(2)}, u32[]{:S(2)}) collective-permute-start(bf16[4,512,256]{2,1,0:T(8,128)(2,1)} %collective-permute-done.30.rest_13_), channel_id=1, source_target_pairs={{0,8},{1,9},{2,10},{3,11},{4,12},{5,13},{6,14},{7,15},{8,0},{9,1},... | collective-permute-start | bytes 3145736 | tf_op jit(solution)/shard_map/ppermute | solution.py:40
  173.5 78.1 %collective-permute-start.26 = (bf16[4,3,256,512]{3,2,1,0:T(8,128)(2,1)}, bf16[4,3,256,512]{3,2,1,0:T(8,128)(2,1)}, u32[]{:S(2)}, u32[]{:S(2)}) collective-permute-start(bf16[4,3,256,512]{3,2,1,0:T(8,128)(2,1)} %collective-permute-done.22.rest_7_), channel_id=1, source_target_pairs={{0,8},{1,9},{2,10},{3,11},{4,12},{5,13},{6,14},{7,15},{8,0},{9,1},... | collective-permute-start | bytes 9437192 | tf_op jit(solution)/shard_map/ppermute | solution.py:40
  173.5 78.0 %collective-permute-start.25 = (bf16[4,3,256,512]{3,2,1,0:T(8,128)(2,1)}, bf16[4,3,256,512]{3,2,1,0:T(8,128)(2,1)}, u32[]{:S(2)}, u32[]{:S(2)}) collective-permute-start(bf16[4,3,256,512]{3,2,1,0:T(8,128)(2,1)} %collective-permute-done.21.rest_6_), channel_id=1, source_target_pairs={{0,8},{1,9},{2,10},{3,11},{4,12},{5,13},{6,14},{7,15},{8,0},{9,1},... | collective-permute-start | bytes 9437192 | tf_op jit(solution)/shard_map/ppermute | solution.py:40
  175.2 76.4 %collective-permute-start.24 = (bf16[4,3,256,512]{3,2,1,0:T(8,128)(2,1)}, bf16[4,3,256,512]{3,2,1,0:T(8,128)(2,1)}, u32[]{:S(2)}, u32[]{:S(2)}) collective-permute-start(bf16[4,3,256,512]{3,2,1,0:T(8,128)(2,1)} %collective-permute-done.20.rest_5_), channel_id=1, source_target_pairs={{0,8},{1,9},{2,10},{3,11},{4,12},{5,13},{6,14},{7,15},{8,0},{9,1},... | collective-permute-start | bytes 9437192 | tf_op jit(solution)/shard_map/ppermute | solution.py:40
  176.9 25.0 %all-to-all-start = ((bf16[16,8,4096]{2,1,0:T(8,128)(2,1)}), bf16[16,8,4096]{2,1,0:T(8,128)(2,1)S(1)}, u32[]{:S(2)}, u32[]{:S(2)}) async-start(bf16[16,8,4096]{2,1,0:T(8,128)(2,1)} %fusion.8), calls=%async_computation | async-start | bytes 2097152 | tf_op jit(solution)/shard_map/all_to_all | solution.py:300
  201.9 25.1 %collective-permute-start.16 = (bf16[128,4096]{1,0:T(8,128)(2,1)S(1)}, bf16[128,4096]{1,0:T(8,128)(2,1)S(1)}, u32[]{:S(2)}, u32[]{:S(2)}) collective-permute-start(bf16[128,4096]{1,0:T(8,128)(2,1)S(1)} %bitcast.37), channel_id=1, source_target_pairs={{0,2},{1,3},{2,4},{3,5},{4,6},{5,7},{6,0},{7,1},{8,10},{9,11},{10,... | collective-permute-start | bytes 3145736 | tf_op jit(solution)/shard_map/ppermute | solution.py:28
  203.2 47.4 %collective-permute-start.15 = (bf16[128,4096]{1,0:T(8,128)(2,1)S(1)}, bf16[128,4096]{1,0:T(8,128)(2,1)S(1)}, u32[]{:S(2)}, u32[]{:S(2)}) collective-permute-start(bf16[128,4096]{1,0:T(8,128)(2,1)S(1)} %bitcast.38), channel_id=1, source_target_pairs={{0,4},{1,5},{2,6},{3,7},{4,0},{5,1},{6,2},{7,3},{8,12},{9,13},{10,... | collective-permute-start | bytes 3145736 | tf_op jit(solution)/shard_map/ppermute | solution.py:28
  227.0 23.6 %collective-permute-start.14 = (bf16[128,4096]{1,0:T(8,128)(2,1)S(1)}, bf16[128,4096]{1,0:T(8,128)(2,1)S(1)}, u32[]{:S(2)}, u32[]{:S(2)}) collective-permute-start(bf16[128,4096]{1,0:T(8,128)(2,1)S(1)} %bitcast.39), channel_id=1, source_target_pairs={{0,6},{1,7},{2,0},{3,1},{4,2},{5,3},{6,4},{7,5},{8,14},{9,15},{10,... | collective-permute-start | bytes 3145736 | tf_op jit(solution)/shard_map/ppermute | solution.py:28
  298.2 23.4 %collective-permute-start.37 = (bf16[128,4096]{1,0:T(8,128)(2,1)}, bf16[128,4096]{1,0:T(8,128)(2,1)S(1)}, u32[]{:S(2)}, u32[]{:S(2)}) collective-permute-start(bf16[128,4096]{1,0:T(8,128)(2,1)} %get-tuple-element.18), channel_id=1, source_target_pairs={{0,2},{1,3},{2,4},{3,5},{4,6},{5,7},{6,0},{7,1},{8,10},{9,11},{10,... | collective-permute-start | bytes 3145736 | tf_op jit(solution)/shard_map/ppermute | solution.py:32
  298.3 31.8 %collective-permute-start.38 = (bf16[128,4096]{1,0:T(8,128)(2,1)}, bf16[128,4096]{1,0:T(8,128)(2,1)S(1)}, u32[]{:S(2)}, u32[]{:S(2)}) collective-permute-start(bf16[128,4096]{1,0:T(8,128)(2,1)} %get-tuple-element.19), channel_id=1, source_target_pairs={{0,4},{1,5},{2,6},{3,7},{4,0},{5,1},{6,2},{7,3},{8,12},{9,13},{10,... | collective-permute-start | bytes 3145736 | tf_op jit(solution)/shard_map/ppermute | solution.py:32
  299.6 42.6 %collective-permute-start.39 = (bf16[128,4096]{1,0:T(8,128)(2,1)}, bf16[128,4096]{1,0:T(8,128)(2,1)S(1)}, u32[]{:S(2)}, u32[]{:S(2)}) collective-permute-start(bf16[128,4096]{1,0:T(8,128)(2,1)} %get-tuple-element.20), channel_id=1, source_target_pairs={{0,6},{1,7},{2,0},{3,1},{4,2},{5,3},{6,4},{7,5},{8,14},{9,15},{10,... | collective-permute-start | bytes 3145736 | tf_op jit(solution)/shard_map/ppermute | solution.py:32
  (33 other events, 501.5 us)

commit v2 on v0

v2 whole, which is shorter than its diff:
```python
import numpy as np

import jax
import jax.numpy as jnp
from jax import lax
from jax.experimental import pallas as pl
from jax.experimental.pallas import tpu as pltpu
from jax.sharding import Mesh
from jax.sharding import PartitionSpec as P

HDIM = 128
AXES = ("z", "xh", "c", "y", "xl")
SIZES = (4, 2, 2, 4, 2)
RING = 4
SHORT = pl.CostEstimate(flops=1 << 20, bytes_accessed=1 << 16, transcendentals=0)
VMEM_LIMIT = 28 * 1024 * 1024


def permutation(move):
    pairs = []
    for source in range(int(np.prod(SIZES))):
        z, xh, c, y, xl = (int(v) for v in np.unravel_index(source, SIZES))
        z, x, c, y = (v % n for v, n in zip(move(z, 2 * xh + xl, c, y), (4, 4, 2, 4)))
        pairs.append((source, int(np.ravel_multi_index((z, x // 2, c, y, x % 2), SIZES))))
    return pairs


def from_y(array, d):
    return lax.ppermute(array, AXES, permutation(lambda z, x, c, y: (z, x, c, y - d)))


def to_y(array, d):
    return lax.ppermute(array, AXES, permutation(lambda z, x, c, y: (z, x, c, y + d)))


def swap_xl(array):
    return lax.ppermute(array, AXES, permutation(lambda z, x, c, y: (z, x ^ 1, c, y)))


def swap_core(array):
    return lax.ppermute(array, AXES, permutation(lambda z, x, c, y: (z, x, 1 - c, y)))


def from_first(array, d):
    return lax.ppermute(
        array, AXES, permutation(lambda z, x, c, y: (z - d * c, x - d * (1 - c), c, y))
    )


def from_second(array, d):
    return lax.ppermute(
        array, AXES, permutation(lambda z, x, c, y: (z - d * (1 - c), x - d * c, c, y))
    )


def after(array, *others):
    return lax.optimization_barrier((array,) + others)[0]


def ring_spots(coords, spots):
    z, x, c = coords[0], coords[1], coords[2]
    found = []
    for n, (j, first, count) in enumerate(spots):
        for k in range(count):
            i = first + k
            px = lax.rem(x + i + c * (j - i), RING)
            pz = lax.rem(z + j + c * (i - j), RING)
            found.append((n, k, pz * 2 + lax.div(px, 2), lax.rem(px, 2)))
    return found


def load(coords, pieces, shapes, copies_of, name, previous=()):
    count = len(shapes)

    def kernel(coords, *rest):
        refs, weights, sems = rest[: len(pieces)], rest[-1 - count : -1], rest[-1]
        copies = [
            pltpu.make_async_copy(source, target, sems.at[n])
            for n, (source, target) in enumerate(copies_of(coords, refs, weights))
        ]
        for copy in copies:
            copy.start()
        for copy in copies:
            copy.wait()

    in_vmem = pl.BlockSpec(memory_space=pltpu.VMEM)
    return pl.pallas_call(
        kernel,
        out_shape=[pltpu.VMEM(shape, jnp.bfloat16) for shape in shapes],
        in_specs=[pl.BlockSpec(memory_space=pltpu.SMEM)]
        + [pl.BlockSpec(memory_space=pltpu.HBM)] * len(pieces)
        + [in_vmem] * len(previous),
        out_specs=[in_vmem] * count,
        input_output_aliases={1 + len(pieces) + n: n for n in range(len(previous))},
        scratch_shapes=[pltpu.SemaphoreType.DMA((32 * count,))],
        compiler_params=pltpu.CompilerParams(vmem_limit_bytes=VMEM_LIMIT),
        cost_estimate=SHORT,
        name=name,
    )(
        coords,
        *[pltpu.with_memory_space_constraint(piece, pltpu.HBM) for piece in pieces],
        *[pltpu.with_memory_space_constraint(array, pltpu.VMEM) for array in previous],
    )


def load_temporal(coords, pieces, spots, previous=()):
    def copies(coords, refs, weights):
        for n, entry, zx, xl in ring_spots(coords, spots):
            for r in range(2):
                s = zx * 2 + coords[2] + r - 2 * r * coords[2]
                rows = pl.ds(pl.multiple_of(s * 256, 256), 256)
                for w, weight in enumerate(weights[:3]):
                    yield refs[n].at[entry, 4 * r + w], weight.at[xl, rows]
                yield refs[n].at[entry, 4 * r + 3], weights[3].at[s, xl]

    shapes = [(2, 4096, 256)] * 3 + [(16, 2, 256, 256)]
    return load(coords, pieces, shapes, copies, "load_temporal", previous)


def load_out(coords, pieces):
    def copies(coords, refs, weights):
        for n, entry, zx, xl in ring_spots(coords, [(j, 0, RING) for j in range(RING)]):
            yield refs[n].at[entry], weights[0].at[zx, pl.ds(xl * 2, 2)]

    return load(coords, pieces, [(8, 4, 256, 256)], copies, "load_out")[0]


def project_out(context, weight, outs):
    starts = np.cumsum([0] + [out.shape[0] for out in outs])

    def step(n, carry):
        part = jnp.dot(
            context[...], weight[n].reshape(-1, 256), preferred_element_type=jnp.float32
        ).astype(jnp.bfloat16)
        columns = pl.ds(pl.multiple_of(n * 256, 256), 256)
        for start, out in zip(starts, outs):
            out[:, columns] = part[start : start + out.shape[0]]
        return carry

    lax.fori_loop(0, weight.shape[0], step, 0)


def spatial_out_kernel(coords, *rest):
    sources, weight, outs, context = rest[:4], rest[4], rest[5:-1], rest[-1]
    y, xl = coords[3], coords[4]
    for d in range(RING):
        block = lax.rem(y + d, RING)
        for n, source in enumerate(sources):
            half = xl + (n % 2) * (1 - 2 * xl)
            columns = pl.ds(pl.multiple_of(half * 512, 512), 512)
            start = d * 256 + (n // 2) * 128
            context[start : start + 128, columns] = source[block]
    project_out(context, weight, outs)


def spatial_out_call(coords, sources, weight):
    in_vmem = pl.BlockSpec(memory_space=pltpu.VMEM)
    return pl.pallas_call(
        spatial_out_kernel,
        out_shape=[jax.ShapeDtypeStruct((256, 2048), jnp.bfloat16)] * RING,
        in_specs=[pl.BlockSpec(memory_space=pltpu.SMEM)] + [in_vmem] * 5,
        out_specs=[in_vmem] * RING,
        scratch_shapes=[pltpu.VMEM((1024, 1024), jnp.bfloat16)],
        compiler_params=pltpu.CompilerParams(vmem_limit_bytes=VMEM_LIMIT),
        cost_estimate=SHORT,
        name="spatial_out",
    )(coords, *sources, pltpu.with_memory_space_constraint(weight, pltpu.VMEM))


def temporal_call(blocks, weights):
    sizes = [block.shape[0] for block in blocks]
    total = sum(sizes)
    count = total // 128
    shapes = [(128, 4096)] * (count // 2) + [(64 * count, 4096)]

    def kernel(*rest):
        tokens, rest = rest[: len(sizes)], rest[len(sizes) :]
        weights, last, outs = rest[:3], rest[3], rest[4:-3]
        rows, projected, context = rest[-3:]
        start = 0
        for token, size in zip(tokens, sizes):
            rows[start : start + size] = token[...]
            start += size

        for w, weight in enumerate(weights):

            def project(n, carry, w=w, weight=weight):
                part = jnp.dot(rows[...], weight[n], preferred_element_type=jnp.float32)
                columns = pl.ds(pl.multiple_of(n * 256, 256), 256)
                projected[w, :, columns] = part.astype(jnp.bfloat16)
                return carry

            lax.fori_loop(0, 2, project, 0)
        video = lax.rem(lax.div(lax.broadcasted_iota(jnp.int32, (128, 128), 0), 2), 4)
        video_key = lax.rem(lax.div(lax.broadcasted_iota(jnp.int32, (128, 128), 1), 2), 4)
        same = video == video_key
        heads = [slice(h * HDIM, (h + 1) * HDIM) for h in range(4)]
        for b in range(count):
            at = slice(b * 128, (b + 1) * 128)
            scores = [
                lax.dot_general(
                    projected[0, at, h],
                    projected[1, at, h],
                    (((1,), (1,)), ((), ())),
                    preferred_element_type=jnp.float32,
                )
                for h in heads
            ]
            exponents = [jnp.where(same, jnp.exp(s * HDIM ** (-0.5)), 0.0) for s in scores]
            shares = [
                (e / jnp.sum(e, axis=-1, keepdims=True)).astype(jnp.bfloat16) for e in exponents
            ]
            for h, share in zip(heads, shares):
                context[at, h] = jnp.dot(
                    share, projected[2, at, h], preferred_element_type=jnp.float32
                ).astype(jnp.bfloat16)
        project_out(context, last, outs)

    in_vmem = pl.BlockSpec(memory_space=pltpu.VMEM)
    return pl.pallas_call(
        kernel,
        out_shape=[jax.ShapeDtypeStruct(shape, jnp.bfloat16) for shape in shapes],
        in_specs=[in_vmem] * (len(sizes) + 4),
        out_specs=[in_vmem] * len(shapes),
        scratch_shapes=[
            pltpu.VMEM((total, 4096), jnp.bfloat16),
            pltpu.VMEM((3, total, 512), jnp.bfloat16),
            pltpu.VMEM((total, 512), jnp.bfloat16),
        ],
        compiler_params=pltpu.CompilerParams(vmem_limit_bytes=VMEM_LIMIT),
        cost_estimate=SHORT,
        name="temporal",
    )(
        *blocks,
        *[pltpu.with_memory_space_constraint(w, pltpu.VMEM) for w in weights],
    )


def spatial_scores(queries, keys_in, values_in):
    shaped = [
        member.reshape(member.shape[:2] + (-1, HDIM)) for member in (queries, keys_in, values_in)
    ]
    scores = jnp.einsum(
        "ighc,jghc->ghij", shaped[0], shaped[1], preferred_element_type=jnp.float32
    ) * HDIM ** (-0.5)
    exponent = jnp.exp(scores)
    weights = (exponent / jnp.sum(exponent, axis=-1, keepdims=True)).astype(jnp.bfloat16)
    return weights, shaped[2]


def spatial_context(weights, values_in):
    context = jnp.einsum(
        "ghij,jghc->ighc", weights, values_in, preferred_element_type=jnp.float32
    )
    return context.astype(jnp.bfloat16)


def norm_call(coords, residual, mine, other):
    def kernel(coords, res, mine, other, middle, normed, total):
        c = coords[2]
        for n in range(8):
            for part, core in ((mine, c), (other, 1 - c)):
                columns = pl.ds(pl.multiple_of(n * 512 + core * 256, 256), 256)
                total[:, columns] = part[:, n * 256 : (n + 1) * 256]

        def step(n, carry):
            rows = pl.ds(pl.multiple_of(n * 16, 16), 16)
            summed = res[rows].astype(jnp.float32) + total[rows].astype(jnp.float32)
            rounded = summed.astype(jnp.bfloat16)
            middle[rows] = rounded
            values = rounded.astype(jnp.float32)
            centred = values - jnp.mean(values, axis=-1, keepdims=True)
            variance = jnp.mean(centred * centred, axis=-1, keepdims=True)
            normed[rows] = (centred * lax.rsqrt(variance + 1e-06)).astype(jnp.bfloat16)
            return carry

        lax.fori_loop(0, 8, step, 0)

    in_vmem = pl.BlockSpec(memory_space=pltpu.VMEM)
    rows = jax.ShapeDtypeStruct((128, 4096), jnp.bfloat16)
    return pl.pallas_call(
        kernel,
        out_shape=[rows, rows],
        in_specs=[pl.BlockSpec(memory_space=pltpu.SMEM)] + [in_vmem] * 3,
        out_specs=[in_vmem] * 2,
        scratch_shapes=[pltpu.VMEM((128, 4096), jnp.bfloat16)],
        compiler_params=pltpu.CompilerParams(vmem_limit_bytes=VMEM_LIMIT),
        cost_estimate=SHORT,
        name="norm",
    )(coords, residual, mine, other)


def shards(
    residual,
    spatial_query,
    spatial_key,
    spatial_value,
    spatial_out,
    temporal_query,
    temporal_key,
    temporal_value,
    temporal_out,
):
    z, xh, c, y, xl = (lax.axis_index(name) for name in AXES)
    coords = jnp.stack([z, 2 * xh + xl, c, y, xl]).astype(jnp.int32)

    layout = (128, 8, 512)
    scores, values_in = spatial_scores(
        *(array.reshape(layout) for array in (spatial_query, spatial_key, spatial_value))
    )

    context = spatial_context(scores, values_in).reshape(RING, 2, 128, 512)
    own, other = (
        lax.dynamic_index_in_dim(context, which, axis=1, keepdims=False) for which in (xl, 1 - xl)
    )

    out_shard = spatial_out.reshape(2, 256, 256)
    out_first = jnp.stack([out_shard] + [from_first(out_shard, d) for d in range(1, RING)])
    out_first, own, other = lax.optimization_barrier((out_first, own, other))
    out_own = [out_first] + [from_second(out_first, d) for d in range(1, RING)]
    other = swap_xl(other)
    sources = [own, other, swap_core(own)]
    *sources, o_1, o_2, o_3 = lax.optimization_barrier((*sources, *out_own[1:]))
    out_own[1:] = o_1, o_2, o_3
    sources.append(swap_core(sources[1]))
    tiles = jnp.stack(
        [w.reshape(256, 2, 256) for w in (temporal_query, temporal_key, temporal_value)]
        + [temporal_out.reshape(2, 256, 256).swapaxes(0, 1)]
    ).transpose(2, 0, 1, 3)
    mine, theirs = (
        lax.dynamic_index_in_dim(tiles, which, axis=0, keepdims=False) for which in (c, 1 - c)
    )
    shard = after(jnp.concatenate([mine, swap_core(theirs)]), *out_own[1:])
    shards_first = [shard] + [from_first(shard, d) for d in range(1, RING)]
    *sources, residual_rows = lax.optimization_barrier((*sources, residual.reshape(128, 4096)))
    parts = spatial_out_call(coords, sources, load_out(coords, out_own))

    far = [to_y(parts[2][:128], 1), to_y(parts[2][128:], -1)]
    near_p = jnp.concatenate([parts[1][:128] + far[0], parts[1][128:]])
    near_m = jnp.concatenate([parts[3][:128], parts[3][128:] + far[1]])
    first = jnp.stack(lax.optimization_barrier((*shards_first, *far))[:RING])
    first, near_p, near_m = lax.optimization_barrier((first, near_p, near_m))
    pieces = [first, from_second(first, 1), from_second(first, -1)]
    total = parts[0].astype(jnp.float32)
    for part in (to_y(near_p, 1), to_y(near_m, -1)):
        total = total + part.astype(jnp.float32)
    total = total.astype(jnp.bfloat16)
    middle, normed = norm_call(coords, residual_rows, total[:128], swap_core(total[128:]))
    normed = lax.all_to_all(
        normed.reshape(16, 8, 4096), ("z", "xh", "c"), split_axis=0, concat_axis=0, tiled=True
    ).reshape(128, 4096)
    normed, *pieces = lax.optimization_barrier((normed, *pieces))
    next_p, next_m = from_y(normed, 1), from_y(normed, -1)
    last = [from_second(pieces[1][:2], 1), from_second(pieces[2][2:], -1)]
    weights = load_temporal(coords, pieces, [(j, 0, RING) for j in (0, 1, 3)])
    *last, next_p, next_m, w_0, w_1, w_2, w_3 = lax.optimization_barrier(
        (*last, next_p, next_m, *weights)
    )
    weights = [w_0, w_1, w_2, w_3]
    weights = load_temporal(coords, last, [(2, 0, 2), (2, 2, 2)], weights)

    far = [from_y(next_p[:64], 1), from_y(next_m[64:], -1)]
    *far, w_0, w_1, w_2, w_3 = lax.optimization_barrier((*far, *weights))
    weights = [w_0, w_1, w_2, w_3]

    def both_cores(blocks):
        *parts, others = temporal_call(blocks + [swap_core(block) for block in blocks], weights)
        others = swap_core(others)
        return [
            part.astype(jnp.float32) + others[128 * n : 128 * (n + 1)].astype(jnp.float32)
            for n, part in enumerate(parts)
        ]

    part_p, part_m, part_far = both_cores([next_p, next_m] + far)
    part_far = part_far.astype(jnp.bfloat16)
    far = [to_y(part_far[:64], 1), to_y(part_far[64:], -1)]
    zeros = jnp.zeros((64, 4096), jnp.bfloat16)
    part_p += jnp.concatenate([far[0], zeros]).astype(jnp.float32)
    part_m += jnp.concatenate([zeros, far[1]]).astype(jnp.float32)
    (total,) = both_cores([normed])
    for part, d in ((part_p, 1), (part_m, -1)):
        total = total + to_y(part.astype(jnp.bfloat16), d).astype(jnp.float32)
    summed = total.astype(jnp.bfloat16).reshape(16, 8, 4096)
    summed = lax.all_to_all(summed, ("z", "xh", "c"), split_axis=0, concat_axis=0, tiled=True)
    finished = middle.astype(jnp.float32) + summed.reshape(128, 4096).astype(jnp.float32)
    return finished.astype(jnp.bfloat16).reshape(residual.shape)


def solution(mesh):
    split = Mesh(mesh.devices.reshape(SIZES), AXES)
    seq, head = ("z", "xh", "c"), ("y", "xl")
    in_specs = (
        P(head, None, seq, None),
        P(None, None, seq, head),
        P(None, None, seq, head),
        P(None, None, seq, head),
        P(head, seq),
        P(seq, head),
        P(seq, head),
        P(seq, head),
        P(head, seq),
    )
    out_specs = P(head, None, seq, None)
    return jax.shard_map(shards, mesh=split, in_specs=in_specs, out_specs=out_specs, check_vma=False)
```

time: 907 us -> 296 us (0.33)
  waiting for transfers between devices: 680 us -> 122 us
  local copies, waits for them, and re-layouts: 69.5 us -> 13.9 us
  Pallas kernels: 0 us -> 51.9 us
  matrix products: 50.4 us -> 2.01 us
  starting transfers between devices: 0.28 us -> 43.6 us
  blocking collectives: 75.3 us -> 52.8 us
  between operations: 14.1 us -> 0.43 us
    all_gather x6 -> x0, waiting for transfers between devices: 345 us -> none  [the longest x1 167 us: shards(): gathered = lax.all_gather(layer_norm(middle), 'head', axis=0, tiled=True)]
    reduce_scatter x2 -> x0, waiting for transfers between devices: 332 us -> none  [the longest x1 167 us: shards(): lax.psum_scatter(jnp.dot(returned.reshape(-1, local_width), tout_full, pr...]
    ppermute x0 -> x37, waiting for transfers between devices: none -> 122 us  [the longest x8 45.3 us: to_y(): lax.ppermute(array, AXES, permutation(lambda z, x, c, y: (z, x, c, y + d)))]
    pallas_call x0 -> x7, Pallas kernels: none -> 51.9 us  [the longest x2 29.4 us: temporal_call(): pl.pallas_call(kernel, out_shape=[jax.ShapeDtypeStruct(shape, jnp.bfloat1...]
    dot_general x9 -> x2, matrix products: 50.4 us -> 2.01 us  [the longest x1 1.14 us: spatial_scores(): jnp.einsum('ighc,jghc->ghij', shaped[0], shaped[1], preferred_element_typ...]
    ppermute x0 -> x37, starting transfers between devices: none -> 43.6 us  [the longest x11 11.5 us: swap_core(): lax.ppermute(array, AXES, permutation(lambda z, x, c, y: (z, x, 1 - c, y)))]
    reshape x5 -> x2, local copies, waits for them, and re-layouts: 30 us -> 2.96 us  [the longest x1 1.5 us: shards(): return finished.astype(jnp.bfloat16).reshape(residual.shape)]
    all_to_all x2, blocking collectives: 75.3 us -> 52.8 us  [the longest x1 31.2 us: shards(): lax.all_to_all(normed.reshape(16, 8, 4096), ('z', 'xh', 'c'), split_axis=...]
  transfers between devices with their start and end apart: 8 -> 37, of which waited for: 7 -> 17; matrix products, arithmetic and copies ran while one was open for 11% -> 5% of each run, Pallas kernels for 0% -> 11%
where the time goes in v2:
time: 296 us; the launch traced here: 295 us
  waiting for transfers between devices  122 us (41%)
  blocking collectives  52.8 us (18%)
  Pallas kernels  51.9 us (18%)
  starting transfers between devices  43.6 us (15%)
  local copies, waits for them, and re-layouts  13.9 us (5%)
  other arithmetic  8.94 us (3%)
    ppermute x8, waiting for transfers between devices, to_y(): lax.ppermute(array, AXES, permutation(lambda z, x, c, y: (z, x, c, y + d)))  45.3 us
    all_to_all x1, blocking collectives, shards(): lax.all_to_all(normed.reshape(16, 8, 4096), ('z', 'xh', 'c'), split_axis=...  31.2 us
    pallas_call x2, Pallas kernels, temporal_call(): pl.pallas_call(kernel, out_shape=[jax.ShapeDtypeStruct(shape, jnp.bfloat1...  29.4 us
    ppermute x1, waiting for transfers between devices, swap_xl(): lax.ppermute(array, AXES, permutation(lambda z, x, c, y: (z, x ^ 1, c, y)))  27.2 us
    ppermute x4, waiting for transfers between devices, from_y(): lax.ppermute(array, AXES, permutation(lambda z, x, c, y: (z, x, c, y - d)))  25.6 us
    all_to_all x1, blocking collectives, shards(): lax.all_to_all(summed, ('z', 'xh', 'c'), split_axis=0, concat_axis=0, til...  21.6 us
    pallas_call x3, Pallas kernels, load(): pl.pallas_call(kernel, out_shape=[pltpu.VMEM(shape, jnp.bfloat16) for sha...  13.3 us
    ppermute x6, waiting for transfers between devices, from_first(): lax.ppermute(array, AXES, permutation(lambda z, x, c, y: (z - d * c, x -...  12.7 us
  transfers between devices with their start and end apart: 37, of which 17 were waited for; matrix products, arithmetic and copies ran while one was open for 5% of the time, Pallas kernels for 11%

profile of v2, /device:TPU:1, one launch (start us, length us, event | category | flops | bytes accessed | tf_op | source)
XLA Modules:
  0.0 295.3 jit_solution(2569548511326835305)
XLA Ops:
  0.0 4.6 %collective-permute-start = (bf16[2,256,256]{2,1,0:T(8,128)(2,1)}, bf16[2,256,256]{2,1,0:T(8,128)(2,1)}, u32[]{:S(2)}, u32[]{:S(2)}) collective-permute-start(bf16[2,256,256]{2,1,0:T(8,128)(2,1)} %bitcast.43), channel_id=1, source_target_pairs={{0,17},{1,0},{2,19},{3,2},{4,21},{5,4},{6,23},{7,6},{8,104},{9,105... | collective-permute-start | bytes 786440 | tf_op jit(solution)/shard_map/ppermute | solution.py:45
  5.3 1.7 reshape_reshape.10
  7.8 1.7 reshape_reshape.11
  15.7 2.3 collective-permute-start.5
  19.1 2.8 collective-permute-start.4
  25.6 27.2 %collective-permute-done.3.rest_1_ = bf16[4,128,512]{2,1,0:T(8,128)(2,1)S(1)} collective-permute-done((bf16[4,128,512]{2,1,0:T(8,128)(2,1)}, bf16[4,128,512]{2,1,0:T(8,128)(2,1)S(1)}, u32[]{:S(2)}, u32[]{:S(2)}) %collective-permute-start.3) | collective-permute-done | bytes 524320 | tf_op jit(solution)/shard_map/ppermute | solution.py:37
  55.0 1.8 collective-permute-start.11
  58.3 3.0 %load_out.1.rest_4_ = bf16[8,4,256,256]{3,2,1,0:T(8,128)(2,1)S(1)} custom-call(s32[5]{0:T(128)S(1)} %stack.56.coords, bf16[4,2,256,256]{3,2,1,0:T(8,128)(2,1)} %copy-done.3, bf16[4,2,256,256]{3,2,1,0:T(8,128)(2,1)} %collective-permute-done.5.rest_1_, bf16[4,2,256,256]{3,2,1,0:T(8,128)(2,1)} %collective-permute-done.6.rest_2_, ...), custom_call_target="tpu_custom_call" | custom-call | flops 1048576 | bytes 65536 | tf_op jit(solution)/shard_map/load_out/pallas_call | solution.py:87
  61.4 6.4 %spatial_out.1 = (bf16[256,2048]{1,0:T(8,128)(2,1)S(1)}, bf16[256,2048]{1,0:T(8,128)(2,1)S(1)}, bf16[256,2048]{1,0:T(8,128)(2,1)S(1)}, bf16[256,2048]{1,0:T(8,128)(2,1)S(1)}) custom-call(s32[5]{0:T(128)S(1)} %stack.56.coords, bf16[4,128,512]{2,1,0:T(8,128)(2,1)S(1)} %get-tuple-element.72.rest_0_, bf16[4,128,512]{2,1,0:T(8,128)(2,1)S(1)} %collective-permute-done.3.rest_1_, ...), custom_call_target="tpu_custom_call" | custom-call | flops 1048576 | bytes 65536 | tf_op jit(solution)/shard_map/spatial_out/pallas_call | solution.py:158
  67.8 2.8 collective-permute-start.14
  70.8 11.2 %collective-permute-done.12 = bf16[8,256,256]{2,1,0:T(8,128)(2,1)} collective-permute-done((bf16[8,256,256]{2,1,0:T(8,128)(2,1)}, bf16[8,256,256]{2,1,0:T(8,128)(2,1)}, u32[]{:S(2)}, u32[]{:S(2)}) %collective-permute-start.12) | collective-permute-done | bytes 1048608 | tf_op jit(solution)/shard_map/ppermute | solution.py:45
  83.5 2.4 pad_maximum_fusion.rest_0_
  86.0 3.4 %collective-permute-start.18 = (bf16[4,8,256,256]{3,2,1,0:T(8,128)(2,1)S(1)}, bf16[4,8,256,256]{3,2,1,0:T(8,128)(2,1)S(1)}, u32[]{:S(2)}, u32[]{:S(2)}) collective-permute-start(bf16[4,8,256,256]{3,2,1,0:T(8,128)(2,1)S(1)} %pad_maximum_fusion.rest_0_), channel_id=1, source_target_pairs={{0,96},{1,97},{2,98},{3,99},{4,100},{5,101},{6,102},{7,103},{8,25}... | collective-permute-start | bytes 12582920 | tf_op jit(solution)/shard_map/ppermute | solution.py:51
  89.3 2.7 collective-permute-start.16
  92.0 20.3 %collective-permute-done.15 = bf16[256,2048]{1,0:T(8,128)(2,1)S(1)} collective-permute-done((bf16[256,2048]{1,0:T(8,128)(2,1)S(1)}, bf16[256,2048]{1,0:T(8,128)(2,1)S(1)}, u32[]{:S(2)}, u32[]{:S(2)}) %collective-permute-start.15) | collective-permute-done | bytes 1048608 | tf_op jit(solution)/shard_map/ppermute | solution.py:33
  113.0 3.9 %collective-permute-start.17 = (bf16[128,2048]{1,0:T(8,128)(2,1)S(1)}, bf16[128,2048]{1,0:T(8,128)(2,1)S(1)}, u32[]{:S(2)}, u32[]{:S(2)}) collective-permute-start(bf16[128,2048]{1,0:T(8,128)(2,1)S(1)} %get-tuple-element.129), channel_id=1, source_target_pairs={{0,8},{1,9},{2,10},{3,11},{4,12},{5,13},{6,14},{7,15},{8,0},{9,1},... | collective-permute-start | bytes 1572872 | tf_op jit(solution)/shard_map/ppermute | solution.py:41
  118.4 2.8 norm.1
  121.2 31.2 %all_to_all.10 = bf16[16,8,4096]{2,1,0:T(8,128)(2,1)S(1)} all-to-all(bf16[16,8,4096]{2,1,0:T(8,128)(2,1)S(1)} %bitcast.41), channel_id=1, replica_groups=mesh['z'=4,'xh'=2,'c'=2,'y'=4,'xl'=2] {'z','xh','c'}, dimensions={0} | all-to-all | bytes 2097152 | tf_op jit(solution)/shard_map/all_to_all | solution.py:349
  155.1 3.1 %collective-permute-start.21 = (bf16[2,8,256,256]{3,2,1,0:T(8,128)(2,1)}, bf16[2,8,256,256]{3,2,1,0:T(8,128)(2,1)S(1)}, u32[]{:S(2)}, u32[]{:S(2)}) collective-permute-start(bf16[2,8,256,256]{3,2,1,0:T(8,128)(2,1)} %slice.59), channel_id=1, source_target_pairs={{0,96},{1,97},{2,98},{3,99},{4,100},{5,101},{6,102},{7,103},{8,25}... | collective-permute-start | bytes 6291464 | tf_op jit(solution)/shard_map/ppermute | solution.py:51
  160.0 6.4 %load_temporal.2 = (bf16[2,4096,256]{2,1,0:T(8,128)(2,1)S(1)}, bf16[2,4096,256]{2,1,0:T(8,128)(2,1)S(1)}, bf16[2,4096,256]{2,1,0:T(8,128)(2,1)S(1)}, bf16[16,2,256,256]{3,2,1,0:T(8,128)(2,1)S(1)}) custom-call(s32[5]{0:T(128)S(1)} %stack.56.coords, bf16[4,8,256,256]{3,2,1,0:T(8,128)(2,1)} %copy-done, bf16[4,8,256,256]{3,2,1,0:T(8,128)(2,1)} %copy-done.1, ...), custom_call_target="tpu_custom_call" | custom-call | flops 1048576 | bytes 65536 | tf_op jit(solution)/shard_map/load_temporal/pallas_call | solution.py:87
  166.3 17.0 %collective-permute-done.23.rest_0_ = bf16[128,4096]{1,0:T(8,128)(2,1)S(1)} collective-permute-done((bf16[128,4096]{1,0:T(8,128)(2,1)S(1)}, bf16[128,4096]{1,0:T(8,128)(2,1)S(1)}, u32[]{:S(2)}, u32[]{:S(2)}) %collective-permute-start.23) | collective-permute-done | bytes 1048608 | tf_op jit(solution)/shard_map/ppermute | solution.py:29
  187.7 3.9 %load_temporal.3 = (bf16[2,4096,256]{2,1,0:T(8,128)(2,1)S(1)}, bf16[2,4096,256]{2,1,0:T(8,128)(2,1)S(1)}, bf16[2,4096,256]{2,1,0:T(8,128)(2,1)S(1)}, bf16[16,2,256,256]{3,2,1,0:T(8,128)(2,1)S(1)}) custom-call(s32[5]{0:T(128)S(1)} %stack.56.coords, ...), custom_call_target="tpu_custom_call", output_to_operand_aliasing={{0}: (3, {}), {1}: (4, {}), {2}: (5, {}), {3}: (6, {})} | custom-call | flops 1048576 | bytes 65536 | tf_op jit(solution)/shard_map/load_temporal/pallas_call | solution.py:87
  191.6 6.2 %collective-permute-done.25.rest_2_ = bf16[64,4096]{1,0:T(8,128)(2,1)S(1)} collective-permute-done((bf16[64,4096]{1,0:T(8,128)(2,1)S(1)}, bf16[64,4096]{1,0:T(8,128)(2,1)S(1)}, u32[]{:S(2)}, u32[]{:S(2)}) %collective-permute-start.25) | collective-permute-done | bytes 524320 | tf_op jit(solution)/shard_map/ppermute | solution.py:29
  198.9 1.7 collective-permute-start.30
  202.9 20.6 %temporal.3 = (bf16[128,4096]{1,0:T(8,128)(2,1)S(1)}, bf16[128,4096]{1,0:T(8,128)(2,1)S(1)}, bf16[128,4096]{1,0:T(8,128)(2,1)S(1)}, bf16[384,4096]{1,0:T(8,128)(2,1)}) custom-call(bf16[128,4096]{1,0:T(8,128)(2,1)S(1)} %collective-permute-done.23.rest_0_, bf16[128,4096]{1,0:T(8,128)(2,1)S(1)} %collective-permute-done.24.rest_1_, ...), custom_call_target="tpu_custom_call" | custom-call | flops 1048576 | bytes 65536 | tf_op jit(solution)/shard_map/temporal/pallas_call | solution.py:220
  224.0 6.8 %collective-permute-done.32 = bf16[384,4096]{1,0:T(8,128)(2,1)S(1)} collective-permute-done((bf16[384,4096]{1,0:T(8,128)(2,1)}, bf16[384,4096]{1,0:T(8,128)(2,1)S(1)}, u32[]{:S(2)}, u32[]{:S(2)}) %collective-permute-start.32) | collective-permute-done | bytes 3145760 | tf_op jit(solution)/shard_map/ppermute | solution.py:41
  231.5 2.4 collective-permute-start.35
  233.9 8.8 %temporal.2 = (bf16[128,4096]{1,0:T(8,128)(2,1)S(1)}, bf16[128,4096]{1,0:T(8,128)(2,1)S(1)}) custom-call(bf16[128,4096]{1,0:T(8,128)(2,1)S(1)} %bitcast.40, bf16[128,4096]{1,0:T(8,128)(2,1)S(1)} %collective-permute-done.20.rest_1_, bf16[2,4096,256]{2,1,0:T(8,128)(2,1)S(1)} %get-tuple-element.113.rest_2_.rest_8_, ...), custom_call_target="tpu_custom_call" | custom-call | flops 1048576 | bytes 65536 | tf_op jit(solution)/shard_map/temporal/pallas_call | solution.py:220
  243.7 1.9 collective-permute-done.33
  246.7 2.7 collective-permute-start.36
  249.4 22.0 %collective-permute-done.34 = bf16[128,4096]{1,0:T(8,128)(2,1)S(1)} collective-permute-done((bf16[128,4096]{1,0:T(8,128)(2,1)S(1)}, bf16[128,4096]{1,0:T(8,128)(2,1)S(1)}, u32[]{:S(2)}, u32[]{:S(2)}) %collective-permute-start.34) | collective-permute-done | bytes 1048608 | tf_op jit(solution)/shard_map/ppermute | solution.py:33
  272.0 21.6 %all_to_all.11 = bf16[16,8,4096]{2,1,0:T(8,128)(2,1)S(1)} all-to-all(bf16[16,8,4096]{2,1,0:T(8,128)(2,1)S(1)} %fusion.3), channel_id=1, replica_groups=mesh['z'=4,'xh'=2,'c'=2,'y'=4,'xl'=2] {'z','xh','c'}, dimensions={0} | all-to-all | bytes 2097152 | tf_op jit(solution)/shard_map/all_to_all | solution.py:384
  (107 shorter events, 37.7 us)
Async XLA Ops:
  0.0 13.1 %collective-permute-start = (bf16[2,256,256]{2,1,0:T(8,128)(2,1)}, bf16[2,256,256]{2,1,0:T(8,128)(2,1)}, u32[]{:S(2)}, u32[]{:S(2)}) collective-permute-start(bf16[2,256,256]{2,1,0:T(8,128)(2,1)} %bitcast.43), channel_id=1, source_target_pairs={{0,17},{1,0},{2,19},{3,2},{4,21},{5,4},{6,23},{7,6},{8,104},{9,105... | collective-permute-start | bytes 786440 | tf_op jit(solution)/shard_map/ppermute | solution.py:45
  4.6 8.5 %collective-permute-start.1 = (bf16[2,256,256]{2,1,0:T(8,128)(2,1)}, bf16[2,256,256]{2,1,0:T(8,128)(2,1)}, u32[]{:S(2)}, u32[]{:S(2)}) collective-permute-start(bf16[2,256,256]{2,1,0:T(8,128)(2,1)} %bitcast.44), channel_id=1, source_target_pairs={{0,16},{1,17},{2,18},{3,19},{4,20},{5,21},{6,22},{7,23},{8,72},{9,... | collective-permute-start | bytes 786440 | tf_op jit(solution)/shard_map/ppermute | solution.py:45
  4.6 9.9 %collective-permute-start.2 = (bf16[2,256,256]{2,1,0:T(8,128)(2,1)}, bf16[2,256,256]{2,1,0:T(8,128)(2,1)}, u32[]{:S(2)}, u32[]{:S(2)}) collective-permute-start(bf16[2,256,256]{2,1,0:T(8,128)(2,1)} %bitcast.45), channel_id=1, source_target_pairs={{0,1},{1,16},{2,3},{3,18},{4,5},{5,20},{6,7},{7,22},{8,40},{9,41},... | collective-permute-start | bytes 786440 | tf_op jit(solution)/shard_map/ppermute | solution.py:45
  15.7 37.1 %collective-permute-start.5 = (bf16[4,2,256,256]{3,2,1,0:T(8,128)(2,1)S(1)}, bf16[4,2,256,256]{3,2,1,0:T(8,128)(2,1)}, u32[]{:S(2)}, u32[]{:S(2)}) collective-permute-start(bf16[4,2,256,256]{3,2,1,0:T(8,128)(2,1)S(1)} %pad_maximum_fusion.1.rest_0_), channel_id=1, source_target_pairs={{0,96},{1,97},{2,98},{3,99},{4,100},{5,101},{6,102},{7,103},{8,25}... | collective-permute-start | bytes 3145736 | tf_op jit(solution)/shard_map/ppermute | solution.py:51
  18.0 34.9 %collective-permute-start.6 = (bf16[4,2,256,256]{3,2,1,0:T(8,128)(2,1)S(1)}, bf16[4,2,256,256]{3,2,1,0:T(8,128)(2,1)}, u32[]{:S(2)}, u32[]{:S(2)}) collective-permute-start(bf16[4,2,256,256]{3,2,1,0:T(8,128)(2,1)S(1)} %pad_maximum_fusion.1.rest_0_), channel_id=1, source_target_pairs={{0,64},{1,65},{2,66},{3,67},{4,68},{5,69},{6,70},{7,71},{8,24},{9,... | collective-permute-start | bytes 3145736 | tf_op jit(solution)/shard_map/ppermute | solution.py:51
  18.5 34.4 %collective-permute-start.7 = (bf16[4,2,256,256]{3,2,1,0:T(8,128)(2,1)S(1)}, bf16[4,2,256,256]{3,2,1,0:T(8,128)(2,1)}, u32[]{:S(2)}, u32[]{:S(2)}) collective-permute-start(bf16[4,2,256,256]{3,2,1,0:T(8,128)(2,1)S(1)} %pad_maximum_fusion.1.rest_0_), channel_id=1, source_target_pairs={{0,32},{1,33},{2,34},{3,35},{4,36},{5,37},{6,38},{7,39},{8,9},{9,2... | collective-permute-start | bytes 3145736 | tf_op jit(solution)/shard_map/ppermute | solution.py:51
  21.9 30.9 %collective-permute-start.3 = (bf16[4,128,512]{2,1,0:T(8,128)(2,1)}, bf16[4,128,512]{2,1,0:T(8,128)(2,1)S(1)}, u32[]{:S(2)}, u32[]{:S(2)}) collective-permute-start(bf16[4,128,512]{2,1,0:T(8,128)(2,1)} %get-tuple-element.66), channel_id=1, source_target_pairs={{0,1},{1,0},{2,3},{3,2},{4,5},{5,4},{6,7},{7,6},{8,9},{9,8},{10,11... | collective-permute-start | bytes 1572872 | tf_op jit(solution)/shard_map/ppermute | solution.py:37
  25.2 27.7 %collective-permute-start.9 = (bf16[4,256,256]{2,1,0:T(8,128)(2,1)S(1)}, bf16[4,256,256]{2,1,0:T(8,128)(2,1)S(1)}, u32[]{:S(2)}, u32[]{:S(2)}) collective-permute-start(bf16[4,256,256]{2,1,0:T(8,128)(2,1)S(1)} %get-tuple-element.138), channel_id=1, source_target_pairs={{0,8},{1,9},{2,10},{3,11},{4,12},{5,13},{6,14},{7,15},{8,0},{9,1},... | collective-permute-start | bytes 1572872 | tf_op jit(solution)/shard_map/ppermute | solution.py:41
  52.9 8.5 %collective-permute-start.8 = (bf16[4,128,512]{2,1,0:T(8,128)(2,1)S(1)}, bf16[4,128,512]{2,1,0:T(8,128)(2,1)S(1)}, u32[]{:S(2)}, u32[]{:S(2)}) collective-permute-start(bf16[4,128,512]{2,1,0:T(8,128)(2,1)S(1)} %collective-permute-done.3.rest_1_), channel_id=1, source_target_pairs={{0,8},{1,9},{2,10},{3,11},{4,12},{5,13},{6,14},{7,15},{8,0},{9,1},... | collective-permute-start | bytes 1572872 | tf_op jit(solution)/shard_map/ppermute | solution.py:41
  54.0 16.6 %collective-permute-start.10 = (bf16[8,256,256]{2,1,0:T(8,128)(2,1)}, bf16[8,256,256]{2,1,0:T(8,128)(2,1)}, u32[]{:S(2)}, u32[]{:S(2)}) collective-permute-start(bf16[8,256,256]{2,1,0:T(8,128)(2,1)} %pad_maximum_fusion.3), channel_id=1, source_target_pairs={{0,17},{1,0},{2,19},{3,2},{4,21},{5,4},{6,23},{7,6},{8,104},{9,105... | collective-permute-start | bytes 3145736 | tf_op jit(solution)/shard_map/ppermute | solution.py:45
  55.0 15.8 %collective-permute-start.11 = (bf16[8,256,256]{2,1,0:T(8,128)(2,1)}, bf16[8,256,256]{2,1,0:T(8,128)(2,1)}, u32[]{:S(2)}, u32[]{:S(2)}) collective-permute-start(bf16[8,256,256]{2,1,0:T(8,128)(2,1)} %pad_maximum_fusion.3), channel_id=1, source_target_pairs={{0,16},{1,17},{2,18},{3,19},{4,20},{5,21},{6,22},{7,23},{8,72},{9,... | collective-permute-start | bytes 3145736 | tf_op jit(solution)/shard_map/ppermute | solution.py:45
  56.8 25.2 %collective-permute-start.12 = (bf16[8,256,256]{2,1,0:T(8,128)(2,1)}, bf16[8,256,256]{2,1,0:T(8,128)(2,1)}, u32[]{:S(2)}, u32[]{:S(2)}) collective-permute-start(bf16[8,256,256]{2,1,0:T(8,128)(2,1)} %pad_maximum_fusion.3), channel_id=1, source_target_pairs={{0,1},{1,16},{2,3},{3,18},{4,5},{5,20},{6,7},{7,22},{8,40},{9,41},... | collective-permute-start | bytes 3145736 | tf_op jit(solution)/shard_map/ppermute | solution.py:45
  67.8 14.2 %collective-permute-start.14 = (bf16[128,2048]{1,0:T(8,128)(2,1)S(1)}, bf16[128,2048]{1,0:T(8,128)(2,1)S(1)}, u32[]{:S(2)}, u32[]{:S(2)}) collective-permute-start(bf16[128,2048]{1,0:T(8,128)(2,1)S(1)} %get-tuple-element.135), channel_id=1, source_target_pairs={{0,6},{1,7},{2,0},{3,1},{4,2},{5,3},{6,4},{7,5},{8,14},{9,15},{10,... | collective-permute-start | bytes 1572872 | tf_op jit(solution)/shard_map/ppermute | solution.py:33
  70.6 12.5 %collective-permute-start.13 = (bf16[128,2048]{1,0:T(8,128)(2,1)S(1)}, bf16[128,2048]{1,0:T(8,128)(2,1)S(1)}, u32[]{:S(2)}, u32[]{:S(2)}) collective-permute-start(bf16[128,2048]{1,0:T(8,128)(2,1)S(1)} %get-tuple-element.136), channel_id=1, source_target_pairs={{0,2},{1,3},{2,4},{3,5},{4,6},{5,7},{6,0},{7,1},{8,10},{9,11},{10,... | collective-permute-start | bytes 1572872 | tf_op jit(solution)/shard_map/ppermute | solution.py:33
  86.0 66.5 %collective-permute-start.18 = (bf16[4,8,256,256]{3,2,1,0:T(8,128)(2,1)S(1)}, bf16[4,8,256,256]{3,2,1,0:T(8,128)(2,1)S(1)}, u32[]{:S(2)}, u32[]{:S(2)}) collective-permute-start(bf16[4,8,256,256]{3,2,1,0:T(8,128)(2,1)S(1)} %pad_maximum_fusion.rest_0_), channel_id=1, source_target_pairs={{0,96},{1,97},{2,98},{3,99},{4,100},{5,101},{6,102},{7,103},{8,25}... | collective-permute-start | bytes 12582920 | tf_op jit(solution)/shard_map/ppermute | solution.py:51
  89.3 63.1 %collective-permute-start.19 = (bf16[4,8,256,256]{3,2,1,0:T(8,128)(2,1)S(1)}, bf16[4,8,256,256]{3,2,1,0:T(8,128)(2,1)S(1)}, u32[]{:S(2)}, u32[]{:S(2)}) collective-permute-start(bf16[4,8,256,256]{3,2,1,0:T(8,128)(2,1)S(1)} %pad_maximum_fusion.rest_0_), channel_id=1, source_target_pairs={{0,32},{1,33},{2,34},{3,35},{4,36},{5,37},{6,38},{7,39},{8,9},{9,2... | collective-permute-start | bytes 12582920 | tf_op jit(solution)/shard_map/ppermute | solution.py:51
  89.3 23.0 %collective-permute-start.15 = (bf16[256,2048]{1,0:T(8,128)(2,1)S(1)}, bf16[256,2048]{1,0:T(8,128)(2,1)S(1)}, u32[]{:S(2)}, u32[]{:S(2)}) collective-permute-start(bf16[256,2048]{1,0:T(8,128)(2,1)S(1)} %get-tuple-element.88), channel_id=1, source_target_pairs={{0,2},{1,3},{2,4},{3,5},{4,6},{5,7},{6,0},{7,1},{8,10},{9,11},{10,... | collective-permute-start | bytes 3145736 | tf_op jit(solution)/shard_map/ppermute | solution.py:33
  89.3 23.0 %collective-permute-start.16 = (bf16[256,2048]{1,0:T(8,128)(2,1)S(1)}, bf16[256,2048]{1,0:T(8,128)(2,1)S(1)}, u32[]{:S(2)}, u32[]{:S(2)}) collective-permute-start(bf16[256,2048]{1,0:T(8,128)(2,1)S(1)} %get-tuple-element.89), channel_id=1, source_target_pairs={{0,6},{1,7},{2,0},{3,1},{4,2},{5,3},{6,4},{7,5},{8,14},{9,15},{10,... | collective-permute-start | bytes 3145736 | tf_op jit(solution)/shard_map/ppermute | solution.py:33
  155.1 29.5 %collective-permute-start.21 = (bf16[2,8,256,256]{3,2,1,0:T(8,128)(2,1)}, bf16[2,8,256,256]{3,2,1,0:T(8,128)(2,1)S(1)}, u32[]{:S(2)}, u32[]{:S(2)}) collective-permute-start(bf16[2,8,256,256]{3,2,1,0:T(8,128)(2,1)} %slice.59), channel_id=1, source_target_pairs={{0,96},{1,97},{2,98},{3,99},{4,100},{5,101},{6,102},{7,103},{8,25}... | collective-permute-start | bytes 6291464 | tf_op jit(solution)/shard_map/ppermute | solution.py:51
  158.4 26.5 %collective-permute-start.22 = (bf16[2,8,256,256]{3,2,1,0:T(8,128)(2,1)S(1)}, bf16[2,8,256,256]{3,2,1,0:T(8,128)(2,1)S(1)}, u32[]{:S(2)}, u32[]{:S(2)}) collective-permute-start(bf16[2,8,256,256]{3,2,1,0:T(8,128)(2,1)S(1)} %slice.60), channel_id=1, source_target_pairs={{0,32},{1,33},{2,34},{3,35},{4,36},{5,37},{6,38},{7,39},{8,9},{9,2... | collective-permute-start | bytes 6291464 | tf_op jit(solution)/shard_map/ppermute | solution.py:51
  158.4 24.9 %collective-permute-start.23 = (bf16[128,4096]{1,0:T(8,128)(2,1)S(1)}, bf16[128,4096]{1,0:T(8,128)(2,1)S(1)}, u32[]{:S(2)}, u32[]{:S(2)}) collective-permute-start(bf16[128,4096]{1,0:T(8,128)(2,1)S(1)} %bitcast.37), channel_id=1, source_target_pairs={{0,6},{1,7},{2,0},{3,1},{4,2},{5,3},{6,4},{7,5},{8,14},{9,15},{10,... | collective-permute-start | bytes 3145736 | tf_op jit(solution)/shard_map/ppermute | solution.py:29
  158.5 26.1 %collective-permute-start.24 = (bf16[128,4096]{1,0:T(8,128)(2,1)S(1)}, bf16[128,4096]{1,0:T(8,128)(2,1)S(1)}, u32[]{:S(2)}, u32[]{:S(2)}) collective-permute-start(bf16[128,4096]{1,0:T(8,128)(2,1)S(1)} %bitcast.38), channel_id=1, source_target_pairs={{0,2},{1,3},{2,4},{3,5},{4,6},{5,7},{6,0},{7,1},{8,10},{9,11},{10,... | collective-permute-start | bytes 3145736 | tf_op jit(solution)/shard_map/ppermute | solution.py:29
  184.9 13.0 %collective-permute-start.25 = (bf16[64,4096]{1,0:T(8,128)(2,1)S(1)}, bf16[64,4096]{1,0:T(8,128)(2,1)S(1)}, u32[]{:S(2)}, u32[]{:S(2)}) collective-permute-start(bf16[64,4096]{1,0:T(8,128)(2,1)S(1)} %slice.61), channel_id=1, source_target_pairs={{0,6},{1,7},{2,0},{3,1},{4,2},{5,3},{6,4},{7,5},{8,14},{9,15},{10,... | collective-permute-start | bytes 1572872 | tf_op jit(solution)/shard_map/ppermute | solution.py:29
  185.0 14.0 %collective-permute-start.26 = (bf16[64,4096]{1,0:T(8,128)(2,1)S(1)}, bf16[64,4096]{1,0:T(8,128)(2,1)S(1)}, u32[]{:S(2)}, u32[]{:S(2)}) collective-permute-start(bf16[64,4096]{1,0:T(8,128)(2,1)S(1)} %slice.62), channel_id=1, source_target_pairs={{0,2},{1,3},{2,4},{3,5},{4,6},{5,7},{6,0},{7,1},{8,10},{9,11},{10,... | collective-permute-start | bytes 1572872 | tf_op jit(solution)/shard_map/ppermute | solution.py:29
  186.5 14.1 %collective-permute-start.28 = (bf16[128,4096]{1,0:T(8,128)(2,1)S(1)}, bf16[128,4096]{1,0:T(8,128)(2,1)S(1)}, u32[]{:S(2)}, u32[]{:S(2)}) collective-permute-start(bf16[128,4096]{1,0:T(8,128)(2,1)S(1)} %collective-permute-done.23.rest_0_), channel_id=1, source_target_pairs={{0,8},{1,9},{2,10},{3,11},{4,12},{5,13},{6,14},{7,15},{8,0},{9,1},... | collective-permute-start | bytes 3145736 | tf_op jit(solution)/shard_map/ppermute | solution.py:41
  187.6 13.0 %collective-permute-start.29 = (bf16[128,4096]{1,0:T(8,128)(2,1)S(1)}, bf16[128,4096]{1,0:T(8,128)(2,1)S(1)}, u32[]{:S(2)}, u32[]{:S(2)}) collective-permute-start(bf16[128,4096]{1,0:T(8,128)(2,1)S(1)} %collective-permute-done.24.rest_1_), channel_id=1, source_target_pairs={{0,8},{1,9},{2,10},{3,11},{4,12},{5,13},{6,14},{7,15},{8,0},{9,1},... | collective-permute-start | bytes 3145736 | tf_op jit(solution)/shard_map/ppermute | solution.py:41
  223.5 7.3 %collective-permute-start.32 = (bf16[384,4096]{1,0:T(8,128)(2,1)}, bf16[384,4096]{1,0:T(8,128)(2,1)S(1)}, u32[]{:S(2)}, u32[]{:S(2)}) collective-permute-start(bf16[384,4096]{1,0:T(8,128)(2,1)} %get-tuple-element.122), channel_id=1, source_target_pairs={{0,8},{1,9},{2,10},{3,11},{4,12},{5,13},{6,14},{7,15},{8,0},{9,1},... | collective-permute-start | bytes 9437192 | tf_op jit(solution)/shard_map/ppermute | solution.py:41
  223.8 10.1 %collective-permute-start.20 = (bf16[128,4096]{1,0:T(8,128)(2,1)S(1)}, bf16[128,4096]{1,0:T(8,128)(2,1)S(1)}, u32[]{:S(2)}, u32[]{:S(2)}) collective-permute-start(bf16[128,4096]{1,0:T(8,128)(2,1)S(1)} %bitcast.39), channel_id=1, source_target_pairs={{0,8},{1,9},{2,10},{3,11},{4,12},{5,13},{6,14},{7,15},{8,0},{9,1},... | collective-permute-start | bytes 3145736 | tf_op jit(solution)/shard_map/ppermute | solution.py:41
  231.2 14.4 %collective-permute-start.33 = (bf16[64,4096]{1,0:T(8,128)(2,1)S(1)}, bf16[64,4096]{1,0:T(8,128)(2,1)S(1)}, u32[]{:S(2)}, u32[]{:S(2)}) collective-permute-start(bf16[64,4096]{1,0:T(8,128)(2,1)S(1)} %get-tuple-element.127), channel_id=1, source_target_pairs={{0,2},{1,3},{2,4},{3,5},{4,6},{5,7},{6,0},{7,1},{8,10},{9,11},{10,... | collective-permute-start | bytes 1572872 | tf_op jit(solution)/shard_map/ppermute | solution.py:33
  231.5 14.1 %collective-permute-start.35 = (bf16[64,4096]{1,0:T(8,128)(2,1)S(1)}, bf16[64,4096]{1,0:T(8,128)(2,1)S(1)}, u32[]{:S(2)}, u32[]{:S(2)}) collective-permute-start(bf16[64,4096]{1,0:T(8,128)(2,1)S(1)} %get-tuple-element.128), channel_id=1, source_target_pairs={{0,6},{1,7},{2,0},{3,1},{4,2},{5,3},{6,4},{7,5},{8,14},{9,15},{10,... | collective-permute-start | bytes 1572872 | tf_op jit(solution)/shard_map/ppermute | solution.py:33
  246.6 24.7 %collective-permute-start.34 = (bf16[128,4096]{1,0:T(8,128)(2,1)S(1)}, bf16[128,4096]{1,0:T(8,128)(2,1)S(1)}, u32[]{:S(2)}, u32[]{:S(2)}) collective-permute-start(bf16[128,4096]{1,0:T(8,128)(2,1)S(1)} %get-tuple-element.125), channel_id=1, source_target_pairs={{0,2},{1,3},{2,4},{3,5},{4,6},{5,7},{6,0},{7,1},{8,10},{9,11},{10,... | collective-permute-start | bytes 3145736 | tf_op jit(solution)/shard_map/ppermute | solution.py:33
  246.7 24.7 %collective-permute-start.36 = (bf16[128,4096]{1,0:T(8,128)(2,1)S(1)}, bf16[128,4096]{1,0:T(8,128)(2,1)S(1)}, u32[]{:S(2)}, u32[]{:S(2)}) collective-permute-start(bf16[128,4096]{1,0:T(8,128)(2,1)S(1)} %get-tuple-element.126), channel_id=1, source_target_pairs={{0,6},{1,7},{2,0},{3,1},{4,2},{5,3},{6,4},{7,5},{8,14},{9,15},{10,... | collective-permute-start | bytes 3145736 | tf_op jit(solution)/shard_map/ppermute | solution.py:33
  (15 other events, 104.8 us)

commit v3 on v2

--- a/solution.py
+++ b/solution.py
@@ -320,7 +320,9 @@
     out_own = [out_first] + [from_second(out_first, d) for d in range(1, RING)]
     other = swap_xl(other)
     sources = [own, other, swap_core(own)]
-    *sources, o_1, o_2, o_3 = lax.optimization_barrier((*sources, *out_own[1:]))
+    *sources, o_1, o_2, o_3, residual_rows = lax.optimization_barrier(
+        (*sources, *out_own[1:], residual.reshape(128, 4096))
+    )
     out_own[1:] = o_1, o_2, o_3
     sources.append(swap_core(sources[1]))
     tiles = jnp.stack(
@@ -332,7 +334,6 @@
     )
     shard = after(jnp.concatenate([mine, swap_core(theirs)]), *out_own[1:])
     shards_first = [shard] + [from_first(shard, d) for d in range(1, RING)]
-    *sources, residual_rows = lax.optimization_barrier((*sources, residual.reshape(128, 4096)))
     parts = spatial_out_call(coords, sources, load_out(coords, out_own))
 
     far = [to_y(parts[2][:128], 1), to_y(parts[2][128:], -1)]
@@ -360,26 +361,27 @@
     weights = load_temporal(coords, last, [(2, 0, 2), (2, 2, 2)], weights)
 
     far = [from_y(next_p[:64], 1), from_y(next_m[64:], -1)]
-    *far, w_0, w_1, w_2, w_3 = lax.optimization_barrier((*far, *weights))
-    weights = [w_0, w_1, w_2, w_3]
-
-    def both_cores(blocks):
-        *parts, others = temporal_call(blocks + [swap_core(block) for block in blocks], weights)
-        others = swap_core(others)
-        return [
-            part.astype(jnp.float32) + others[128 * n : 128 * (n + 1)].astype(jnp.float32)
-            for n, part in enumerate(parts)
-        ]
-
-    part_p, part_m, part_far = both_cores([next_p, next_m] + far)
-    part_far = part_far.astype(jnp.bfloat16)
-    far = [to_y(part_far[:64], 1), to_y(part_far[64:], -1)]
+    near = [next_p, next_m, swap_core(next_p), swap_core(next_m)]
+    *near, own_swapped = lax.optimization_barrier((*near, swap_core(normed)))
+
+    part_p, part_m, others = temporal_call(near, weights)
+    *far, part_p, part_m, others = lax.optimization_barrier((*far, part_p, part_m, others))
+    others = swap_core(others)
+    part, far_others = temporal_call(far + [swap_core(half) for half in far], weights)
+    far_others, others = lax.optimization_barrier((far_others, others))
+    part = (part.astype(jnp.float32) + swap_core(far_others).astype(jnp.float32)).astype(jnp.bfloat16)
+    far = [to_y(part[:64], 1), to_y(part[64:], -1)]
+    own, own_others = temporal_call([normed, own_swapped], weights)
+    *far, own, own_others = lax.optimization_barrier((*far, own, own_others))
+    total = own.astype(jnp.float32) + swap_core(own_others).astype(jnp.float32)
     zeros = jnp.zeros((64, 4096), jnp.bfloat16)
-    part_p += jnp.concatenate([far[0], zeros]).astype(jnp.float32)
-    part_m += jnp.concatenate([zeros, far[1]]).astype(jnp.float32)
-    (total,) = both_cores([normed])
-    for part, d in ((part_p, 1), (part_m, -1)):
-        total = total + to_y(part.astype(jnp.bfloat16), d).astype(jnp.float32)
+    for d, part, other, passed in (
+        (1, part_p, others[:128], [far[0], zeros]),
+        (-1, part_m, others[128:], [zeros, far[1]]),
+    ):
+        part = part.astype(jnp.float32) + other.astype(jnp.float32)
+        part = (part + jnp.concatenate(passed).astype(jnp.float32)).astype(jnp.bfloat16)
+        total = total + to_y(part, d).astype(jnp.float32)
     summed = total.astype(jnp.bfloat16).reshape(16, 8, 4096)
     summed = lax.all_to_all(summed, ("z", "xh", "c"), split_axis=0, concat_axis=0, tiled=True)
     finished = middle.astype(jnp.float32) + summed.reshape(128, 4096).astype(jnp.float32)

time: 296 us -> 288 us (0.973)
  waiting for transfers between devices: 122 us -> 113 us
    ppermute x4, waiting for transfers between devices: 25.6 us -> 17.1 us  [from_y(): lax.ppermute(array, AXES, permutation(lambda z, x, c, y: (z, x, c, y - d)))]
    ppermute x11 -> x12, waiting for transfers between devices: 10.7 us -> 8.62 us  [swap_core(): lax.ppermute(array, AXES, permutation(lambda z, x, c, y: (z, x, 1 - c, y)))]
    pallas_call x2 -> x3, Pallas kernels: 29.4 us -> 31.3 us  [temporal_call(): pl.pallas_call(kernel, out_shape=[jax.ShapeDtypeStruct(shape, jnp.bfloat1...]
    ppermute x11 -> x12, starting transfers between devices: 11.5 us -> 13.1 us  [swap_core(): lax.ppermute(array, AXES, permutation(lambda z, x, c, y: (z, x, 1 - c, y)))]
  transfers between devices with their start and end apart: 37 -> 38, of which waited for: 17 -> 14; matrix products, arithmetic and copies ran while one was open for 5% -> 5% of each run, Pallas kernels for 11% -> 19%
where the time goes in v3:
time: 288 us
  waiting for transfers between devices  113 us (39%)
  Pallas kernels  53.8 us (19%)
  blocking collectives  51.9 us (18%)
  starting transfers between devices  44.3 us (15%)
  local copies, waits for them, and re-layouts  11.8 us (4%)
  other arithmetic  11.1 us (4%)
    ppermute x8, waiting for transfers between devices, to_y(): lax.ppermute(array, AXES, permutation(lambda z, x, c, y: (z, x, c, y + d)))  43.5 us
    pallas_call x3, Pallas kernels, temporal_call(): pl.pallas_call(kernel, out_shape=[jax.ShapeDtypeStruct(shape, jnp.bfloat1...  31.3 us
    all_to_all x1, blocking collectives, shards(): lax.all_to_all(normed.reshape(16, 8, 4096), ('z', 'xh', 'c'), split_axis=...  30.4 us
    ppermute x1, waiting for transfers between devices, swap_xl(): lax.ppermute(array, AXES, permutation(lambda z, x, c, y: (z, x ^ 1, c, y)))  27.1 us
    all_to_all x1, blocking collectives, shards(): lax.all_to_all(summed, ('z', 'xh', 'c'), split_axis=0, concat_axis=0, til...  21.6 us
    ppermute x4, waiting for transfers between devices, from_y(): lax.ppermute(array, AXES, permutation(lambda z, x, c, y: (z, x, c, y - d)))  17.1 us
    ppermute x6, waiting for transfers between devices, from_first(): lax.ppermute(array, AXES, permutation(lambda z, x, c, y: (z - d * c, x -...  15.6 us
    pallas_call x3, Pallas kernels, load(): pl.pallas_call(kernel, out_shape=[pltpu.VMEM(shape, jnp.bfloat16) for sha...  13.3 us
  transfers between devices with their start and end apart: 38, of which 14 were waited for; matrix products, arithmetic and copies ran while one was open for 5% of the time, Pallas kernels for 19%

profile of v3, /device:TPU:1, one launch (start us, length us, event | category | flops | bytes accessed | tf_op | source)
XLA Modules:
  0.0 287.9 jit_solution(8250093039372815256)
XLA Ops:
  0.0 4.6 %collective-permute-start = (bf16[2,256,256]{2,1,0:T(8,128)(2,1)}, bf16[2,256,256]{2,1,0:T(8,128)(2,1)}, u32[]{:S(2)}, u32[]{:S(2)}) collective-permute-start(bf16[2,256,256]{2,1,0:T(8,128)(2,1)} %bitcast.43), channel_id=1, source_target_pairs={{0,17},{1,0},{2,19},{3,2},{4,21},{5,4},{6,23},{7,6},{8,104},{9,105... | collective-permute-start | bytes 786440 | tf_op jit(solution)/shard_map/ppermute | solution.py:45
  12.4 2.1 collective-permute-done.2
  14.5 2.3 pad_maximum_fusion.1.rest_0_
  16.7 2.2 collective-permute-start.5
  20.0 2.8 collective-permute-start.4
  26.8 27.1 %collective-permute-done.3.rest_1_ = bf16[4,128,512]{2,1,0:T(8,128)(2,1)S(1)} collective-permute-done((bf16[4,128,512]{2,1,0:T(8,128)(2,1)S(1)}, bf16[4,128,512]{2,1,0:T(8,128)(2,1)S(1)}, u32[]{:S(2)}, u32[]{:S(2)}) %collective-permute-start.3) | collective-permute-done | bytes 524320 | tf_op jit(solution)/shard_map/ppermute | solution.py:37
  54.0 2.3 pad_maximum_fusion.3
  58.4 3.0 %load_out.1.rest_4_ = bf16[8,4,256,256]{3,2,1,0:T(8,128)(2,1)S(1)} custom-call(s32[5]{0:T(128)S(1)} %stack.56.coords, bf16[4,2,256,256]{3,2,1,0:T(8,128)(2,1)} %pad_maximum_fusion.1.rest_0_, bf16[4,2,256,256]{3,2,1,0:T(8,128)(2,1)} %collective-permute-done.5.rest_1_, bf16[4,2,256,256]{3,2,1,0:T(8,128)(2,1)} %collective-permute-done.6.rest_2_, ...), custom_call_target="tpu_custom_call" | custom-call | flops 1048576 | bytes 65536 | tf_op jit(solution)/shard_map/load_out/pallas_call | solution.py:87
  61.4 6.4 %spatial_out.1 = (bf16[256,2048]{1,0:T(8,128)(2,1)S(1)}, bf16[256,2048]{1,0:T(8,128)(2,1)S(1)}, bf16[256,2048]{1,0:T(8,128)(2,1)S(1)}, bf16[256,2048]{1,0:T(8,128)(2,1)S(1)}) custom-call(s32[5]{0:T(128)S(1)} %stack.56.coords, bf16[4,128,512]{2,1,0:T(8,128)(2,1)S(1)} %get-tuple-element.76.rest_0_, bf16[4,128,512]{2,1,0:T(8,128)(2,1)S(1)} %collective-permute-done.3.rest_1_, ...), custom_call_target="tpu_custom_call" | custom-call | flops 1048576 | bytes 65536 | tf_op jit(solution)/shard_map/spatial_out/pallas_call | solution.py:158
  67.9 2.8 collective-permute-start.14
  70.7 2.3 collective-permute-done.11
  73.0 11.2 %collective-permute-done.12 = bf16[8,256,256]{2,1,0:T(8,128)(2,1)} collective-permute-done((bf16[8,256,256]{2,1,0:T(8,128)(2,1)}, bf16[8,256,256]{2,1,0:T(8,128)(2,1)}, u32[]{:S(2)}, u32[]{:S(2)}) %collective-permute-start.12) | collective-permute-done | bytes 1048608 | tf_op jit(solution)/shard_map/ppermute | solution.py:45
  84.5 2.4 pad_maximum_fusion.rest_0_
  87.0 3.3 %collective-permute-start.18 = (bf16[4,8,256,256]{3,2,1,0:T(8,128)(2,1)S(1)}, bf16[4,8,256,256]{3,2,1,0:T(8,128)(2,1)S(1)}, u32[]{:S(2)}, u32[]{:S(2)}) collective-permute-start(bf16[4,8,256,256]{3,2,1,0:T(8,128)(2,1)S(1)} %pad_maximum_fusion.rest_0_), channel_id=1, source_target_pairs={{0,96},{1,97},{2,98},{3,99},{4,100},{5,101},{6,102},{7,103},{8,25}... | collective-permute-start | bytes 12582920 | tf_op jit(solution)/shard_map/ppermute | solution.py:51
  93.0 20.3 %collective-permute-done.15 = bf16[256,2048]{1,0:T(8,128)(2,1)S(1)} collective-permute-done((bf16[256,2048]{1,0:T(8,128)(2,1)S(1)}, bf16[256,2048]{1,0:T(8,128)(2,1)S(1)}, u32[]{:S(2)}, u32[]{:S(2)}) %collective-permute-start.15) | collective-permute-done | bytes 1048608 | tf_op jit(solution)/shard_map/ppermute | solution.py:33
  114.0 3.8 %collective-permute-start.17 = (bf16[128,2048]{1,0:T(8,128)(2,1)S(1)}, bf16[128,2048]{1,0:T(8,128)(2,1)S(1)}, u32[]{:S(2)}, u32[]{:S(2)}) collective-permute-start(bf16[128,2048]{1,0:T(8,128)(2,1)S(1)} %get-tuple-element.143), channel_id=1, source_target_pairs={{0,8},{1,9},{2,10},{3,11},{4,12},{5,13},{6,14},{7,15},{8,0},{9,1},... | collective-permute-start | bytes 1572872 | tf_op jit(solution)/shard_map/ppermute | solution.py:41
  119.4 2.8 norm.1
  122.2 30.4 %all_to_all.10 = bf16[16,8,4096]{2,1,0:T(8,128)(2,1)S(1)} all-to-all(bf16[16,8,4096]{2,1,0:T(8,128)(2,1)S(1)} %bitcast.41), channel_id=1, replica_groups=mesh['z'=4,'xh'=2,'c'=2,'y'=4,'xl'=2] {'z','xh','c'}, dimensions={0} | all-to-all | bytes 2097152 | tf_op jit(solution)/shard_map/all_to_all | solution.py:350
  154.6 3.1 %collective-permute-start.20 = (bf16[2,8,256,256]{3,2,1,0:T(8,128)(2,1)S(1)}, bf16[2,8,256,256]{3,2,1,0:T(8,128)(2,1)S(1)}, u32[]{:S(2)}, u32[]{:S(2)}) collective-permute-start(bf16[2,8,256,256]{3,2,1,0:T(8,128)(2,1)S(1)} %slice.56), channel_id=1, source_target_pairs={{0,96},{1,97},{2,98},{3,99},{4,100},{5,101},{6,102},{7,103},{8,25}... | collective-permute-start | bytes 6291464 | tf_op jit(solution)/shard_map/ppermute | solution.py:51
  160.2 6.4 %load_temporal.2 = (bf16[2,4096,256]{2,1,0:T(8,128)(2,1)S(1)}, bf16[2,4096,256]{2,1,0:T(8,128)(2,1)S(1)}, bf16[2,4096,256]{2,1,0:T(8,128)(2,1)S(1)}, bf16[16,2,256,256]{3,2,1,0:T(8,128)(2,1)S(1)}) custom-call(s32[5]{0:T(128)S(1)} %stack.56.coords, bf16[4,8,256,256]{3,2,1,0:T(8,128)(2,1)} %copy-done, bf16[4,8,256,256]{3,2,1,0:T(8,128)(2,1)} %copy-done.1, ...), custom_call_target="tpu_custom_call" | custom-call | flops 1048576 | bytes 65536 | tf_op jit(solution)/shard_map/load_temporal/pallas_call | solution.py:87
  166.6 16.3 %collective-permute-done.22.rest_0_ = bf16[128,4096]{1,0:T(8,128)(2,1)S(1)} collective-permute-done((bf16[128,4096]{1,0:T(8,128)(2,1)S(1)}, bf16[128,4096]{1,0:T(8,128)(2,1)S(1)}, u32[]{:S(2)}, u32[]{:S(2)}) %collective-permute-start.22) | collective-permute-done | bytes 1048608 | tf_op jit(solution)/shard_map/ppermute | solution.py:29
  187.6 3.9 %load_temporal.3 = (bf16[2,4096,256]{2,1,0:T(8,128)(2,1)S(1)}, bf16[2,4096,256]{2,1,0:T(8,128)(2,1)S(1)}, bf16[2,4096,256]{2,1,0:T(8,128)(2,1)S(1)}, bf16[16,2,256,256]{3,2,1,0:T(8,128)(2,1)S(1)}) custom-call(s32[5]{0:T(128)S(1)} %stack.56.coords, ...), custom_call_target="tpu_custom_call", output_to_operand_aliasing={{0}: (3, {}), {1}: (4, {}), {2}: (5, {}), {3}: (6, {})} | custom-call | flops 1048576 | bytes 65536 | tf_op jit(solution)/shard_map/load_temporal/pallas_call | solution.py:87
  191.6 13.8 %temporal.3 = (bf16[128,4096]{1,0:T(8,128)(2,1)S(1)}, bf16[128,4096]{1,0:T(8,128)(2,1)S(1)}, bf16[256,4096]{1,0:T(8,128)(2,1)S(1)}) custom-call(bf16[128,4096]{1,0:T(8,128)(2,1)S(1)} %collective-permute-done.22.rest_0_, bf16[128,4096]{1,0:T(8,128)(2,1)S(1)} %collective-permute-done.23.rest_1_, bf16[128,4096]{1,0:T(8,128)(2,1)S(1)} %collective-permute-done.26.rest_2_, ...), custom_call_target="tpu_custom_call" | custom-call | flops 1048576 | bytes 65536 | tf_op jit(solution)/shard_map/temporal/pallas_call | solution.py:220
  207.1 4.0 %collective-permute-done.29.rest_2_ = bf16[64,4096]{1,0:T(8,128)(2,1)S(1)} collective-permute-done((bf16[64,4096]{1,0:T(8,128)(2,1)S(1)}, bf16[64,4096]{1,0:T(8,128)(2,1)S(1)}, u32[]{:S(2)}, u32[]{:S(2)}) %collective-permute-start.29) | collective-permute-done | bytes 524320 | tf_op jit(solution)/shard_map/ppermute | solution.py:41
  211.9 8.8 %temporal.4 = (bf16[128,4096]{1,0:T(8,128)(2,1)S(1)}, bf16[128,4096]{1,0:T(8,128)(2,1)S(1)}) custom-call(bf16[64,4096]{1,0:T(8,128)(2,1)S(1)} %collective-permute-done.24.rest_0_, bf16[64,4096]{1,0:T(8,128)(2,1)S(1)} %collective-permute-done.25.rest_1_, bf16[64,4096]{1,0:T(8,128)(2,1)S(1)} %collective-permute-done.29.rest_2_, ...), custom_call_target="tpu_custom_call" | custom-call | flops 1048576 | bytes 65536 | tf_op jit(solution)/shard_map/temporal/pallas_call | solution.py:220
  221.1 2.3 collective-permute-done.32
  223.8 2.7 collective-permute-start.34
  226.5 8.8 %temporal.5 = (bf16[128,4096]{1,0:T(8,128)(2,1)S(1)}, bf16[128,4096]{1,0:T(8,128)(2,1)S(1)}) custom-call(bf16[128,4096]{1,0:T(8,128)(2,1)S(1)} %bitcast.40, bf16[128,4096]{1,0:T(8,128)(2,1)S(1)} %collective-permute-done.28.rest_1_, bf16[2,4096,256]{2,1,0:T(8,128)(2,1)S(1)} %get-tuple-element.116.rest_4_.rest_2_, ...), custom_call_target="tpu_custom_call" | custom-call | flops 1048576 | bytes 65536 | tf_op jit(solution)/shard_map/temporal/pallas_call | solution.py:220
  235.3 2.9 %collective-permute-done.33 = bf16[64,4096]{1,0:T(8,128)(2,1)S(1)} collective-permute-done((bf16[64,4096]{1,0:T(8,128)(2,1)S(1)}, bf16[64,4096]{1,0:T(8,128)(2,1)S(1)}, u32[]{:S(2)}, u32[]{:S(2)}) %collective-permute-start.33) | collective-permute-done | bytes 524320 | tf_op jit(solution)/shard_map/ppermute | solution.py:33
  239.3 2.7 collective-permute-start.37
  243.7 20.2 %collective-permute-done.36 = bf16[128,4096]{1,0:T(8,128)(2,1)S(1)} collective-permute-done((bf16[128,4096]{1,0:T(8,128)(2,1)S(1)}, bf16[128,4096]{1,0:T(8,128)(2,1)S(1)}, u32[]{:S(2)}, u32[]{:S(2)}) %collective-permute-start.36) | collective-permute-done | bytes 1048608 | tf_op jit(solution)/shard_map/ppermute | solution.py:33
  264.6 21.6 %all_to_all.11 = bf16[16,8,4096]{2,1,0:T(8,128)(2,1)S(1)} all-to-all(bf16[16,8,4096]{2,1,0:T(8,128)(2,1)S(1)} %fusion.3), channel_id=1, replica_groups=mesh['z'=4,'xh'=2,'c'=2,'y'=4,'xl'=2] {'z','xh','c'}, dimensions={0} | all-to-all | bytes 2097152 | tf_op jit(solution)/shard_map/all_to_all | solution.py:386
  (110 shorter events, 38.0 us)
Async XLA Ops:
  0.0 12.3 %collective-permute-start = (bf16[2,256,256]{2,1,0:T(8,128)(2,1)}, bf16[2,256,256]{2,1,0:T(8,128)(2,1)}, u32[]{:S(2)}, u32[]{:S(2)}) collective-permute-start(bf16[2,256,256]{2,1,0:T(8,128)(2,1)} %bitcast.43), channel_id=1, source_target_pairs={{0,17},{1,0},{2,19},{3,2},{4,21},{5,4},{6,23},{7,6},{8,104},{9,105... | collective-permute-start | bytes 786440 | tf_op jit(solution)/shard_map/ppermute | solution.py:45
  4.6 7.8 %collective-permute-start.1 = (bf16[2,256,256]{2,1,0:T(8,128)(2,1)}, bf16[2,256,256]{2,1,0:T(8,128)(2,1)}, u32[]{:S(2)}, u32[]{:S(2)}) collective-permute-start(bf16[2,256,256]{2,1,0:T(8,128)(2,1)} %bitcast.44), channel_id=1, source_target_pairs={{0,16},{1,17},{2,18},{3,19},{4,20},{5,21},{6,22},{7,23},{8,72},{9,... | collective-permute-start | bytes 786440 | tf_op jit(solution)/shard_map/ppermute | solution.py:45
  4.6 9.9 %collective-permute-start.2 = (bf16[2,256,256]{2,1,0:T(8,128)(2,1)}, bf16[2,256,256]{2,1,0:T(8,128)(2,1)}, u32[]{:S(2)}, u32[]{:S(2)}) collective-permute-start(bf16[2,256,256]{2,1,0:T(8,128)(2,1)} %bitcast.45), channel_id=1, source_target_pairs={{0,1},{1,16},{2,3},{3,18},{4,5},{5,20},{6,7},{7,22},{8,40},{9,41},... | collective-permute-start | bytes 786440 | tf_op jit(solution)/shard_map/ppermute | solution.py:45
  16.7 37.2 %collective-permute-start.5 = (bf16[4,2,256,256]{3,2,1,0:T(8,128)(2,1)}, bf16[4,2,256,256]{3,2,1,0:T(8,128)(2,1)}, u32[]{:S(2)}, u32[]{:S(2)}) collective-permute-start(bf16[4,2,256,256]{3,2,1,0:T(8,128)(2,1)} %pad_maximum_fusion.1.rest_0_), channel_id=1, source_target_pairs={{0,96},{1,97},{2,98},{3,99},{4,100},{5,101},{6,102},{7,103},{8,25}... | collective-permute-start | bytes 3145736 | tf_op jit(solution)/shard_map/ppermute | solution.py:51
  18.9 35.0 %collective-permute-start.6 = (bf16[4,2,256,256]{3,2,1,0:T(8,128)(2,1)}, bf16[4,2,256,256]{3,2,1,0:T(8,128)(2,1)}, u32[]{:S(2)}, u32[]{:S(2)}) collective-permute-start(bf16[4,2,256,256]{3,2,1,0:T(8,128)(2,1)} %pad_maximum_fusion.1.rest_0_), channel_id=1, source_target_pairs={{0,64},{1,65},{2,66},{3,67},{4,68},{5,69},{6,70},{7,71},{8,24},{9,... | collective-permute-start | bytes 3145736 | tf_op jit(solution)/shard_map/ppermute | solution.py:51
  19.4 34.5 %collective-permute-start.7 = (bf16[4,2,256,256]{3,2,1,0:T(8,128)(2,1)}, bf16[4,2,256,256]{3,2,1,0:T(8,128)(2,1)}, u32[]{:S(2)}, u32[]{:S(2)}) collective-permute-start(bf16[4,2,256,256]{3,2,1,0:T(8,128)(2,1)} %pad_maximum_fusion.1.rest_0_), channel_id=1, source_target_pairs={{0,32},{1,33},{2,34},{3,35},{4,36},{5,37},{6,38},{7,39},{8,9},{9,2... | collective-permute-start | bytes 3145736 | tf_op jit(solution)/shard_map/ppermute | solution.py:51
  22.8 31.1 %collective-permute-start.3 = (bf16[4,128,512]{2,1,0:T(8,128)(2,1)S(1)}, bf16[4,128,512]{2,1,0:T(8,128)(2,1)S(1)}, u32[]{:S(2)}, u32[]{:S(2)}) collective-permute-start(bf16[4,128,512]{2,1,0:T(8,128)(2,1)S(1)} %get-tuple-element.73), channel_id=1, source_target_pairs={{0,1},{1,0},{2,3},{3,2},{4,5},{5,4},{6,7},{7,6},{8,9},{9,8},{10,11... | collective-permute-start | bytes 1572872 | tf_op jit(solution)/shard_map/ppermute | solution.py:37
  25.3 28.7 %collective-permute-start.9 = (bf16[4,256,256]{2,1,0:T(8,128)(2,1)}, bf16[4,256,256]{2,1,0:T(8,128)(2,1)}, u32[]{:S(2)}, u32[]{:S(2)}) collective-permute-start(bf16[4,256,256]{2,1,0:T(8,128)(2,1)} %get-tuple-element.152), channel_id=1, source_target_pairs={{0,8},{1,9},{2,10},{3,11},{4,12},{5,13},{6,14},{7,15},{8,0},{9,1},... | collective-permute-start | bytes 1572872 | tf_op jit(solution)/shard_map/ppermute | solution.py:41
  53.9 7.5 %collective-permute-start.8 = (bf16[4,128,512]{2,1,0:T(8,128)(2,1)S(1)}, bf16[4,128,512]{2,1,0:T(8,128)(2,1)S(1)}, u32[]{:S(2)}, u32[]{:S(2)}) collective-permute-start(bf16[4,128,512]{2,1,0:T(8,128)(2,1)S(1)} %collective-permute-done.3.rest_1_), channel_id=1, source_target_pairs={{0,8},{1,9},{2,10},{3,11},{4,12},{5,13},{6,14},{7,15},{8,0},{9,1},... | collective-permute-start | bytes 1572872 | tf_op jit(solution)/shard_map/ppermute | solution.py:41
  56.3 14.4 %collective-permute-start.10 = (bf16[8,256,256]{2,1,0:T(8,128)(2,1)}, bf16[8,256,256]{2,1,0:T(8,128)(2,1)}, u32[]{:S(2)}, u32[]{:S(2)}) collective-permute-start(bf16[8,256,256]{2,1,0:T(8,128)(2,1)} %pad_maximum_fusion.3), channel_id=1, source_target_pairs={{0,17},{1,0},{2,19},{3,2},{4,21},{5,4},{6,23},{7,6},{8,104},{9,105... | collective-permute-start | bytes 3145736 | tf_op jit(solution)/shard_map/ppermute | solution.py:45
  57.2 15.8 %collective-permute-start.11 = (bf16[8,256,256]{2,1,0:T(8,128)(2,1)}, bf16[8,256,256]{2,1,0:T(8,128)(2,1)}, u32[]{:S(2)}, u32[]{:S(2)}) collective-permute-start(bf16[8,256,256]{2,1,0:T(8,128)(2,1)} %pad_maximum_fusion.3), channel_id=1, source_target_pairs={{0,16},{1,17},{2,18},{3,19},{4,20},{5,21},{6,22},{7,23},{8,72},{9,... | collective-permute-start | bytes 3145736 | tf_op jit(solution)/shard_map/ppermute | solution.py:45
  58.3 25.8 %collective-permute-start.12 = (bf16[8,256,256]{2,1,0:T(8,128)(2,1)}, bf16[8,256,256]{2,1,0:T(8,128)(2,1)}, u32[]{:S(2)}, u32[]{:S(2)}) collective-permute-start(bf16[8,256,256]{2,1,0:T(8,128)(2,1)} %pad_maximum_fusion.3), channel_id=1, source_target_pairs={{0,1},{1,16},{2,3},{3,18},{4,5},{5,20},{6,7},{7,22},{8,40},{9,41},... | collective-permute-start | bytes 3145736 | tf_op jit(solution)/shard_map/ppermute | solution.py:45
  67.9 16.3 %collective-permute-start.14 = (bf16[128,2048]{1,0:T(8,128)(2,1)S(1)}, bf16[128,2048]{1,0:T(8,128)(2,1)S(1)}, u32[]{:S(2)}, u32[]{:S(2)}) collective-permute-start(bf16[128,2048]{1,0:T(8,128)(2,1)S(1)} %get-tuple-element.149), channel_id=1, source_target_pairs={{0,6},{1,7},{2,0},{3,1},{4,2},{5,3},{6,4},{7,5},{8,14},{9,15},{10,... | collective-permute-start | bytes 1572872 | tf_op jit(solution)/shard_map/ppermute | solution.py:33
  70.7 13.5 %collective-permute-start.13 = (bf16[128,2048]{1,0:T(8,128)(2,1)S(1)}, bf16[128,2048]{1,0:T(8,128)(2,1)S(1)}, u32[]{:S(2)}, u32[]{:S(2)}) collective-permute-start(bf16[128,2048]{1,0:T(8,128)(2,1)S(1)} %get-tuple-element.150), channel_id=1, source_target_pairs={{0,2},{1,3},{2,4},{3,5},{4,6},{5,7},{6,0},{7,1},{8,10},{9,11},{10,... | collective-permute-start | bytes 1572872 | tf_op jit(solution)/shard_map/ppermute | solution.py:33
  87.0 65.6 %collective-permute-start.18 = (bf16[4,8,256,256]{3,2,1,0:T(8,128)(2,1)S(1)}, bf16[4,8,256,256]{3,2,1,0:T(8,128)(2,1)S(1)}, u32[]{:S(2)}, u32[]{:S(2)}) collective-permute-start(bf16[4,8,256,256]{3,2,1,0:T(8,128)(2,1)S(1)} %pad_maximum_fusion.rest_0_), channel_id=1, source_target_pairs={{0,96},{1,97},{2,98},{3,99},{4,100},{5,101},{6,102},{7,103},{8,25}... | collective-permute-start | bytes 12582920 | tf_op jit(solution)/shard_map/ppermute | solution.py:51
  90.3 62.3 %collective-permute-start.19 = (bf16[4,8,256,256]{3,2,1,0:T(8,128)(2,1)S(1)}, bf16[4,8,256,256]{3,2,1,0:T(8,128)(2,1)S(1)}, u32[]{:S(2)}, u32[]{:S(2)}) collective-permute-start(bf16[4,8,256,256]{3,2,1,0:T(8,128)(2,1)S(1)} %pad_maximum_fusion.rest_0_), channel_id=1, source_target_pairs={{0,32},{1,33},{2,34},{3,35},{4,36},{5,37},{6,38},{7,39},{8,9},{9,2... | collective-permute-start | bytes 12582920 | tf_op jit(solution)/shard_map/ppermute | solution.py:51
  90.3 23.0 %collective-permute-start.15 = (bf16[256,2048]{1,0:T(8,128)(2,1)S(1)}, bf16[256,2048]{1,0:T(8,128)(2,1)S(1)}, u32[]{:S(2)}, u32[]{:S(2)}) collective-permute-start(bf16[256,2048]{1,0:T(8,128)(2,1)S(1)} %get-tuple-element.91), channel_id=1, source_target_pairs={{0,2},{1,3},{2,4},{3,5},{4,6},{5,7},{6,0},{7,1},{8,10},{9,11},{10,... | collective-permute-start | bytes 3145736 | tf_op jit(solution)/shard_map/ppermute | solution.py:33
  91.5 21.9 %collective-permute-start.16 = (bf16[256,2048]{1,0:T(8,128)(2,1)S(1)}, bf16[256,2048]{1,0:T(8,128)(2,1)S(1)}, u32[]{:S(2)}, u32[]{:S(2)}) collective-permute-start(bf16[256,2048]{1,0:T(8,128)(2,1)S(1)} %get-tuple-element.92), channel_id=1, source_target_pairs={{0,6},{1,7},{2,0},{3,1},{4,2},{5,3},{6,4},{7,5},{8,14},{9,15},{10,... | collective-permute-start | bytes 3145736 | tf_op jit(solution)/shard_map/ppermute | solution.py:33
  154.6 29.1 %collective-permute-start.20 = (bf16[2,8,256,256]{3,2,1,0:T(8,128)(2,1)S(1)}, bf16[2,8,256,256]{3,2,1,0:T(8,128)(2,1)S(1)}, u32[]{:S(2)}, u32[]{:S(2)}) collective-permute-start(bf16[2,8,256,256]{3,2,1,0:T(8,128)(2,1)S(1)} %slice.56), channel_id=1, source_target_pairs={{0,96},{1,97},{2,98},{3,99},{4,100},{5,101},{6,102},{7,103},{8,25}... | collective-permute-start | bytes 6291464 | tf_op jit(solution)/shard_map/ppermute | solution.py:51
  157.9 26.5 %collective-permute-start.21 = (bf16[2,8,256,256]{3,2,1,0:T(8,128)(2,1)S(1)}, bf16[2,8,256,256]{3,2,1,0:T(8,128)(2,1)S(1)}, u32[]{:S(2)}, u32[]{:S(2)}) collective-permute-start(bf16[2,8,256,256]{3,2,1,0:T(8,128)(2,1)S(1)} %slice.57), channel_id=1, source_target_pairs={{0,32},{1,33},{2,34},{3,35},{4,36},{5,37},{6,38},{7,39},{8,9},{9,2... | collective-permute-start | bytes 6291464 | tf_op jit(solution)/shard_map/ppermute | solution.py:51
  157.9 24.9 %collective-permute-start.22 = (bf16[128,4096]{1,0:T(8,128)(2,1)S(1)}, bf16[128,4096]{1,0:T(8,128)(2,1)S(1)}, u32[]{:S(2)}, u32[]{:S(2)}) collective-permute-start(bf16[128,4096]{1,0:T(8,128)(2,1)S(1)} %bitcast.37), channel_id=1, source_target_pairs={{0,6},{1,7},{2,0},{3,1},{4,2},{5,3},{6,4},{7,5},{8,14},{9,15},{10,... | collective-permute-start | bytes 3145736 | tf_op jit(solution)/shard_map/ppermute | solution.py:29
  159.0 24.7 %collective-permute-start.23 = (bf16[128,4096]{1,0:T(8,128)(2,1)S(1)}, bf16[128,4096]{1,0:T(8,128)(2,1)S(1)}, u32[]{:S(2)}, u32[]{:S(2)}) collective-permute-start(bf16[128,4096]{1,0:T(8,128)(2,1)S(1)} %bitcast.38), channel_id=1, source_target_pairs={{0,2},{1,3},{2,4},{3,5},{4,6},{5,7},{6,0},{7,1},{8,10},{9,11},{10,... | collective-permute-start | bytes 3145736 | tf_op jit(solution)/shard_map/ppermute | solution.py:29
  159.5 32.1 %collective-permute-start.28 = (bf16[128,4096]{1,0:T(8,128)(2,1)S(1)}, bf16[128,4096]{1,0:T(8,128)(2,1)S(1)}, u32[]{:S(2)}, u32[]{:S(2)}) collective-permute-start(bf16[128,4096]{1,0:T(8,128)(2,1)S(1)} %bitcast.39), channel_id=1, source_target_pairs={{0,8},{1,9},{2,10},{3,11},{4,12},{5,13},{6,14},{7,15},{8,0},{9,1},... | collective-permute-start | bytes 3145736 | tf_op jit(solution)/shard_map/ppermute | solution.py:41
  184.3 7.3 %collective-permute-start.26 = (bf16[128,4096]{1,0:T(8,128)(2,1)S(1)}, bf16[128,4096]{1,0:T(8,128)(2,1)S(1)}, u32[]{:S(2)}, u32[]{:S(2)}) collective-permute-start(bf16[128,4096]{1,0:T(8,128)(2,1)S(1)} %collective-permute-done.22.rest_0_), channel_id=1, source_target_pairs={{0,8},{1,9},{2,10},{3,11},{4,12},{5,13},{6,14},{7,15},{8,0},{9,1},... | collective-permute-start | bytes 3145736 | tf_op jit(solution)/shard_map/ppermute | solution.py:41
  186.1 19.3 %collective-permute-start.24 = (bf16[64,4096]{1,0:T(8,128)(2,1)S(1)}, bf16[64,4096]{1,0:T(8,128)(2,1)S(1)}, u32[]{:S(2)}, u32[]{:S(2)}) collective-permute-start(bf16[64,4096]{1,0:T(8,128)(2,1)S(1)} %slice.58), channel_id=1, source_target_pairs={{0,6},{1,7},{2,0},{3,1},{4,2},{5,3},{6,4},{7,5},{8,14},{9,15},{10,... | collective-permute-start | bytes 1572872 | tf_op jit(solution)/shard_map/ppermute | solution.py:29
  186.2 19.3 %collective-permute-start.25 = (bf16[64,4096]{1,0:T(8,128)(2,1)S(1)}, bf16[64,4096]{1,0:T(8,128)(2,1)S(1)}, u32[]{:S(2)}, u32[]{:S(2)}) collective-permute-start(bf16[64,4096]{1,0:T(8,128)(2,1)S(1)} %slice.59), channel_id=1, source_target_pairs={{0,2},{1,3},{2,4},{3,5},{4,6},{5,7},{6,0},{7,1},{8,10},{9,11},{10,... | collective-permute-start | bytes 1572872 | tf_op jit(solution)/shard_map/ppermute | solution.py:29
  205.4 15.2 %collective-permute-start.31 = (bf16[256,4096]{1,0:T(8,128)(2,1)S(1)}, bf16[256,4096]{1,0:T(8,128)(2,1)S(1)}, u32[]{:S(2)}, u32[]{:S(2)}) collective-permute-start(bf16[256,4096]{1,0:T(8,128)(2,1)S(1)} %get-tuple-element.127), channel_id=1, source_target_pairs={{0,8},{1,9},{2,10},{3,11},{4,12},{5,13},{6,14},{7,15},{8,0},{9,1},... | collective-permute-start | bytes 6291464 | tf_op jit(solution)/shard_map/ppermute | solution.py:41
  223.8 14.4 %collective-permute-start.33 = (bf16[64,4096]{1,0:T(8,128)(2,1)S(1)}, bf16[64,4096]{1,0:T(8,128)(2,1)S(1)}, u32[]{:S(2)}, u32[]{:S(2)}) collective-permute-start(bf16[64,4096]{1,0:T(8,128)(2,1)S(1)} %get-tuple-element.142), channel_id=1, source_target_pairs={{0,2},{1,3},{2,4},{3,5},{4,6},{5,7},{6,0},{7,1},{8,10},{9,11},{10,... | collective-permute-start | bytes 1572872 | tf_op jit(solution)/shard_map/ppermute | solution.py:33
  223.8 14.3 %collective-permute-start.34 = (bf16[64,4096]{1,0:T(8,128)(2,1)S(1)}, bf16[64,4096]{1,0:T(8,128)(2,1)S(1)}, u32[]{:S(2)}, u32[]{:S(2)}) collective-permute-start(bf16[64,4096]{1,0:T(8,128)(2,1)S(1)} %get-tuple-element.141), channel_id=1, source_target_pairs={{0,6},{1,7},{2,0},{3,1},{4,2},{5,3},{6,4},{7,5},{8,14},{9,15},{10,... | collective-permute-start | bytes 1572872 | tf_op jit(solution)/shard_map/ppermute | solution.py:33
  239.2 24.7 %collective-permute-start.36 = (bf16[128,4096]{1,0:T(8,128)(2,1)S(1)}, bf16[128,4096]{1,0:T(8,128)(2,1)S(1)}, u32[]{:S(2)}, u32[]{:S(2)}) collective-permute-start(bf16[128,4096]{1,0:T(8,128)(2,1)S(1)} %get-tuple-element.139), channel_id=1, source_target_pairs={{0,2},{1,3},{2,4},{3,5},{4,6},{5,7},{6,0},{7,1},{8,10},{9,11},{10,... | collective-permute-start | bytes 3145736 | tf_op jit(solution)/shard_map/ppermute | solution.py:33
  239.3 24.7 %collective-permute-start.37 = (bf16[128,4096]{1,0:T(8,128)(2,1)S(1)}, bf16[128,4096]{1,0:T(8,128)(2,1)S(1)}, u32[]{:S(2)}, u32[]{:S(2)}) collective-permute-start(bf16[128,4096]{1,0:T(8,128)(2,1)S(1)} %get-tuple-element.140), channel_id=1, source_target_pairs={{0,6},{1,7},{2,0},{3,1},{4,2},{5,3},{6,4},{7,5},{8,14},{9,15},{10,... | collective-permute-start | bytes 3145736 | tf_op jit(solution)/shard_map/ppermute | solution.py:33
  241.9 22.0 %collective-permute-start.35 = (bf16[128,4096]{1,0:T(8,128)(2,1)S(1)}, bf16[128,4096]{1,0:T(8,128)(2,1)S(1)}, u32[]{:S(2)}, u32[]{:S(2)}) collective-permute-start(bf16[128,4096]{1,0:T(8,128)(2,1)S(1)} %get-tuple-element.133), channel_id=1, source_target_pairs={{0,8},{1,9},{2,10},{3,11},{4,12},{5,13},{6,14},{7,15},{8,0},{9,1},... | collective-permute-start | bytes 3145736 | tf_op jit(solution)/shard_map/ppermute | solution.py:41
  (16 other events, 111.7 us)

commit v4 on v3

--- a/solution.py
+++ b/solution.py
@@ -118,8 +118,10 @@
 
 
 def load_out(coords, pieces):
+    spots = [(0, 0, 2), (0, 2, 2), (1, 0, 2), (3, 2, 2), (1, 2, 2), (3, 0, 2), (2, 0, 2), (2, 2, 2)]
+
     def copies(coords, refs, weights):
-        for n, entry, zx, xl in ring_spots(coords, [(j, 0, RING) for j in range(RING)]):
+        for n, entry, zx, xl in ring_spots(coords, spots):
             yield refs[n].at[entry], weights[0].at[zx, pl.ds(xl * 2, 2)]
 
     return load(coords, pieces, [(8, 4, 256, 256)], copies, "load_out")[0]
@@ -315,15 +317,18 @@
     )
 
     out_shard = spatial_out.reshape(2, 256, 256)
-    out_first = jnp.stack([out_shard] + [from_first(out_shard, d) for d in range(1, RING)])
-    out_first, own, other = lax.optimization_barrier((out_first, own, other))
-    out_own = [out_first] + [from_second(out_first, d) for d in range(1, RING)]
+    out_low = jnp.stack([out_shard, from_first(out_shard, 1)])
+    out_high = jnp.stack([from_first(out_shard, 2), from_first(out_shard, -1)])
+    out_low, out_high, own, other = lax.optimization_barrier((out_low, out_high, own, other))
+    out_own = [out_low, out_high, from_second(out_low, 1), from_second(out_high, -1)]
+    out_own += [from_second(out_high, 1), from_second(out_low, -1)]
+    out_own += [from_second(out_own[2], 1), from_second(out_own[3], -1)]
     other = swap_xl(other)
     sources = [own, other, swap_core(own)]
-    *sources, o_1, o_2, o_3, residual_rows = lax.optimization_barrier(
-        (*sources, *out_own[1:], residual.reshape(128, 4096))
-    )
-    out_own[1:] = o_1, o_2, o_3
+    *sources, residual_rows = lax.optimization_barrier(
+        (*sources, residual.reshape(128, 4096), *out_own)
+    )
+    sources, out_own, residual_rows = sources[:3], sources[4:] + [residual_rows], sources[3]
     sources.append(swap_core(sources[1]))
     tiles = jnp.stack(
         [w.reshape(256, 2, 256) for w in (temporal_query, temporal_key, temporal_value)]
@@ -366,8 +371,10 @@
 
     part_p, part_m, others = temporal_call(near, weights)
     *far, part_p, part_m, others = lax.optimization_barrier((*far, part_p, part_m, others))
+    far += [swap_core(half) for half in far]
+    *far, others = lax.optimization_barrier((*far, others))
     others = swap_core(others)
-    part, far_others = temporal_call(far + [swap_core(half) for half in far], weights)
+    part, far_others = temporal_call(far, weights)
     far_others, others = lax.optimization_barrier((far_others, others))
     part = (part.astype(jnp.float32) + swap_core(far_others).astype(jnp.float32)).astype(jnp.bfloat16)
     far = [to_y(part[:64], 1), to_y(part[64:], -1)]

time: 288 us -> 280 us (0.972)
  waiting for transfers between devices: 113 us -> 93.2 us
  starting transfers between devices: 44.3 us -> 50.2 us
    ppermute x1, waiting for transfers between devices: 27.1 us -> 0.6 us  [swap_xl(): lax.ppermute(array, AXES, permutation(lambda z, x, c, y: (z, x ^ 1, c, y)))]
    ppermute x7 -> x10, waiting for transfers between devices: 0.63 us -> 13.3 us  [from_second(): lax.ppermute(array, AXES, permutation(lambda z, x, c, y: (z - d * (1 - c)...]
    ppermute x7 -> x10, starting transfers between devices: 9.82 us -> 12.2 us  [from_second(): lax.ppermute(array, AXES, permutation(lambda z, x, c, y: (z - d * (1 - c)...]
  transfers between devices with their start and end apart: 38 -> 41, of which waited for: 14 -> 18; matrix products, arithmetic and copies ran while one was open for 5% -> 6% of each run, Pallas kernels for 19% -> 19%
where the time goes in v4:
time: 280 us
  waiting for transfers between devices  93.2 us (33%)
  blocking collectives  54.3 us (19%)
  Pallas kernels  53.9 us (19%)
  starting transfers between devices  50.2 us (18%)
  local copies, waits for them, and re-layouts  14.2 us (5%)
  other arithmetic  11.1 us (4%)
    ppermute x8, waiting for transfers between devices, to_y(): lax.ppermute(array, AXES, permutation(lambda z, x, c, y: (z, x, c, y + d)))  43.4 us
    all_to_all x1, blocking collectives, shards(): lax.all_to_all(normed.reshape(16, 8, 4096), ('z', 'xh', 'c'), split_axis=...  31.8 us
    pallas_call x3, Pallas kernels, temporal_call(): pl.pallas_call(kernel, out_shape=[jax.ShapeDtypeStruct(shape, jnp.bfloat1...  31.4 us
    all_to_all x1, blocking collectives, shards(): lax.all_to_all(summed, ('z', 'xh', 'c'), split_axis=0, concat_axis=0, til...  22.6 us
    ppermute x4, waiting for transfers between devices, from_y(): lax.ppermute(array, AXES, permutation(lambda z, x, c, y: (z, x, c, y - d)))  16.3 us
    ppermute x12, starting transfers between devices, swap_core(): lax.ppermute(array, AXES, permutation(lambda z, x, c, y: (z, x, 1 - c, y)))  15.4 us
    ppermute x6, waiting for transfers between devices, from_first(): lax.ppermute(array, AXES, permutation(lambda z, x, c, y: (z - d * c, x -...  13.4 us
    ppermute x10, waiting for transfers between devices, from_second(): lax.ppermute(array, AXES, permutation(lambda z, x, c, y: (z - d * (1 - c)...  13.3 us
  transfers between devices with their start and end apart: 41, of which 18 were waited for; matrix products, arithmetic and copies ran while one was open for 6% of the time, Pallas kernels for 19%

profile of v4, /device:TPU:1, one launch (start us, length us, event | category | flops | bytes accessed | tf_op | source)
XLA Modules:
  0.0 279.5 jit_solution(5401535072961073419)
XLA Ops:
  0.0 4.4 %collective-permute-start.1 = (bf16[2,256,256]{2,1,0:T(8,128)(2,1)}, bf16[2,256,256]{2,1,0:T(8,128)(2,1)}, u32[]{:S(2)}, u32[]{:S(2)}) collective-permute-start(bf16[2,256,256]{2,1,0:T(8,128)(2,1)} %bitcast.43), channel_id=1, source_target_pairs={{0,16},{1,17},{2,18},{3,19},{4,20},{5,21},{6,22},{7,23},{8,72},{9,... | collective-permute-start | bytes 786440 | tf_op jit(solution)/shard_map/ppermute | solution.py:45
  5.2 1.9 collective-permute-start
  22.2 2.7 collective-permute-start.4
  24.9 2.8 %collective-permute-done.6.rest_3_ = bf16[2,2,256,256]{3,2,1,0:T(8,128)(2,1)} collective-permute-done((bf16[2,2,256,256]{3,2,1,0:T(8,128)(2,1)S(1)}, bf16[2,2,256,256]{3,2,1,0:T(8,128)(2,1)}, u32[]{:S(2)}, u32[]{:S(2)}) %collective-permute-start.6) | collective-permute-done | bytes 524320 | tf_op jit(solution)/shard_map/ppermute | solution.py:51
  29.2 4.2 %collective-permute-done.7.rest_4_ = bf16[2,2,256,256]{3,2,1,0:T(8,128)(2,1)S(1)} collective-permute-done((bf16[2,2,256,256]{3,2,1,0:T(8,128)(2,1)S(1)}, bf16[2,2,256,256]{3,2,1,0:T(8,128)(2,1)S(1)}, u32[]{:S(2)}, u32[]{:S(2)}) %collective-permute-start.7) | collective-permute-done | bytes 524320 | tf_op jit(solution)/shard_map/ppermute | solution.py:51
  34.2 3.5 %collective-permute-start.9 = (bf16[2,2,256,256]{3,2,1,0:T(8,128)(2,1)}, bf16[2,2,256,256]{3,2,1,0:T(8,128)(2,1)}, u32[]{:S(2)}, u32[]{:S(2)}) collective-permute-start(bf16[2,2,256,256]{3,2,1,0:T(8,128)(2,1)} %collective-permute-done.5.rest_2_), channel_id=1, source_target_pairs={{0,96},{1,97},{2,98},{3,99},{4,100},{5,101},{6,102},{7,103},{8,25}... | collective-permute-start | bytes 1572872 | tf_op jit(solution)/shard_map/ppermute | solution.py:51
  40.2 2.1 collective-permute-start.12
  44.3 3.7 %collective-permute-done.10.rest_7_ = bf16[2,2,256,256]{3,2,1,0:T(8,128)(2,1)} collective-permute-done((bf16[2,2,256,256]{3,2,1,0:T(8,128)(2,1)}, bf16[2,2,256,256]{3,2,1,0:T(8,128)(2,1)}, u32[]{:S(2)}, u32[]{:S(2)}) %collective-permute-start.10) | collective-permute-done | bytes 524320 | tf_op jit(solution)/shard_map/ppermute | solution.py:51
  48.0 1.9 collective-permute-done.9.rest_6_
  49.9 2.3 pad_maximum_fusion.2
  53.7 3.0 %load_out.1.rest_4_ = bf16[8,4,256,256]{3,2,1,0:T(8,128)(2,1)S(1)} custom-call(s32[5]{0:T(128)S(1)} %stack.59.coords, bf16[2,2,256,256]{3,2,1,0:T(8,128)(2,1)} %copy-done.6, bf16[2,2,256,256]{3,2,1,0:T(8,128)(2,1)} %copy-done.5, bf16[2,2,256,256]{3,2,1,0:T(8,128)(2,1)} %collective-permute-done.5.rest_2_, ...), custom_call_target="tpu_custom_call" | custom-call | flops 1048576 | bytes 65536 | tf_op jit(solution)/shard_map/load_out/pallas_call | solution.py:87
  56.7 6.4 %spatial_out.1 = (bf16[256,2048]{1,0:T(8,128)(2,1)S(1)}, bf16[256,2048]{1,0:T(8,128)(2,1)S(1)}, bf16[256,2048]{1,0:T(8,128)(2,1)S(1)}, bf16[256,2048]{1,0:T(8,128)(2,1)S(1)}) custom-call(s32[5]{0:T(128)S(1)} %stack.59.coords, bf16[4,128,512]{2,1,0:T(8,128)(2,1)S(1)} %get-tuple-element.88.rest_0_, bf16[4,128,512]{2,1,0:T(8,128)(2,1)S(1)} %collective-permute-done.3.rest_1_, ...), custom_call_target="tpu_custom_call" | custom-call | flops 1048576 | bytes 65536 | tf_op jit(solution)/shard_map/spatial_out/pallas_call | solution.py:160
  63.2 2.8 %collective-permute-start.17 = (bf16[128,2048]{1,0:T(8,128)(2,1)S(1)}, bf16[128,2048]{1,0:T(8,128)(2,1)S(1)}, u32[]{:S(2)}, u32[]{:S(2)}) collective-permute-start(bf16[128,2048]{1,0:T(8,128)(2,1)S(1)} %get-tuple-element.171), channel_id=1, source_target_pairs={{0,6},{1,7},{2,0},{3,1},{4,2},{5,3},{6,4},{7,5},{8,14},{9,15},{10,... | collective-permute-start | bytes 1572872 | tf_op jit(solution)/shard_map/ppermute | solution.py:33
  68.2 11.2 %collective-permute-done.15 = bf16[8,256,256]{2,1,0:T(8,128)(2,1)} collective-permute-done((bf16[8,256,256]{2,1,0:T(8,128)(2,1)}, bf16[8,256,256]{2,1,0:T(8,128)(2,1)}, u32[]{:S(2)}, u32[]{:S(2)}) %collective-permute-start.15) | collective-permute-done | bytes 1048608 | tf_op jit(solution)/shard_map/ppermute | solution.py:45
  79.7 2.4 pad_maximum_fusion.rest_0_
  86.5 19.7 %collective-permute-done.18 = bf16[256,2048]{1,0:T(8,128)(2,1)S(1)} collective-permute-done((bf16[256,2048]{1,0:T(8,128)(2,1)S(1)}, bf16[256,2048]{1,0:T(8,128)(2,1)S(1)}, u32[]{:S(2)}, u32[]{:S(2)}) %collective-permute-start.18) | collective-permute-done | bytes 1048608 | tf_op jit(solution)/shard_map/ppermute | solution.py:33
  106.9 4.5 %collective-permute-start.20 = (bf16[128,2048]{1,0:T(8,128)(2,1)S(1)}, bf16[128,2048]{1,0:T(8,128)(2,1)S(1)}, u32[]{:S(2)}, u32[]{:S(2)}) collective-permute-start(bf16[128,2048]{1,0:T(8,128)(2,1)S(1)} %get-tuple-element.165), channel_id=1, source_target_pairs={{0,8},{1,9},{2,10},{3,11},{4,12},{5,13},{6,14},{7,15},{8,0},{9,1},... | collective-permute-start | bytes 1572872 | tf_op jit(solution)/shard_map/ppermute | solution.py:41
  112.9 2.8 %norm.1 = (bf16[128,4096]{1,0:T(8,128)(2,1)S(1)}, bf16[128,4096]{1,0:T(8,128)(2,1)S(1)}) custom-call(s32[5]{0:T(128)S(1)} %stack.59.coords, bf16[128,4096]{1,0:T(8,128)(2,1)S(1)} %reshape.34.res, bf16[128,2048]{1,0:T(8,128)(2,1)S(1)} %get-tuple-element.166.mine, bf16[128,2048]{1,0:T(8,128)(2,1)S(1)} %collective-permute-done.20.other), custom_call_target="tpu_custom_call" | custom-call | flops 1048576 | bytes 65536 | tf_op jit(solution)/shard_map/norm/pallas_call | solution.py:283
  115.7 31.8 %all_to_all.10 = bf16[16,8,4096]{2,1,0:T(8,128)(2,1)S(1)} all-to-all(bf16[16,8,4096]{2,1,0:T(8,128)(2,1)S(1)} %bitcast.41), channel_id=1, replica_groups=mesh['z'=4,'xh'=2,'c'=2,'y'=4,'xl'=2] {'z','xh','c'}, dimensions={0} | all-to-all | bytes 2097152 | tf_op jit(solution)/shard_map/all_to_all | solution.py:355
  147.7 1.8 copy-done.1
  154.0 6.4 %load_temporal.2 = (bf16[2,4096,256]{2,1,0:T(8,128)(2,1)S(1)}, bf16[2,4096,256]{2,1,0:T(8,128)(2,1)S(1)}, bf16[2,4096,256]{2,1,0:T(8,128)(2,1)S(1)}, bf16[16,2,256,256]{3,2,1,0:T(8,128)(2,1)S(1)}) custom-call(s32[5]{0:T(128)S(1)} %stack.59.coords, bf16[4,8,256,256]{3,2,1,0:T(8,128)(2,1)} %copy-done, bf16[4,8,256,256]{3,2,1,0:T(8,128)(2,1)} %copy-done.1, ...), custom_call_target="tpu_custom_call" | custom-call | flops 1048576 | bytes 65536 | tf_op jit(solution)/shard_map/load_temporal/pallas_call | solution.py:87
  160.4 14.8 %collective-permute-done.25.rest_0_ = bf16[128,4096]{1,0:T(8,128)(2,1)S(1)} collective-permute-done((bf16[128,4096]{1,0:T(8,128)(2,1)S(1)}, bf16[128,4096]{1,0:T(8,128)(2,1)S(1)}, u32[]{:S(2)}, u32[]{:S(2)}) %collective-permute-start.25) | collective-permute-done | bytes 1048608 | tf_op jit(solution)/shard_map/ppermute | solution.py:29
  180.6 3.9 %load_temporal.3 = (bf16[2,4096,256]{2,1,0:T(8,128)(2,1)S(1)}, bf16[2,4096,256]{2,1,0:T(8,128)(2,1)S(1)}, bf16[2,4096,256]{2,1,0:T(8,128)(2,1)S(1)}, bf16[16,2,256,256]{3,2,1,0:T(8,128)(2,1)S(1)}) custom-call(s32[5]{0:T(128)S(1)} %stack.59.coords, ...), custom_call_target="tpu_custom_call", output_to_operand_aliasing={{0}: (3, {}), {1}: (4, {}), {2}: (5, {}), {3}: (6, {})} | custom-call | flops 1048576 | bytes 65536 | tf_op jit(solution)/shard_map/load_temporal/pallas_call | solution.py:87
  184.6 13.8 %temporal.3 = (bf16[128,4096]{1,0:T(8,128)(2,1)S(1)}, bf16[128,4096]{1,0:T(8,128)(2,1)S(1)}, bf16[256,4096]{1,0:T(8,128)(2,1)S(1)}) custom-call(bf16[128,4096]{1,0:T(8,128)(2,1)S(1)} %collective-permute-done.25.rest_0_, bf16[128,4096]{1,0:T(8,128)(2,1)S(1)} %collective-permute-done.26.rest_1_, bf16[128,4096]{1,0:T(8,128)(2,1)S(1)} %collective-permute-done.29.rest_2_, ...), custom_call_target="tpu_custom_call" | custom-call | flops 1048576 | bytes 65536 | tf_op jit(solution)/shard_map/temporal/pallas_call | solution.py:222
  202.1 8.8 %temporal.4 = (bf16[128,4096]{1,0:T(8,128)(2,1)S(1)}, bf16[128,4096]{1,0:T(8,128)(2,1)S(1)}) custom-call(bf16[64,4096]{1,0:T(8,128)(2,1)S(1)} %collective-permute-done.27.rest_0_, bf16[64,4096]{1,0:T(8,128)(2,1)S(1)} %collective-permute-done.28.rest_1_, bf16[64,4096]{1,0:T(8,128)(2,1)S(1)} %collective-permute-done.32.rest_2_, ...), custom_call_target="tpu_custom_call" | custom-call | flops 1048576 | bytes 65536 | tf_op jit(solution)/shard_map/temporal/pallas_call | solution.py:222
  211.2 2.5 collective-permute-done.35
  214.1 2.7 collective-permute-start.37
  216.7 8.8 %temporal.5 = (bf16[128,4096]{1,0:T(8,128)(2,1)S(1)}, bf16[128,4096]{1,0:T(8,128)(2,1)S(1)}) custom-call(bf16[128,4096]{1,0:T(8,128)(2,1)S(1)} %bitcast.40, bf16[128,4096]{1,0:T(8,128)(2,1)S(1)} %collective-permute-done.31.rest_1_, bf16[2,4096,256]{2,1,0:T(8,128)(2,1)S(1)} %get-tuple-element.133.rest_4_.rest_2_, ...), custom_call_target="tpu_custom_call" | custom-call | flops 1048576 | bytes 65536 | tf_op jit(solution)/shard_map/temporal/pallas_call | solution.py:222
  225.6 3.0 %collective-permute-done.36 = bf16[64,4096]{1,0:T(8,128)(2,1)S(1)} collective-permute-done((bf16[64,4096]{1,0:T(8,128)(2,1)S(1)}, bf16[64,4096]{1,0:T(8,128)(2,1)S(1)}, u32[]{:S(2)}, u32[]{:S(2)}) %collective-permute-start.36) | collective-permute-done | bytes 524320 | tf_op jit(solution)/shard_map/ppermute | solution.py:33
  229.7 2.7 collective-permute-start.40
  233.9 20.6 %collective-permute-done.39 = bf16[128,4096]{1,0:T(8,128)(2,1)S(1)} collective-permute-done((bf16[128,4096]{1,0:T(8,128)(2,1)S(1)}, bf16[128,4096]{1,0:T(8,128)(2,1)S(1)}, u32[]{:S(2)}, u32[]{:S(2)}) %collective-permute-start.39) | collective-permute-done | bytes 1048608 | tf_op jit(solution)/shard_map/ppermute | solution.py:33
  255.2 22.6 %all_to_all.11 = bf16[16,8,4096]{2,1,0:T(8,128)(2,1)S(1)} all-to-all(bf16[16,8,4096]{2,1,0:T(8,128)(2,1)S(1)} %fusion.3), channel_id=1, replica_groups=mesh['z'=4,'xh'=2,'c'=2,'y'=4,'xl'=2] {'z','xh','c'}, dimensions={0} | all-to-all | bytes 2097152 | tf_op jit(solution)/shard_map/all_to_all | solution.py:393
  (125 shorter events, 52.7 us)
Async XLA Ops:
  0.0 15.0 %collective-permute-start.1 = (bf16[2,256,256]{2,1,0:T(8,128)(2,1)}, bf16[2,256,256]{2,1,0:T(8,128)(2,1)}, u32[]{:S(2)}, u32[]{:S(2)}) collective-permute-start(bf16[2,256,256]{2,1,0:T(8,128)(2,1)} %bitcast.43), channel_id=1, source_target_pairs={{0,16},{1,17},{2,18},{3,19},{4,20},{5,21},{6,22},{7,23},{8,72},{9,... | collective-permute-start | bytes 786440 | tf_op jit(solution)/shard_map/ppermute | solution.py:45
  4.4 10.5 %collective-permute-start.2 = (bf16[2,256,256]{2,1,0:T(8,128)(2,1)}, bf16[2,256,256]{2,1,0:T(8,128)(2,1)S(1)}, u32[]{:S(2)}, u32[]{:S(2)}) collective-permute-start(bf16[2,256,256]{2,1,0:T(8,128)(2,1)} %bitcast.44), channel_id=1, source_target_pairs={{0,1},{1,16},{2,3},{3,18},{4,5},{5,20},{6,7},{7,22},{8,40},{9,41},... | collective-permute-start | bytes 786440 | tf_op jit(solution)/shard_map/ppermute | solution.py:45
  5.2 11.6 %collective-permute-start = (bf16[2,256,256]{2,1,0:T(8,128)(2,1)}, bf16[2,256,256]{2,1,0:T(8,128)(2,1)}, u32[]{:S(2)}, u32[]{:S(2)}) collective-permute-start(bf16[2,256,256]{2,1,0:T(8,128)(2,1)} %bitcast.45), channel_id=1, source_target_pairs={{0,17},{1,0},{2,19},{3,2},{4,21},{5,4},{6,23},{7,6},{8,104},{9,105... | collective-permute-start | bytes 786440 | tf_op jit(solution)/shard_map/ppermute | solution.py:45
  18.0 9.7 %collective-permute-start.6 = (bf16[2,2,256,256]{3,2,1,0:T(8,128)(2,1)S(1)}, bf16[2,2,256,256]{3,2,1,0:T(8,128)(2,1)}, u32[]{:S(2)}, u32[]{:S(2)}) collective-permute-start(bf16[2,2,256,256]{3,2,1,0:T(8,128)(2,1)S(1)} %pad_maximum_fusion.6.rest_1_), channel_id=1, source_target_pairs={{0,32},{1,33},{2,34},{3,35},{4,36},{5,37},{6,38},{7,39},{8,9},{9,2... | collective-permute-start | bytes 1572872 | tf_op jit(solution)/shard_map/ppermute | solution.py:51
  20.8 12.6 %collective-permute-start.7 = (bf16[2,2,256,256]{3,2,1,0:T(8,128)(2,1)S(1)}, bf16[2,2,256,256]{3,2,1,0:T(8,128)(2,1)S(1)}, u32[]{:S(2)}, u32[]{:S(2)}) collective-permute-start(bf16[2,2,256,256]{3,2,1,0:T(8,128)(2,1)S(1)} %pad_maximum_fusion.6.rest_1_), channel_id=1, source_target_pairs={{0,96},{1,97},{2,98},{3,99},{4,100},{5,101},{6,102},{7,103},{8,25}... | collective-permute-start | bytes 1572872 | tf_op jit(solution)/shard_map/ppermute | solution.py:51
  22.0 18.1 %collective-permute-start.8 = (bf16[2,2,256,256]{3,2,1,0:T(8,128)(2,1)S(1)}, bf16[2,2,256,256]{3,2,1,0:T(8,128)(2,1)}, u32[]{:S(2)}, u32[]{:S(2)}) collective-permute-start(bf16[2,2,256,256]{3,2,1,0:T(8,128)(2,1)S(1)} %pad_maximum_fusion.5.rest_0_), channel_id=1, source_target_pairs={{0,32},{1,33},{2,34},{3,35},{4,36},{5,37},{6,38},{7,39},{8,9},{9,2... | collective-permute-start | bytes 1572872 | tf_op jit(solution)/shard_map/ppermute | solution.py:51
  22.2 21.5 %collective-permute-start.4 = (bf16[4,128,512]{2,1,0:T(8,128)(2,1)S(1)}, bf16[4,128,512]{2,1,0:T(8,128)(2,1)S(1)}, u32[]{:S(2)}, u32[]{:S(2)}) collective-permute-start(bf16[4,128,512]{2,1,0:T(8,128)(2,1)S(1)} %get-tuple-element.88.rest_0_), channel_id=1, source_target_pairs={{0,8},{1,9},{2,10},{3,11},{4,12},{5,13},{6,14},{7,15},{8,0},{9,1},... | collective-permute-start | bytes 1572872 | tf_op jit(solution)/shard_map/ppermute | solution.py:41
  27.7 16.6 %collective-permute-start.3 = (bf16[4,128,512]{2,1,0:T(8,128)(2,1)}, bf16[4,128,512]{2,1,0:T(8,128)(2,1)S(1)}, u32[]{:S(2)}, u32[]{:S(2)}) collective-permute-start(bf16[4,128,512]{2,1,0:T(8,128)(2,1)} %get-tuple-element.84), channel_id=1, source_target_pairs={{0,1},{1,0},{2,3},{3,2},{4,5},{5,4},{6,7},{7,6},{8,9},{9,8},{10,11... | collective-permute-start | bytes 1572872 | tf_op jit(solution)/shard_map/ppermute | solution.py:37
  27.7 20.3 %collective-permute-start.10 = (bf16[2,2,256,256]{3,2,1,0:T(8,128)(2,1)}, bf16[2,2,256,256]{3,2,1,0:T(8,128)(2,1)}, u32[]{:S(2)}, u32[]{:S(2)}) collective-permute-start(bf16[2,2,256,256]{3,2,1,0:T(8,128)(2,1)} %collective-permute-done.6.rest_3_), channel_id=1, source_target_pairs={{0,32},{1,33},{2,34},{3,35},{4,36},{5,37},{6,38},{7,39},{8,9},{9,2... | collective-permute-start | bytes 1572872 | tf_op jit(solution)/shard_map/ppermute | solution.py:51
  34.2 15.8 %collective-permute-start.9 = (bf16[2,2,256,256]{3,2,1,0:T(8,128)(2,1)}, bf16[2,2,256,256]{3,2,1,0:T(8,128)(2,1)}, u32[]{:S(2)}, u32[]{:S(2)}) collective-permute-start(bf16[2,2,256,256]{3,2,1,0:T(8,128)(2,1)} %collective-permute-done.5.rest_2_), channel_id=1, source_target_pairs={{0,96},{1,97},{2,98},{3,99},{4,100},{5,101},{6,102},{7,103},{8,25}... | collective-permute-start | bytes 1572872 | tf_op jit(solution)/shard_map/ppermute | solution.py:51
  40.2 9.7 %collective-permute-start.12 = (bf16[4,256,256]{2,1,0:T(8,128)(2,1)}, bf16[4,256,256]{2,1,0:T(8,128)(2,1)}, u32[]{:S(2)}, u32[]{:S(2)}) collective-permute-start(bf16[4,256,256]{2,1,0:T(8,128)(2,1)} %get-tuple-element.174), channel_id=1, source_target_pairs={{0,8},{1,9},{2,10},{3,11},{4,12},{5,13},{6,14},{7,15},{8,0},{9,1},... | collective-permute-start | bytes 1572872 | tf_op jit(solution)/shard_map/ppermute | solution.py:41
  52.2 14.3 %collective-permute-start.13 = (bf16[8,256,256]{2,1,0:T(8,128)(2,1)}, bf16[8,256,256]{2,1,0:T(8,128)(2,1)}, u32[]{:S(2)}, u32[]{:S(2)}) collective-permute-start(bf16[8,256,256]{2,1,0:T(8,128)(2,1)} %pad_maximum_fusion.2), channel_id=1, source_target_pairs={{0,17},{1,0},{2,19},{3,2},{4,21},{5,4},{6,23},{7,6},{8,104},{9,105... | collective-permute-start | bytes 3145736 | tf_op jit(solution)/shard_map/ppermute | solution.py:45
  52.4 15.8 %collective-permute-start.14 = (bf16[8,256,256]{2,1,0:T(8,128)(2,1)}, bf16[8,256,256]{2,1,0:T(8,128)(2,1)}, u32[]{:S(2)}, u32[]{:S(2)}) collective-permute-start(bf16[8,256,256]{2,1,0:T(8,128)(2,1)} %pad_maximum_fusion.2), channel_id=1, source_target_pairs={{0,16},{1,17},{2,18},{3,19},{4,20},{5,21},{6,22},{7,23},{8,72},{9,... | collective-permute-start | bytes 3145736 | tf_op jit(solution)/shard_map/ppermute | solution.py:45
  53.5 25.9 %collective-permute-start.15 = (bf16[8,256,256]{2,1,0:T(8,128)(2,1)}, bf16[8,256,256]{2,1,0:T(8,128)(2,1)}, u32[]{:S(2)}, u32[]{:S(2)}) collective-permute-start(bf16[8,256,256]{2,1,0:T(8,128)(2,1)} %pad_maximum_fusion.2), channel_id=1, source_target_pairs={{0,1},{1,16},{2,3},{3,18},{4,5},{5,20},{6,7},{7,22},{8,40},{9,41},... | collective-permute-start | bytes 3145736 | tf_op jit(solution)/shard_map/ppermute | solution.py:45
  63.2 16.2 %collective-permute-start.17 = (bf16[128,2048]{1,0:T(8,128)(2,1)S(1)}, bf16[128,2048]{1,0:T(8,128)(2,1)S(1)}, u32[]{:S(2)}, u32[]{:S(2)}) collective-permute-start(bf16[128,2048]{1,0:T(8,128)(2,1)S(1)} %get-tuple-element.171), channel_id=1, source_target_pairs={{0,6},{1,7},{2,0},{3,1},{4,2},{5,3},{6,4},{7,5},{8,14},{9,15},{10,... | collective-permute-start | bytes 1572872 | tf_op jit(solution)/shard_map/ppermute | solution.py:33
  66.0 13.4 %collective-permute-start.16 = (bf16[128,2048]{1,0:T(8,128)(2,1)S(1)}, bf16[128,2048]{1,0:T(8,128)(2,1)S(1)}, u32[]{:S(2)}, u32[]{:S(2)}) collective-permute-start(bf16[128,2048]{1,0:T(8,128)(2,1)S(1)} %get-tuple-element.172), channel_id=1, source_target_pairs={{0,2},{1,3},{2,4},{3,5},{4,6},{5,7},{6,0},{7,1},{8,10},{9,11},{10,... | collective-permute-start | bytes 1572872 | tf_op jit(solution)/shard_map/ppermute | solution.py:33
  82.2 65.3 %collective-permute-start.21 = (bf16[4,8,256,256]{3,2,1,0:T(8,128)(2,1)S(1)}, bf16[4,8,256,256]{3,2,1,0:T(8,128)(2,1)S(1)}, u32[]{:S(2)}, u32[]{:S(2)}) collective-permute-start(bf16[4,8,256,256]{3,2,1,0:T(8,128)(2,1)S(1)} %pad_maximum_fusion.rest_0_), channel_id=1, source_target_pairs={{0,96},{1,97},{2,98},{3,99},{4,100},{5,101},{6,102},{7,103},{8,25}... | collective-permute-start | bytes 12582920 | tf_op jit(solution)/shard_map/ppermute | solution.py:51
  83.3 64.2 %collective-permute-start.22 = (bf16[4,8,256,256]{3,2,1,0:T(8,128)(2,1)S(1)}, bf16[4,8,256,256]{3,2,1,0:T(8,128)(2,1)S(1)}, u32[]{:S(2)}, u32[]{:S(2)}) collective-permute-start(bf16[4,8,256,256]{3,2,1,0:T(8,128)(2,1)S(1)} %pad_maximum_fusion.rest_0_), channel_id=1, source_target_pairs={{0,32},{1,33},{2,34},{3,35},{4,36},{5,37},{6,38},{7,39},{8,9},{9,2... | collective-permute-start | bytes 12582920 | tf_op jit(solution)/shard_map/ppermute | solution.py:51
  83.7 22.5 %collective-permute-start.18 = (bf16[256,2048]{1,0:T(8,128)(2,1)S(1)}, bf16[256,2048]{1,0:T(8,128)(2,1)S(1)}, u32[]{:S(2)}, u32[]{:S(2)}) collective-permute-start(bf16[256,2048]{1,0:T(8,128)(2,1)S(1)} %get-tuple-element.108), channel_id=1, source_target_pairs={{0,2},{1,3},{2,4},{3,5},{4,6},{5,7},{6,0},{7,1},{8,10},{9,11},{10,... | collective-permute-start | bytes 3145736 | tf_op jit(solution)/shard_map/ppermute | solution.py:33
  85.0 21.2 %collective-permute-start.19 = (bf16[256,2048]{1,0:T(8,128)(2,1)S(1)}, bf16[256,2048]{1,0:T(8,128)(2,1)S(1)}, u32[]{:S(2)}, u32[]{:S(2)}) collective-permute-start(bf16[256,2048]{1,0:T(8,128)(2,1)S(1)} %get-tuple-element.109), channel_id=1, source_target_pairs={{0,6},{1,7},{2,0},{3,1},{4,2},{5,3},{6,4},{7,5},{8,14},{9,15},{10,... | collective-permute-start | bytes 3145736 | tf_op jit(solution)/shard_map/ppermute | solution.py:33
  149.5 27.2 %collective-permute-start.23 = (bf16[2,8,256,256]{3,2,1,0:T(8,128)(2,1)S(1)}, bf16[2,8,256,256]{3,2,1,0:T(8,128)(2,1)S(1)}, u32[]{:S(2)}, u32[]{:S(2)}) collective-permute-start(bf16[2,8,256,256]{3,2,1,0:T(8,128)(2,1)S(1)} %slice.56), channel_id=1, source_target_pairs={{0,96},{1,97},{2,98},{3,99},{4,100},{5,101},{6,102},{7,103},{8,25}... | collective-permute-start | bytes 6291464 | tf_op jit(solution)/shard_map/ppermute | solution.py:51
  151.0 26.5 %collective-permute-start.24 = (bf16[2,8,256,256]{3,2,1,0:T(8,128)(2,1)S(1)}, bf16[2,8,256,256]{3,2,1,0:T(8,128)(2,1)S(1)}, u32[]{:S(2)}, u32[]{:S(2)}) collective-permute-start(bf16[2,8,256,256]{3,2,1,0:T(8,128)(2,1)S(1)} %slice.57), channel_id=1, source_target_pairs={{0,32},{1,33},{2,34},{3,35},{4,36},{5,37},{6,38},{7,39},{8,9},{9,2... | collective-permute-start | bytes 6291464 | tf_op jit(solution)/shard_map/ppermute | solution.py:51
  151.2 23.9 %collective-permute-start.25 = (bf16[128,4096]{1,0:T(8,128)(2,1)S(1)}, bf16[128,4096]{1,0:T(8,128)(2,1)S(1)}, u32[]{:S(2)}, u32[]{:S(2)}) collective-permute-start(bf16[128,4096]{1,0:T(8,128)(2,1)S(1)} %bitcast.37), channel_id=1, source_target_pairs={{0,6},{1,7},{2,0},{3,1},{4,2},{5,3},{6,4},{7,5},{8,14},{9,15},{10,... | collective-permute-start | bytes 3145736 | tf_op jit(solution)/shard_map/ppermute | solution.py:29
  152.0 24.7 %collective-permute-start.26 = (bf16[128,4096]{1,0:T(8,128)(2,1)S(1)}, bf16[128,4096]{1,0:T(8,128)(2,1)S(1)}, u32[]{:S(2)}, u32[]{:S(2)}) collective-permute-start(bf16[128,4096]{1,0:T(8,128)(2,1)S(1)} %bitcast.38), channel_id=1, source_target_pairs={{0,2},{1,3},{2,4},{3,5},{4,6},{5,7},{6,0},{7,1},{8,10},{9,11},{10,... | collective-permute-start | bytes 3145736 | tf_op jit(solution)/shard_map/ppermute | solution.py:29
  152.7 31.8 %collective-permute-start.31 = (bf16[128,4096]{1,0:T(8,128)(2,1)S(1)}, bf16[128,4096]{1,0:T(8,128)(2,1)S(1)}, u32[]{:S(2)}, u32[]{:S(2)}) collective-permute-start(bf16[128,4096]{1,0:T(8,128)(2,1)S(1)} %bitcast.39), channel_id=1, source_target_pairs={{0,8},{1,9},{2,10},{3,11},{4,12},{5,13},{6,14},{7,15},{8,0},{9,1},... | collective-permute-start | bytes 3145736 | tf_op jit(solution)/shard_map/ppermute | solution.py:41
  179.0 19.3 %collective-permute-start.27 = (bf16[64,4096]{1,0:T(8,128)(2,1)S(1)}, bf16[64,4096]{1,0:T(8,128)(2,1)S(1)}, u32[]{:S(2)}, u32[]{:S(2)}) collective-permute-start(bf16[64,4096]{1,0:T(8,128)(2,1)S(1)} %slice.58), channel_id=1, source_target_pairs={{0,6},{1,7},{2,0},{3,1},{4,2},{5,3},{6,4},{7,5},{8,14},{9,15},{10,... | collective-permute-start | bytes 1572872 | tf_op jit(solution)/shard_map/ppermute | solution.py:29
  179.1 19.3 %collective-permute-start.28 = (bf16[64,4096]{1,0:T(8,128)(2,1)S(1)}, bf16[64,4096]{1,0:T(8,128)(2,1)S(1)}, u32[]{:S(2)}, u32[]{:S(2)}) collective-permute-start(bf16[64,4096]{1,0:T(8,128)(2,1)S(1)} %slice.59), channel_id=1, source_target_pairs={{0,2},{1,3},{2,4},{3,5},{4,6},{5,7},{6,0},{7,1},{8,10},{9,11},{10,... | collective-permute-start | bytes 1572872 | tf_op jit(solution)/shard_map/ppermute | solution.py:29
  214.0 14.6 %collective-permute-start.36 = (bf16[64,4096]{1,0:T(8,128)(2,1)S(1)}, bf16[64,4096]{1,0:T(8,128)(2,1)S(1)}, u32[]{:S(2)}, u32[]{:S(2)}) collective-permute-start(bf16[64,4096]{1,0:T(8,128)(2,1)S(1)} %get-tuple-element.164), channel_id=1, source_target_pairs={{0,2},{1,3},{2,4},{3,5},{4,6},{5,7},{6,0},{7,1},{8,10},{9,11},{10,... | collective-permute-start | bytes 1572872 | tf_op jit(solution)/shard_map/ppermute | solution.py:33
  214.1 14.5 %collective-permute-start.37 = (bf16[64,4096]{1,0:T(8,128)(2,1)S(1)}, bf16[64,4096]{1,0:T(8,128)(2,1)S(1)}, u32[]{:S(2)}, u32[]{:S(2)}) collective-permute-start(bf16[64,4096]{1,0:T(8,128)(2,1)S(1)} %get-tuple-element.163), channel_id=1, source_target_pairs={{0,6},{1,7},{2,0},{3,1},{4,2},{5,3},{6,4},{7,5},{8,14},{9,15},{10,... | collective-permute-start | bytes 1572872 | tf_op jit(solution)/shard_map/ppermute | solution.py:33
  229.6 24.9 %collective-permute-start.39 = (bf16[128,4096]{1,0:T(8,128)(2,1)S(1)}, bf16[128,4096]{1,0:T(8,128)(2,1)S(1)}, u32[]{:S(2)}, u32[]{:S(2)}) collective-permute-start(bf16[128,4096]{1,0:T(8,128)(2,1)S(1)} %get-tuple-element.161), channel_id=1, source_target_pairs={{0,2},{1,3},{2,4},{3,5},{4,6},{5,7},{6,0},{7,1},{8,10},{9,11},{10,... | collective-permute-start | bytes 3145736 | tf_op jit(solution)/shard_map/ppermute | solution.py:33
  229.7 24.8 %collective-permute-start.40 = (bf16[128,4096]{1,0:T(8,128)(2,1)S(1)}, bf16[128,4096]{1,0:T(8,128)(2,1)S(1)}, u32[]{:S(2)}, u32[]{:S(2)}) collective-permute-start(bf16[128,4096]{1,0:T(8,128)(2,1)S(1)} %get-tuple-element.162), channel_id=1, source_target_pairs={{0,6},{1,7},{2,0},{3,1},{4,2},{5,3},{6,4},{7,5},{8,14},{9,15},{10,... | collective-permute-start | bytes 3145736 | tf_op jit(solution)/shard_map/ppermute | solution.py:33
  232.3 22.2 %collective-permute-start.38 = (bf16[128,4096]{1,0:T(8,128)(2,1)S(1)}, bf16[128,4096]{1,0:T(8,128)(2,1)S(1)}, u32[]{:S(2)}, u32[]{:S(2)}) collective-permute-start(bf16[128,4096]{1,0:T(8,128)(2,1)S(1)} %get-tuple-element.155), channel_id=1, source_target_pairs={{0,8},{1,9},{2,10},{3,11},{4,12},{5,13},{6,14},{7,15},{8,0},{9,1},... | collective-permute-start | bytes 3145736 | tf_op jit(solution)/shard_map/ppermute | solution.py:41
  (23 other events, 200.5 us)
